TPU v7x, 32 devices: a whole 2x2x4 slice. The times are simulated.
32 devices in a mesh: grp: 2 (over y), row: 4 (over z), col: 2 (over x), dep: 2 (over core).
Axes of the slice: x: 2, y: 2, z: 4, core: 2. Of those that a mesh axis runs over, the one named last changes fastest.
Arguments:
- alignment_embedding: bfloat16 [512, 64, 64], P(('grp', 'dep'), ('row', 'col')), parts along dimension 0, may hold values from -6 to 6
- contact_embedding: float32 [128, 64, 128], P(('grp', 'row', 'dep'), 'col'), parts along dimension 0, may hold values from -6 to 6
- alignment_feedforward_multiplier: float32 [2, 64], replicated, may hold values from 0.25 to 1.75
- alignment_expand_matrix: bfloat16 [2, 2, 64, 256], replicated, may hold values from -0.75 to 0.75
- alignment_contract_matrix: bfloat16 [2, 256, 64], replicated, may hold values from -0.375 to 0.375
- product_standardize_multiplier: float32 [2, 64], replicated, may hold values from 0.25 to 1.75
- first_operand_matrix: bfloat16 [2, 64, 32], replicated, may hold values from -0.75 to 0.75
- second_operand_matrix: bfloat16 [2, 64, 32], replicated, may hold values from -0.75 to 0.75
- product_result_matrix: bfloat16 [2, 1024, 128], replicated, may hold values from -2 to 2
- product_result_offset: float32 [2, 128], replicated, may hold values from -3 to 3
- contact_feedforward_multiplier: float32 [2, 128], replicated, may hold values from 0.25 to 1.75
- contact_expand_matrix: bfloat16 [2, 2, 128, 512], replicated, may hold values from -0.5 to 0.5
- contact_contract_matrix: bfloat16 [2, 512, 128], replicated, may hold values from -0.25 to 0.25
Outputs:
- pair_out: float32 [128, 64, 128], P(('grp', 'row', 'dep'), 'col'), parts along dimension 0
There are 2 independent parts, one for each index of `grp`. A program takes and returns all parts, laid end to end along the dimension named above; an argument that names none is the same for every part. Nothing has to cross between parts.
All inputs are finite; a program needn't handle non-finite values.
Results may differ from a plain program's by a relative error of at most 0.0062.
Values may be sent and summed in bfloat16 or wider, within the bound.
No kernel may reach another device: no remote copies, remote signals or barrier semaphores. Data moves between devices by JAX's collectives and lax.ppermute only.
A program may use at most 128 MiB of HBM per device.

v0:
```python
import jax
import jax.numpy as jnp
from jax import lax
from jax.sharding import PartitionSpec as P

NUM_MODULES = 2


def standardize_features(values, gain):
    mean = jnp.mean(values, axis=-1, keepdims=True)
    centered = values - mean
    var = jnp.mean(centered * centered, axis=-1, keepdims=True)
    return centered * lax.rsqrt(var + 1e-05) * gain


def swish_gating(inputs, w_in, w_out):
    gate = jnp.dot(inputs, w_in[0], preferred_element_type=jnp.float32)
    upper = jnp.dot(inputs, w_in[1], preferred_element_type=jnp.float32)
    hidden = (jax.nn.silu(gate) * upper).astype(jnp.bfloat16)
    return jnp.dot(hidden, w_out, preferred_element_type=jnp.float32)


def per_device(
    alignment_embedding,
    contact_embedding,
    alignment_feedforward_multiplier,
    alignment_expand_matrix,
    alignment_contract_matrix,
    product_standardize_multiplier,
    first_operand_matrix,
    second_operand_matrix,
    product_result_matrix,
    product_result_offset,
    contact_feedforward_multiplier,
    contact_expand_matrix,
    contact_contract_matrix,
):
    expansion_portion, amino_shard_entries, feature_total = alignment_embedding.shape
    width = first_operand_matrix.shape[2]
    pair_ch = contact_embedding.shape[2]
    n_col = lax.axis_size("col")
    n_row = lax.axis_size("row")
    n_dep = lax.axis_size("dep")
    projection_depth = expansion_portion * n_dep
    row_block = amino_shard_entries * n_col
    col_block = amino_shard_entries * n_row
    my_rows = row_block // n_dep
    module_carry = alignment_embedding.astype(jnp.float32)
    field = contact_embedding
    for module_step in range(NUM_MODULES):
        standardized_source = (
            standardize_features(module_carry, alignment_feedforward_multiplier[module_step])
            .astype(jnp.bfloat16)
            .reshape(-1, feature_total)
        )
        module_carry = module_carry + swish_gating(
            standardized_source,
            alignment_expand_matrix[module_step],
            alignment_contract_matrix[module_step],
        ).reshape(module_carry.shape)
        standardized_source = (
            standardize_features(module_carry, product_standardize_multiplier[module_step])
            .astype(jnp.bfloat16)
            .reshape(-1, feature_total)
        )
        left_local = (
            jnp.dot(
                standardized_source,
                first_operand_matrix[module_step],
                preferred_element_type=jnp.float32,
            )
            .astype(jnp.bfloat16)
            .reshape(expansion_portion, amino_shard_entries, width)
        )
        right_local = (
            jnp.dot(
                standardized_source,
                second_operand_matrix[module_step],
                preferred_element_type=jnp.float32,
            )
            .astype(jnp.bfloat16)
            .reshape(expansion_portion, amino_shard_entries, width)
        )
        left_rows = lax.all_gather(left_local, "col", axis=1, tiled=True)
        right_every = lax.all_gather(right_local, ("row", "col"), axis=1, tiled=True)
        right_cols = lax.dynamic_slice_in_dim(
            right_every, lax.axis_index("col") * col_block, col_block, 1
        ).reshape(expansion_portion, col_block * width)
        w_out = product_result_matrix[module_step].astype(jnp.float32)
        left_block_deep, right_deep = (
            lax.all_gather(left_rows, "dep", axis=0, tiled=True),
            lax.all_gather(right_cols, "dep", axis=0, tiled=True),
        )
        left_deep = lax.dynamic_slice_in_dim(
            left_block_deep, lax.axis_index("dep") * my_rows, my_rows, 1
        ).reshape(projection_depth, my_rows * width)
        outer = lax.dot_general(
            left_deep, right_deep, (((0,), (0,)), ((), ())), preferred_element_type=jnp.float32
        )
        outer = (
            outer.reshape(my_rows, width, col_block, width)
            .transpose(0, 2, 1, 3)
            .reshape(my_rows * col_block, width * width)
            / projection_depth
        )
        projected = jnp.dot(outer, w_out, precision=lax.Precision.HIGHEST).reshape(
            my_rows, col_block, pair_ch
        )
        field = field + projected + product_result_offset[module_step]
        standardized_source = (
            standardize_features(field, contact_feedforward_multiplier[module_step])
            .astype(jnp.bfloat16)
            .reshape(-1, pair_ch)
        )
        field = field + swish_gating(
            standardized_source,
            contact_expand_matrix[module_step],
            contact_contract_matrix[module_step],
        ).reshape(field.shape)
    return field


def solution(mesh):
    return jax.shard_map(
        per_device,
        mesh=mesh,
        in_specs=(
            P(("grp", "dep"), ("row", "col"), None),
            P(("grp", "row", "dep"), "col", None),
            P(),
            P(),
            P(),
            P(),
            P(),
            P(),
            P(),
            P(),
            P(),
            P(),
            P(),
        ),
        out_specs=P(("grp", "row", "dep"), "col", None),
        check_vma=False,
    )
```

profile of v0, /device:TPU:0, one launch (start us, length us, event | category | flops | bytes accessed | tf_op | source)
XLA Modules:
  0.0 151.1 jit_solution(6665901455110867210)
XLA Ops:
  0.0 1.3 slice_bitcast_fusion.1
  1.3 0.8 slice_bitcast_fusion.3
  2.0 0.9 convert_reduce_fusion
  3.0 1.0 fusion.13
  4.0 1.0 fusion.15
  5.0 0.2 copy.30
  5.2 1.1 fusion.27
  6.2 1.1 fusion.3
  7.4 0.3 fusion.71
  7.9 0.2 copy.37
  8.1 0.3 fusion.21
  8.4 0.4 fusion.2
  8.8 0.3 fusion.72
  9.3 0.2 copy.39
  9.5 0.2 convolution_convert_fusion
  9.6 0.2 copy.42
  9.8 46.9 %all_gather.30 = bf16[128,64,32]{2,1,0:T(8,128)(2,1)S(1)} all-gather(bf16[128,8,32]{2,1,0:T(8,128)(2,1)S(1)} %bitcast.172), channel_id=1, replica_groups=mesh['grp'=2,'row'=4,'col'=2,'dep'=2] {'row','col'}, dimensions={1}, use_global_device_ids=true | all-gather | bytes 589824 | tf_op jit(solution)/shard_map/all_gather | solution.py:85
  56.8 1.1 copy.43
  57.9 2.2 %all_gather.31 = bf16[256,1024]{0,1:T(8,128)(2,1)S(1)} all-gather(bf16[128,1024]{0,1:T(8,128)(2,1)S(1)} %bitcast.170), channel_id=1, replica_groups=mesh['grp'=2,'row'=4,'col'=2,'dep'=2] {'dep'}, dimensions={0}, use_global_device_ids=true | all-gather | bytes 786432 | tf_op jit(solution)/shard_map/all_gather | solution.py:92
  60.1 0.9 convolution_convert_fusion.1
  61.0 0.2 copy.40
  61.2 9.0 %all_gather.28 = bf16[128,16,32]{2,1,0:T(8,128)(2,1)S(1)} all-gather(bf16[128,8,32]{2,1,0:T(8,128)(2,1)S(1)} %bitcast.173), channel_id=1, replica_groups=mesh['grp'=2,'row'=4,'col'=2,'dep'=2] {'col'}, dimensions={1}, use_global_device_ids=true | all-gather | bytes 196608 | tf_op jit(solution)/shard_map/all_gather | solution.py:84
  70.2 0.4 copy.41
  70.6 2.0 %all_gather.29 = bf16[256,16,32]{0,2,1:T(8,128)(2,1)S(1)} all-gather(bf16[128,16,32]{0,2,1:T(8,128)(2,1)S(1)} %copy.41), channel_id=1, replica_groups=mesh['grp'=2,'row'=4,'col'=2,'dep'=2] {'dep'}, dimensions={0}, use_global_device_ids=true | all-gather | bytes 393216 | tf_op jit(solution)/shard_map/all_gather | solution.py:91
  72.6 2.6 %multiply_bitcast_fusion = f32[8,32,32,32]{3,2,1,0:T(8,128)} fusion(bf16[32,32,256,1]{2,1,0,3:T(8,128)(2,1)S(1)} %bitcast.168, bf16[256,16,32]{0,2,1:T(8,128)(2,1)S(1)} %all_gather.29, s32[]{:T(128)S(6)} %select_n.8), kind=kOutput, calls=%fused_computation | convolution fusion | flops 134479872 | bytes 1703940 | tf_op jit(solution)/shard_map/dot_general | solution.py:97
  75.3 3.7 %div.76 = f32[8,32,1024]{2,1,0:T(8,128)S(1)} reshape(f32[8,32,32,32]{3,2,1,0:T(8,128)} %multiply_bitcast_fusion) | data formatting | bytes 2097152 | tf_op jit(solution)/shard_map/div | solution.py:101
  79.1 0.6 fusion.16
  79.7 0.2 copy.32
  79.9 0.2 convolution_convert_fusion.2
  80.0 0.2 copy.35
  80.2 45.4 %all_gather.26 = bf16[128,64,32]{2,1,0:T(8,128)(2,1)S(1)} all-gather(bf16[128,8,32]{2,1,0:T(8,128)(2,1)S(1)} %bitcast.174), channel_id=1, replica_groups=mesh['grp'=2,'row'=4,'col'=2,'dep'=2] {'row','col'}, dimensions={1}, use_global_device_ids=true | all-gather | bytes 589824 | tf_op jit(solution)/shard_map/all_gather | solution.py:85
  125.8 1.1 copy.36
  126.8 2.2 %all_gather.27 = bf16[256,1024]{0,1:T(8,128)(2,1)S(1)} all-gather(bf16[128,1024]{0,1:T(8,128)(2,1)S(1)} %bitcast.171), channel_id=1, replica_groups=mesh['grp'=2,'row'=4,'col'=2,'dep'=2] {'dep'}, dimensions={0}, use_global_device_ids=true | all-gather | bytes 786432 | tf_op jit(solution)/shard_map/all_gather | solution.py:92
  129.2 0.2 copy.33
  129.4 9.0 %all_gather.24 = bf16[128,16,32]{2,1,0:T(8,128)(2,1)S(1)} all-gather(bf16[128,8,32]{2,1,0:T(8,128)(2,1)S(1)} %bitcast.175), channel_id=1, replica_groups=mesh['grp'=2,'row'=4,'col'=2,'dep'=2] {'col'}, dimensions={1}, use_global_device_ids=true | all-gather | bytes 196608 | tf_op jit(solution)/shard_map/all_gather | solution.py:84
  138.4 0.4 copy.34
  138.9 2.2 %all_gather.25 = bf16[256,16,32]{0,2,1:T(8,128)(2,1)S(1)} all-gather(bf16[128,16,32]{0,2,1:T(8,128)(2,1)S(1)} %copy.34), channel_id=1, replica_groups=mesh['grp'=2,'row'=4,'col'=2,'dep'=2] {'dep'}, dimensions={0}, use_global_device_ids=true | all-gather | bytes 393216 | tf_op jit(solution)/shard_map/all_gather | solution.py:91
  141.1 2.6 %multiply_bitcast_fusion.1 = f32[8,32,32,32]{3,2,1,0:T(8,128)} fusion(bf16[32,32,256,1]{2,1,0,3:T(8,128)(2,1)S(1)} %bitcast.169, bf16[256,16,32]{0,2,1:T(8,128)(2,1)S(1)} %all_gather.25, s32[]{:T(128)S(6)} %select_n.8), kind=kOutput, calls=%fused_computation.1 | convolution fusion | flops 134479872 | bytes 1703940 | tf_op jit(solution)/shard_map/dot_general | solution.py:97
  143.7 3.8 %div.67 = f32[8,32,1024]{2,1,0:T(8,128)S(1)} reshape(f32[8,32,32,32]{3,2,1,0:T(8,128)} %multiply_bitcast_fusion.1) | data formatting | bytes 2097152 | tf_op jit(solution)/shard_map/div | solution.py:101
  147.6 0.7 fusion.73
  148.3 0.2 multiply_reduce_fusion.3
  148.6 0.2 fusion.39
  148.8 0.2 fusion.4
  149.1 0.3 fusion.74
  149.4 0.2 multiply_reduce_fusion.2
  149.8 0.2 fusion.35
  150.0 0.2 fusion.5
  150.2 0.9 convolution_add_fusion.2
  (44 shorter events, 1.0 us)
Async XLA Ops:
  0.0 7.4 %copy-start.5 = (bf16[2,256,64]{1,2,0:T(8,128)(2,1)S(1)}, bf16[2,256,64]{1,2,0:T(8,128)(2,1)}, u32[]{:S(2)}) copy-start(bf16[2,256,64]{1,2,0:T(8,128)(2,1)} %param.17) | copy-start | bytes 196612
  0.0 7.4 %copy-start = (bf16[128,8,64]{0,2,1:T(8,128)(2,1)S(1)}, bf16[128,8,64]{0,2,1:T(8,128)(2,1)}, u32[]{:S(2)}) copy-start(bf16[128,8,64]{0,2,1:T(8,128)(2,1)} %param.13) | copy-start | bytes 393220
  5.2 3.0 %copy-start.6 = (bf16[2,2,64,256]{3,2,1,0:T(8,128)(2,1)S(1)}, bf16[2,2,64,256]{3,2,1,0:T(8,128)(2,1)}, u32[]{:S(2)}) copy-start(bf16[2,2,64,256]{3,2,1,0:T(8,128)(2,1)} %param.16) | copy-start | bytes 393220
  8.1 1.3 copy-start.7
  72.6 6.4 %copy-start.1 = (bf16[2,1024,128]{2,1,0:T(8,128)(2,1)S(1)}, bf16[2,1024,128]{2,1,0:T(8,128)(2,1)}, u32[]{:S(2)}) copy-start(bf16[2,1024,128]{2,1,0:T(8,128)(2,1)} %param.21) | copy-start | bytes 1572868
  79.0 50.0 %copy-start.8 = (bf16[2,64,32]{1,2,0:T(8,128)(2,1)S(1)}, bf16[2,64,32]{1,2,0:T(8,128)(2,1)}, u32[]{:S(2)}) copy-start(bf16[2,64,32]{1,2,0:T(8,128)(2,1)} %param.19) | copy-start | bytes 24580
  141.1 6.5 %copy-start.3 = (f32[8,32,128]{2,1,0:T(8,128)S(1)}, f32[8,32,128]{2,1,0:T(8,128)}, u32[]{:S(2)}) copy-start(f32[8,32,128]{2,1,0:T(8,128)} %param.14) | copy-start | bytes 393220
  141.1 6.5 %copy-start.9 = (f32[128]{0:T(128)S(1)}, f32[128]{0:T(128)}, u32[]{:S(2)}) copy-start(f32[128]{0:T(128)} %get-tuple-element.10) | copy-start | bytes 1540
  143.7 4.6 %copy-start.11 = (f32[2,128]{1,0:T(2,128)S(1)}, f32[2,128]{1,0:T(2,128)}, u32[]{:S(2)}) copy-start(f32[2,128]{1,0:T(2,128)} %param.23) | copy-start | bytes 3076
  143.7 4.9 %copy-start.4 = (bf16[2,2,128,512]{3,2,1,0:T(8,128)(2,1)S(1)}, bf16[2,2,128,512]{3,2,1,0:T(8,128)(2,1)}, u32[]{:S(2)}) copy-start(bf16[2,2,128,512]{3,2,1,0:T(8,128)(2,1)} %param.24) | copy-start | bytes 1572868
  143.7 5.4 %copy-start.2 = (bf16[2,512,128]{2,1,0:T(8,128)(2,1)S(1)}, bf16[2,512,128]{2,1,0:T(8,128)(2,1)}, u32[]{:S(2)}) copy-start(bf16[2,512,128]{2,1,0:T(8,128)(2,1)} %param.25) | copy-start | bytes 786436
  143.7 5.4 %copy-start.10 = (f32[128]{0:T(128)S(1)}, f32[128]{0:T(128)}, u32[]{:S(2)}) copy-start(f32[128]{0:T(128)} %get-tuple-element.9) | copy-start | bytes 1540
where the time goes:
time: 152 us; the launch traced here: 151 us
  blocking collectives  119 us (78%)
  local copies, waits for them, and re-layouts  14.5 us (10%)
  matrix products  13.4 us (9%)
  other arithmetic  3.85 us (3%)
    all_gather x2, blocking collectives, per_device(): lax.all_gather(right_local, ('row', 'col'), axis=1, tiled=True)  92.3 us
    all_gather x2, blocking collectives, per_device(): left_rows = lax.all_gather(left_local, 'col', axis=1, tiled=True)  18.1 us
    div x2, local copies, waits for them, and re-layouts, per_device(): outer.reshape(my_rows, width, col_block, width).transpose(0, 2, 1, 3)  7.58 us
    dot_general x2, matrix products, per_device(): lax.dot_general(left_deep, right_deep, (((0,), (0,)), ((), ())), preferre...  5.29 us
    all_gather x2, blocking collectives, per_device(): lax.all_gather(right_cols, 'dep', axis=0, tiled=True)  4.37 us
    all_gather x2, blocking collectives, per_device(): lax.all_gather(left_rows, 'dep', axis=0, tiled=True)  4.17 us

commit v1 on v0

v1 whole, which is shorter than its diff:
```python
import functools

import jax
import jax.numpy as jnp
from jax import lax
from jax.experimental import pallas as pl
from jax.experimental.pallas import tpu as pltpu
from jax.sharding import PartitionSpec as P

NUM_MODULES = 2
LANES = 128
SUB = 8
F32 = jnp.float32
BF16 = jnp.bfloat16
VMEM_LIMIT = 32 * 1024 * 1024


def dot_tn(a, b):
    return lax.dot_general(a, b, (((0,), (0,)), ((), ())), preferred_element_type=F32)


def dot_nt(a, b):
    return lax.dot_general(a, b, (((1,), (1,)), ((), ())), preferred_element_type=F32)


def dot_nn(a, b):
    return lax.dot_general(a, b, (((1,), (0,)), ((), ())), preferred_element_type=F32)


def silu(x):
    return x * (1.0 / (1.0 + jnp.exp(-x)))


def norm_rows(m, gain):
    mean = jnp.mean(m, axis=0, keepdims=True)
    centered = m - mean
    var = jnp.mean(centered * centered, axis=0, keepdims=True)
    return centered * lax.rsqrt(var + 1e-05) * gain


def norm_lanes(x, gain):
    mean = jnp.mean(x, axis=1, keepdims=True)
    centered = x - mean
    var = jnp.mean(centered * centered, axis=1, keepdims=True)
    return centered * lax.rsqrt(var + 1e-05) * gain


def column_gain(g_ref, step, lanes):
    row = g_ref[step : step + 1, :]
    return jnp.broadcast_to(row, (lanes, row.shape[1])).T


def msa_kernel(step, first, seqs, amino, m_ref, g1_ref, win_ref, wout_ref, g2_ref, wl_ref, wr_ref, *rest):
    if first:
        m_out, left_out, right_out, xs, ls = rest
        xs[...] = m_ref[...].astype(F32)
    else:
        left_out, right_out, ls = rest
    width = wl_ref.shape[2]
    per = 2
    lanes = per * seqs
    gain1 = column_gain(g1_ref, step, lanes)
    gain2 = column_gain(g2_ref, step, lanes)
    for start in range(0, amino, per):
        if first:
            m = jnp.concatenate(
                [xs[pl.ds(start + k, seqs, stride=amino), :].T for k in range(per)], axis=1
            )
        else:
            m = m_ref[:, start * seqs : start * seqs + lanes]
        xm = norm_rows(m, gain1).astype(BF16)
        gate = dot_tn(win_ref[step, 0], xm)
        upper = dot_tn(win_ref[step, 1], xm)
        hidden = (silu(gate) * upper).astype(BF16)
        m = m + dot_tn(wout_ref[step], hidden)
        if first:
            m_out[:, start * seqs : start * seqs + lanes] = m
        xo = norm_rows(m, gain2).astype(BF16)
        left = dot_tn(wl_ref[step], xo)
        right = dot_tn(wr_ref[step], xo)
        for k in range(per):
            rows = slice((start + k) * width, (start + k + 1) * width)
            ls[rows, :] = left[:, k * seqs : (k + 1) * seqs]
            right_out[rows, :] = right[:, k * seqs : (k + 1) * seqs].astype(BF16)
    for p in range(0, width, 2):
        pair = [ls[pl.ds(p + k, amino, stride=width), :] for k in range(2)]
        left_out[p * amino : (p + 2) * amino, :] = jnp.concatenate(pair, axis=0).astype(BF16)


def msa_call(step, first, seqs, amino, m, g1, win, wout, g2, wl, wr):
    width = wl.shape[2]
    feats = win.shape[2]
    factor = jax.ShapeDtypeStruct((amino * width, seqs), BF16)
    outs = [factor, factor]
    scratch = [pltpu.VMEM((amino * width, seqs), F32)]
    if first:
        outs = [jax.ShapeDtypeStruct((feats, amino * seqs), F32)] + outs
        scratch = [pltpu.VMEM((seqs * amino, feats), F32)] + scratch
    return pl.pallas_call(
        functools.partial(msa_kernel, step, first, seqs, amino),
        out_shape=outs,
        in_specs=[pl.BlockSpec(memory_space=pltpu.VMEM)] * 7,
        out_specs=[pl.BlockSpec(memory_space=pltpu.VMEM)] * len(outs),
        scratch_shapes=scratch,
        compiler_params=pltpu.CompilerParams(vmem_limit_bytes=VMEM_LIMIT),
        cost_estimate=pl.CostEstimate(flops=150_000_000, bytes_accessed=500_000, transcendentals=300_000),
        name="msa" + str(step),
    )(m, g1, win, wout, g2, wl, wr)


def swap_groups(parts, width):
    n = len(parts)
    lanes = parts[0].shape[1]
    group = lax.broadcasted_iota(jnp.int32, parts[0].shape, 1) // width
    bit = 1
    while bit < n:
        low = (group & bit) == 0
        shift = bit * width
        new = list(parts)
        for a in range(n):
            if a & bit == 0:
                x, y = parts[a], parts[a | bit]
                new[a] = jnp.where(low, x, pltpu.roll(y, shift, 1))
                new[a | bit] = jnp.where(low, pltpu.roll(x, lanes - shift, 1), y)
        parts = new
        bit *= 2
    return parts


def pair_kernel(step, n_row, n_col, n_dep, amino, width, depth, *refs):
    lefts, rest = refs[:n_col], refs[n_col:]
    rights, (w_ref, keep_ref, send_ref, ls, rs, g_scr, a_scr) = rest[:n_row], rest[n_row:]
    ratio = n_row // n_col
    per_dep = n_col // n_dep
    row, col, dep = lax.axis_index("row"), lax.axis_index("col"), lax.axis_index("dep")
    for dc in range(n_col):
        source = lax.rem(col - dc + n_col, n_col)
        slot = lax.rem(source - dep * per_dep + n_col, n_col)
        ls[slot] = lefts[dc][...]
    for dr in range(ratio):
        off = lax.rem(lax.rem(row, ratio) - dr + ratio, ratio)
        for dc in range(n_col):
            source = lax.rem(col - dc + n_col, n_col)
            rs[off * n_col + source] = rights[dr * n_col + dc][...]
    block = rs.shape[1]
    right = rs[...].reshape(n_row * block, rs.shape[2])
    groups = LANES // width
    tiles = n_row * block // LANES
    rows_tile = groups * amino

    def relayout(t):
        lane = pl.ds(t * LANES, LANES) if isinstance(t, int) else pl.ds(pl.multiple_of(t * LANES, LANES), LANES)
        for big in range(width // groups):
            parts = [
                g_scr[(big * groups + k) * amino : (big * groups + k + 1) * amino, lane] for k in range(groups)
            ]
            parts = swap_groups(parts, width)
            a_scr[pl.ds(t * rows_tile, rows_tile), big * LANES : (big + 1) * LANES] = jnp.concatenate(
                parts, axis=0
            ).astype(BF16)

    def one_left(blk):
        g_scr[...] = dot_nt(ls[blk], right)
        if tiles <= 8:
            for t in range(tiles):
                relayout(t)
        else:
            lax.fori_loop(0, tiles, lambda t, _: (relayout(t), 0)[1], 0)
        return dot_nn(a_scr[...], w_ref[step]) * (1.0 / depth)

    for blk in range(per_dep):
        keep_ref[blk] = one_left(blk)
    for blk in range(per_dep, n_col):
        send_ref[blk - per_dep] = one_left(blk)


def pair_call(step, n_row, n_col, n_dep, amino, width, depth, lefts, rights, w):
    rows = n_row * amino * amino
    pair_ch = w.shape[2]
    per_dep = n_col // n_dep
    out = jax.ShapeDtypeStruct((per_dep, rows, pair_ch), F32)
    send = jax.ShapeDtypeStruct((n_col - per_dep, rows, pair_ch), F32)
    block, seqs = rights[0].shape
    return pl.pallas_call(
        functools.partial(pair_kernel, step, n_row, n_col, n_dep, amino, width, depth),
        out_shape=[out, send],
        in_specs=[pl.BlockSpec(memory_space=pltpu.VMEM)] * (n_col + n_row + 1),
        out_specs=[pl.BlockSpec(memory_space=pltpu.VMEM)] * 2,
        scratch_shapes=[
            pltpu.VMEM((n_col, block, seqs), BF16),
            pltpu.VMEM((n_row, block, seqs), BF16),
            pltpu.VMEM((block, n_row * block), F32),
            pltpu.VMEM((rows, width * width), BF16),
        ],
        compiler_params=pltpu.CompilerParams(vmem_limit_bytes=VMEM_LIMIT),
        cost_estimate=pl.CostEstimate(flops=600_000_000, bytes_accessed=1_500_000, transcendentals=0),
        name="pair" + str(step),
    )(*lefts, *rights, w)


def trans_kernel(step, first, last, amino, cols, z_ref, keep_ref, recv_ref, b_ref, g_ref, win_ref, wout_ref, out_ref):
    for blk in range(keep_ref.shape[0]):
        base = blk * amino * cols
        if first:
            z = jnp.concatenate([z_ref[pl.ds(base + j, amino, stride=cols), :] for j in range(cols)], axis=0)
        else:
            z = z_ref[blk]
        z = z + (keep_ref[blk] + recv_ref[blk]) + b_ref[step : step + 1, :]
        xp = norm_lanes(z, g_ref[step : step + 1, :]).astype(BF16)
        gate = dot_nn(xp, win_ref[step, 0])
        upper = dot_nn(xp, win_ref[step, 1])
        hidden = (silu(gate) * upper).astype(BF16)
        z = z + dot_nn(hidden, wout_ref[step])
        if last:
            for j in range(cols):
                out_ref[pl.ds(base + j, amino, stride=cols), :] = z[j * amino : (j + 1) * amino, :]
        else:
            out_ref[blk] = z


def trans_call(step, amino, cols, z, keep, recv, b, g, win, wout):
    first, last = step == 0, step == NUM_MODULES - 1
    per_dep, rows, pair_ch = keep.shape
    shape = (per_dep * rows, pair_ch) if last else keep.shape
    return pl.pallas_call(
        functools.partial(trans_kernel, step, first, last, amino, cols),
        out_shape=jax.ShapeDtypeStruct(shape, F32),
        in_specs=[pl.BlockSpec(memory_space=pltpu.VMEM)] * 7,
        out_specs=pl.BlockSpec(memory_space=pltpu.VMEM),
        compiler_params=pltpu.CompilerParams(vmem_limit_bytes=VMEM_LIMIT),
        cost_estimate=pl.CostEstimate(flops=150_000_000, bytes_accessed=1_500_000, transcendentals=300_000),
        name="trans" + str(step),
    )(z, keep, recv, b, g, win, wout)


def per_device(n_row, n_col, n_dep, msa, pair, g_ff, w_in, w_out, g_op, w_l, w_r, w_res, b_res, g_pair, p_in, p_out):
    seqs, amino, feats = msa.shape
    width = w_l.shape[2]
    depth = seqs * n_dep
    ratio = n_row // n_col
    cols = amino * n_row
    row, col = lax.axis_index("row"), lax.axis_index("col")

    def rows_by(k):
        return lambda x: lax.ppermute(x, "row", [(r, (r + k) % n_row) for r in range(n_row)])

    def group_by(k):
        pairs = [(r, r // ratio * ratio + (r % ratio + k) % ratio) for r in range(n_row)]
        return lambda x: lax.ppermute(x, "row", pairs)

    def cols_by(k):
        return lambda x: lax.ppermute(x, "col", [(c, (c + k) % n_col) for c in range(n_col)])

    def pick(items, index):
        got = items[0]
        for k in range(1, len(items)):
            got = jnp.where(index == k, items[k], got)
        return got

    def spread_far(right):
        return [right] + [rows_by(k * ratio)(right) for k in range(1, n_col)]

    def spread_cols(items):
        group = row // ratio
        wanted = [pick(items, (group - (col + dc) + 2 * n_col) % n_col) for dc in range(n_col)]
        return [wanted[0]] + [cols_by(dc)(wanted[dc]) for dc in range(1, n_col)]

    def spread_rows(items):
        both = jnp.concatenate(items, axis=0)
        size = items[0].shape[0]
        got = list(items)
        for dr in range(1, ratio):
            moved = group_by(dr)(both)
            got += [moved[k * size : (k + 1) * size] for k in range(n_col)]
        return got

    m, left0, right0 = msa_call(
        0, True, seqs, amino, msa.reshape(seqs * amino, feats), g_ff, w_in, w_out, g_op, w_l, w_r
    )
    left1, right1 = msa_call(1, False, seqs, amino, m, g_ff, w_in, w_out, g_op, w_l, w_r)
    z = pair.reshape(-1, pair.shape[2])
    far = [spread_far(right0), spread_far(right1)]
    lefts = [
        [left] + [cols_by(dc)(left) for dc in range(1, n_col)] for left in (left0, left1)
    ]
    for step in range(NUM_MODULES):
        rights = spread_rows(spread_cols(far[step]))
        keep, send = pair_call(
            step, n_row, n_col, n_dep, amino, width, depth, lefts[step], rights, w_res
        )
        recv = lax.ppermute(send, "dep", [(d, (d + 1) % n_dep) for d in range(n_dep)])
        z = trans_call(step, amino, cols, z, keep, recv, b_res, g_pair, p_in, p_out)
    return z.reshape(pair.shape)


def solution(mesh):
    return jax.shard_map(
        functools.partial(per_device, mesh.shape["row"], mesh.shape["col"], mesh.shape["dep"]),
        mesh=mesh,
        in_specs=(
            P(("grp", "dep"), ("row", "col"), None),
            P(("grp", "row", "dep"), "col", None),
        )
        + (P(),) * 11,
        out_specs=P(("grp", "row", "dep"), "col", None),
        check_vma=False,
    )
```

time: 152 us -> 32 us (0.21)
  blocking collectives: 119 us -> 0 us
  matrix products: 13.4 us -> 0 us
  starting transfers between devices: 0 us -> 12.6 us
  local copies, waits for them, and re-layouts: 14.5 us -> 3.4 us
  Pallas kernels: 0 us -> 8.61 us
  waiting for transfers between devices: 0 us -> 6.93 us
  other arithmetic: 3.85 us -> 0.05 us
    all_gather x8 -> x0, blocking collectives: 119 us -> none  [the longest x2 92.3 us: per_device(): lax.all_gather(right_local, ('row', 'col'), axis=1, tiled=True)]
    dot_general x20 -> x0, matrix products: 13.4 us -> none  [the longest x2 5.29 us: per_device(): lax.dot_general(left_deep, right_deep, (((0,), (0,)), ((), ())), preferre...]
    ppermute x0 -> x10, starting transfers between devices: none -> 12.6 us  [the longest x4 5.34 us: cols_by(): lax.ppermute(x, 'col', [(c, (c + k) % n_col) for c in range(n_col)])]
    pallas_call x0 -> x6, Pallas kernels: none -> 8.61 us  [the longest x2 3.62 us: msa_call(): pl.pallas_call(functools.partial(msa_kernel, step, first, seqs, amino), o...]
    div x2 -> x0, local copies, waits for them, and re-layouts: 7.58 us -> none  [per_device(): outer.reshape(my_rows, width, col_block, width).transpose(0, 2, 1, 3)]
    ppermute x0 -> x10, waiting for transfers between devices: none -> 6.93 us  [the longest x2 3.61 us: rows_by(): lax.ppermute(x, 'row', [(r, (r + k) % n_row) for r in range(n_row)])]
    unnamed x24 -> x28, local copies, waits for them, and re-layouts: 0.05 us -> 3.38 us
    dynamic_slice x4 -> x0, local copies, waits for them, and re-layouts: 2.37 us -> none  [per_device(): lax.dynamic_slice_in_dim(right_every, lax.axis_index('col') * col_block,...]
  transfers between devices with their start and end apart: 0 -> 10, of which waited for: 0 -> 4; matrix products, arithmetic and copies ran while one was open for 0% -> 0% of each run, Pallas kernels for 0% -> 17%
where the time goes in v1:
time: 32 us; the launch traced here: 31.8 us
  starting transfers between devices  12.6 us (39%)
  Pallas kernels  8.61 us (27%)
  waiting for transfers between devices  6.93 us (22%)
  local copies, waits for them, and re-layouts  3.4 us (11%)
    ppermute x4, starting transfers between devices, cols_by(): lax.ppermute(x, 'col', [(c, (c + k) % n_col) for c in range(n_col)])  5.34 us
    ppermute x2, starting transfers between devices, rows_by(): lax.ppermute(x, 'row', [(r, (r + k) % n_row) for r in range(n_row)])  4.19 us
    pallas_call x2, Pallas kernels, msa_call(): pl.pallas_call(functools.partial(msa_kernel, step, first, seqs, amino), o...  3.62 us
    ppermute x2, waiting for transfers between devices, rows_by(): lax.ppermute(x, 'row', [(r, (r + k) % n_row) for r in range(n_row)])  3.61 us
    unnamed x28, local copies, waits for them, and re-layouts  3.38 us
    pallas_call x2, Pallas kernels, pair_call(): pl.pallas_call(functools.partial(pair_kernel, step, n_row, n_col, n_dep,...  3.05 us
    ppermute x2, starting transfers between devices, group_by(): return lambda x: lax.ppermute(x, 'row', pairs)  2.42 us
    pallas_call x2, Pallas kernels, trans_call(): pl.pallas_call(functools.partial(trans_kernel, step, first, last, amino,...  1.94 us
  transfers between devices with their start and end apart: 10, of which 4 were waited for; matrix products, arithmetic and copies ran while one was open for 0% of the time, Pallas kernels for 17%

profile of v1, /device:TPU:0, one launch (start us, length us, event | category | flops | bytes accessed | tf_op | source)
XLA Modules:
  0.0 31.8 jit_solution(16933553142973503982)
XLA Ops:
  0.0 1.0 %copy.15.wout_ref = bf16[2,256,64]{2,1,0:T(8,128)(2,1)S(1)} copy(bf16[2,256,64]{1,2,0:T(8,128)(2,1)} %param.17) | data formatting | bytes 131072 | tf_op args[4]
  1.0 0.0 copy-done.10
  1.0 0.0 copy-start.11
  1.0 0.1 copy.16.wl_ref
  1.1 0.6 %copy-done.11 = bf16[2,64,32]{1,2,0:T(8,128)(2,1)S(1)} copy-done((bf16[2,64,32]{1,2,0:T(8,128)(2,1)S(1)}, bf16[2,64,32]{1,2,0:T(8,128)(2,1)}, u32[]{:S(2)}) %copy-start.11) | copy-done | bytes 8216
  1.7 0.1 copy.17.wr_ref
  1.8 0.0 copy-done.9
  1.8 0.0 copy-start.2
  1.9 0.0 copy-start.5
  1.9 0.2 copy.14
  2.1 0.0 copy-start.4
  2.1 0.7 %copy-done.2 = bf16[2,2,64,256]{3,2,1,0:T(8,128)(2,1)S(1)} copy-done((bf16[2,2,64,256]{3,2,1,0:T(8,128)(2,1)S(1)}, bf16[2,2,64,256]{3,2,1,0:T(8,128)(2,1)}, u32[]{:S(2)}) %copy-start.2) | copy-done | bytes 131096
  2.8 0.0 copy-done.5
  2.8 0.0 copy-done.4
  2.8 1.8 %msa0.1 = (f32[64,1024]{1,0:T(8,128)S(1)}, bf16[256,128]{1,0:T(8,128)(2,1)S(1)}, bf16[256,128]{1,0:T(8,128)(2,1)S(1)}) custom-call(bf16[1024,64]{1,0:T(8,128)(2,1)S(1)} %bitcast.3, f32[2,64]{1,0:T(2,128)S(1)} %copy-done.4, bf16[2,2,64,256]{3,2,1,0:T(8,128)(2,1)S(1)} %copy-done.2, bf16[2,256,64]{2,1,0:T(8,128)(2,1)S(1)} %copy.15.wout_ref, ...), custom_call_target="tpu_custom_call" | custom-call | flops 150000000 | bytes 500000 | tf_op jit(solution)/shard_map/msa0/pallas_call | solution.py:99
  4.6 4.1 %collective-permute-start.1 = (bf16[256,128]{1,0:T(8,128)(2,1)S(1)}, bf16[256,128]{1,0:T(8,128)(2,1)S(1)}, u32[]{:S(2)}, u32[]{:S(2)}) collective-permute-start(bf16[256,128]{1,0:T(8,128)(2,1)S(1)} %get-tuple-element.15), channel_id=1, source_target_pairs={{0,8},{4,12},{8,0},{12,4},{1,9},{5,13},{9,1},{13,5},{2,10},{6,14},... | collective-permute-start | bytes 196616 | tf_op jit(solution)/shard_map/ppermute | solution.py:245
  8.7 1.8 %msa1.1 = (bf16[256,128]{1,0:T(8,128)(2,1)S(1)}, bf16[256,128]{1,0:T(8,128)(2,1)S(1)}) custom-call(f32[64,1024]{1,0:T(8,128)S(1)} %get-tuple-element.18.m_ref, f32[2,64]{1,0:T(2,128)S(1)} %copy-done.4, bf16[2,2,64,256]{3,2,1,0:T(8,128)(2,1)S(1)} %copy-done.2, bf16[2,256,64]{2,1,0:T(8,128)(2,1)S(1)} %copy.15.wout_ref, f32[2,64]{1,0:T(2,128)S(1)} %copy-done.5, ...), custom_call_target="tpu_custom_call" | custom-call | flops 150000000 | bytes 500000 | tf_op jit(solution)/shard_map/msa1/pallas_call | solution.py:99
  10.5 0.1 collective-permute-start.6
  10.6 1.7 %collective-permute-done.1 = bf16[256,128]{1,0:T(8,128)(2,1)S(1)} collective-permute-done((bf16[256,128]{1,0:T(8,128)(2,1)S(1)}, bf16[256,128]{1,0:T(8,128)(2,1)S(1)}, u32[]{:S(2)}, u32[]{:S(2)}) %collective-permute-start.1) | collective-permute-done | bytes 65568 | tf_op jit(solution)/shard_map/ppermute | solution.py:245
  12.4 0.0 copy-start.8
  12.4 1.8 %collective-permute-start.2 = (bf16[256,128]{1,0:T(8,128)(2,1)S(1)}, bf16[256,128]{1,0:T(8,128)(2,1)S(1)}, u32[]{:S(2)}, u32[]{:S(2)}) collective-permute-start(bf16[256,128]{1,0:T(8,128)(2,1)S(1)} %get-tuple-element.29), channel_id=1, source_target_pairs={{0,2},{2,0},{1,3},{3,1},{4,6},{6,4},{5,7},{7,5},{8,10},{10,8},{9,1... | collective-permute-start | bytes 196616 | tf_op jit(solution)/shard_map/ppermute | solution.py:252
  14.1 1.9 %collective-permute-done.6 = bf16[256,128]{1,0:T(8,128)(2,1)S(1)} collective-permute-done((bf16[256,128]{1,0:T(8,128)(2,1)S(1)}, bf16[256,128]{1,0:T(8,128)(2,1)S(1)}, u32[]{:S(2)}, u32[]{:S(2)}) %collective-permute-start.6) | collective-permute-done | bytes 65568 | tf_op jit(solution)/shard_map/ppermute | solution.py:245
  16.0 1.6 %collective-permute-start.7 = (bf16[256,128]{1,0:T(8,128)(2,1)S(1)}, bf16[256,128]{1,0:T(8,128)(2,1)S(1)}, u32[]{:S(2)}, u32[]{:S(2)}) collective-permute-start(bf16[256,128]{1,0:T(8,128)(2,1)S(1)} %get-tuple-element.25), channel_id=1, source_target_pairs={{0,2},{2,0},{1,3},{3,1},{4,6},{6,4},{5,7},{7,5},{8,10},{10,8},{9,1... | collective-permute-start | bytes 196616 | tf_op jit(solution)/shard_map/ppermute | solution.py:252
  17.6 0.0 collective-permute-done.2.refs_3_
  17.6 2.3 %collective-permute-start.3 = (bf16[512,128]{1,0:T(8,128)(2,1)S(1)}, bf16[512,128]{1,0:T(8,128)(2,1)S(1)}, u32[]{:S(2)}, u32[]{:S(2)}) collective-permute-start(bf16[512,128]{1,0:T(8,128)(2,1)S(1)} %pad_maximum_fusion), channel_id=1, source_target_pairs={{0,4},{4,0},{8,12},{12,8},{1,5},{5,1},{9,13},{13,9},{2,6},{6,2},{1... | collective-permute-start | bytes 393224 | tf_op jit(solution)/shard_map/ppermute | solution.py:249
  19.9 1.2 %collective-permute-start.5 = (bf16[256,128]{1,0:T(8,128)(2,1)S(1)}, bf16[256,128]{1,0:T(8,128)(2,1)S(1)}, u32[]{:S(2)}, u32[]{:S(2)}) collective-permute-start(bf16[256,128]{1,0:T(8,128)(2,1)S(1)} %get-tuple-element.19.refs_0_), channel_id=1, source_target_pairs={{0,2},{2,0},{1,3},{3,1},{4,6},{6,4},{5,7},{7,5},{8,10},{10,8},{9,1... | collective-permute-start | bytes 196616 | tf_op jit(solution)/shard_map/ppermute | solution.py:252
  21.1 0.8 %collective-permute-start = (bf16[256,128]{1,0:T(8,128)(2,1)S(1)}, bf16[256,128]{1,0:T(8,128)(2,1)S(1)}, u32[]{:S(2)}, u32[]{:S(2)}) collective-permute-start(bf16[256,128]{1,0:T(8,128)(2,1)S(1)} %get-tuple-element.14.refs_0_), channel_id=1, source_target_pairs={{0,2},{2,0},{1,3},{3,1},{4,6},{6,4},{5,7},{7,5},{8,10},{10,8},{9,1... | collective-permute-start | bytes 196616 | tf_op jit(solution)/shard_map/ppermute | solution.py:252
  21.9 0.0 collective-permute-done.7.refs_3_
  21.9 0.1 collective-permute-start.8
  22.1 1.7 %collective-permute-done.3 = bf16[512,128]{1,0:T(8,128)(2,1)S(1)} collective-permute-done((bf16[512,128]{1,0:T(8,128)(2,1)S(1)}, bf16[512,128]{1,0:T(8,128)(2,1)S(1)}, u32[]{:S(2)}, u32[]{:S(2)}) %collective-permute-start.3) | collective-permute-done | bytes 131104 | tf_op jit(solution)/shard_map/ppermute | solution.py:249
  23.8 1.6 %collective-permute-done.refs_1_ = bf16[256,128]{1,0:T(8,128)(2,1)S(1)} collective-permute-done((bf16[256,128]{1,0:T(8,128)(2,1)S(1)}, bf16[256,128]{1,0:T(8,128)(2,1)S(1)}, u32[]{:S(2)}, u32[]{:S(2)}) %collective-permute-start) | collective-permute-done | bytes 65568 | tf_op jit(solution)/shard_map/ppermute | solution.py:252
  25.4 0.0 copy-done.8
  25.4 1.5 %pair0.1 = (f32[1,256,128]{2,1,0:T(8,128)S(1)}, f32[1,256,128]{2,1,0:T(8,128)S(1)}) custom-call(bf16[256,128]{1,0:T(8,128)(2,1)S(1)} %get-tuple-element.14.refs_0_, bf16[256,128]{1,0:T(8,128)(2,1)S(1)} %collective-permute-done.refs_1_, bf16[256,128]{1,0:T(8,128)(2,1)S(1)} %get-tuple-element.30.refs_2_, bf16[256,128]{1,0:T(8,128)(2,1)S(1)} %collective-permute-done.2.refs_3_, ...), custom_call_target="tpu_custom_call" | custom-call | flops 600000000 | bytes 1500000 | tf_op jit(solution)/shard_map/pair0/pallas_call | solution.py:184
  26.9 0.1 collective-permute-start.4
  27.0 0.0 collective-permute-done.8
  27.0 0.0 collective-permute-done.5.refs_1_
  27.0 0.0 copy-start
  27.1 0.0 copy-start.1
  27.1 0.0 copy-start.3
  27.1 0.0 copy-start.7
  27.1 1.5 %pair1.1 = (f32[1,256,128]{2,1,0:T(8,128)S(1)}, f32[1,256,128]{2,1,0:T(8,128)S(1)}) custom-call(bf16[256,128]{1,0:T(8,128)(2,1)S(1)} %get-tuple-element.19.refs_0_, bf16[256,128]{1,0:T(8,128)(2,1)S(1)} %collective-permute-done.5.refs_1_, bf16[256,128]{1,0:T(8,128)(2,1)S(1)} %get-tuple-element.26.refs_2_, ...), custom_call_target="tpu_custom_call" | custom-call | flops 600000000 | bytes 1500000 | tf_op jit(solution)/shard_map/pair1/pallas_call | solution.py:184
  28.6 0.5 %collective-permute-start.9 = (f32[1,256,128]{2,1,0:T(8,128)S(1)}, f32[1,256,128]{2,1,0:T(8,128)S(1)}, u32[]{:S(2)}, u32[]{:S(2)}) collective-permute-start(f32[1,256,128]{2,1,0:T(8,128)S(1)} %get-tuple-element.22), channel_id=1, source_target_pairs={{0,1},{1,0},{2,3},{3,2},{4,5},{5,4},{6,7},{7,6},{8,9},{9,8},{10,11... | collective-permute-start | bytes 393224 | tf_op jit(solution)/shard_map/ppermute | solution.py:291
  29.2 0.0 collective-permute-done.4.recv_ref
  29.2 0.0 copy-done.1
  29.2 0.7 %copy-done.6 = f32[2,128]{1,0:T(2,128)S(1)} copy-done((f32[2,128]{1,0:T(2,128)S(1)}, f32[2,128]{1,0:T(2,128)}, u32[]{:S(2)}) %copy-start.6) | copy-done | bytes 1048
  29.9 0.6 %trans0.1.z_ref = f32[1,256,128]{2,1,0:T(8,128)S(1)} custom-call(f32[256,128]{1,0:T(8,128)S(1)} %bitcast.4, f32[1,256,128]{2,1,0:T(8,128)S(1)} %get-tuple-element.16.keep_ref, f32[1,256,128]{2,1,0:T(8,128)S(1)} %collective-permute-done.4.recv_ref, f32[2,128]{1,0:T(2,128)S(1)} %copy-done.6, f32[2,128]{1,0:T(2,128)S(1)} %copy-done.7, ...), custom_call_target="tpu_custom_call" | custom-call | flops 150000000 | bytes 1500000 | tf_op jit(solution)/shard_map/trans0/pallas_call | solution.py:225
  30.5 0.0 collective-permute-done.9.recv_ref
  30.5 1.3 %trans1.1 = f32[256,128]{1,0:T(8,128)} custom-call(f32[1,256,128]{2,1,0:T(8,128)S(1)} %trans0.1.z_ref, f32[1,256,128]{2,1,0:T(8,128)S(1)} %get-tuple-element.21.keep_ref, f32[1,256,128]{2,1,0:T(8,128)S(1)} %collective-permute-done.9.recv_ref, f32[2,128]{1,0:T(2,128)S(1)} %copy-done.6, f32[2,128]{1,0:T(2,128)S(1)} %copy-done.7, ...), custom_call_target="tpu_custom_call" | custom-call | flops 150000000 | bytes 1500000 | tf_op jit(solution)/shard_map/trans1/pallas_call | solution.py:225
  (12 shorter events, 0.1 us)
Async XLA Ops:
  0.0 1.0 %copy-start.10 = (bf16[2,64,32]{1,2,0:T(8,128)(2,1)S(1)}, bf16[2,64,32]{1,2,0:T(8,128)(2,1)}, u32[]{:S(2)}) copy-start(bf16[2,64,32]{1,2,0:T(8,128)(2,1)} %param.19) | copy-start | bytes 24580
  0.0 1.8 %copy-start.9 = (bf16[128,8,64]{0,2,1:T(8,128)(2,1)S(1)}, bf16[128,8,64]{0,2,1:T(8,128)(2,1)}, u32[]{:S(2)}) copy-start(bf16[128,8,64]{0,2,1:T(8,128)(2,1)} %param.13) | copy-start | bytes 393220
  1.0 0.7 %copy-start.11 = (bf16[2,64,32]{1,2,0:T(8,128)(2,1)S(1)}, bf16[2,64,32]{1,2,0:T(8,128)(2,1)}, u32[]{:S(2)}) copy-start(bf16[2,64,32]{1,2,0:T(8,128)(2,1)} %param.20) | copy-start | bytes 24580
  1.8 0.9 %copy-start.2 = (bf16[2,2,64,256]{3,2,1,0:T(8,128)(2,1)S(1)}, bf16[2,2,64,256]{3,2,1,0:T(8,128)(2,1)}, u32[]{:S(2)}) copy-start(bf16[2,2,64,256]{3,2,1,0:T(8,128)(2,1)} %win_ref.6) | copy-start | bytes 393220
  1.9 0.9 %copy-start.5 = (f32[2,64]{1,0:T(2,128)S(1)}, f32[2,64]{1,0:T(2,128)}, u32[]{:S(2)}) copy-start(f32[2,64]{1,0:T(2,128)} %g2_ref.3) | copy-start | bytes 1540
  2.1 0.7 %copy-start.4 = (f32[2,64]{1,0:T(2,128)S(1)}, f32[2,64]{1,0:T(2,128)}, u32[]{:S(2)}) copy-start(f32[2,64]{1,0:T(2,128)} %g1_ref.3) | copy-start | bytes 1540
  4.6 7.8 %collective-permute-start.1 = (bf16[256,128]{1,0:T(8,128)(2,1)S(1)}, bf16[256,128]{1,0:T(8,128)(2,1)S(1)}, u32[]{:S(2)}, u32[]{:S(2)}) collective-permute-start(bf16[256,128]{1,0:T(8,128)(2,1)S(1)} %get-tuple-element.15), channel_id=1, source_target_pairs={{0,8},{4,12},{8,0},{12,4},{1,9},{5,13},{9,1},{13,5},{2,10},{6,14},... | collective-permute-start | bytes 196616 | tf_op jit(solution)/shard_map/ppermute | solution.py:245
  10.5 5.5 %collective-permute-start.6 = (bf16[256,128]{1,0:T(8,128)(2,1)S(1)}, bf16[256,128]{1,0:T(8,128)(2,1)S(1)}, u32[]{:S(2)}, u32[]{:S(2)}) collective-permute-start(bf16[256,128]{1,0:T(8,128)(2,1)S(1)} %get-tuple-element.20), channel_id=1, source_target_pairs={{0,8},{4,12},{8,0},{12,4},{1,9},{5,13},{9,1},{13,5},{2,10},{6,14},... | collective-permute-start | bytes 196616 | tf_op jit(solution)/shard_map/ppermute | solution.py:245
  12.4 13.0 %copy-start.8 = (bf16[2,1024,128]{2,1,0:T(8,128)(2,1)S(1)}, bf16[2,1024,128]{2,1,0:T(8,128)(2,1)}, u32[]{:S(2)}) copy-start(bf16[2,1024,128]{2,1,0:T(8,128)(2,1)} %refs_6_.3) | copy-start | bytes 1572868
  12.4 5.2 %collective-permute-start.2 = (bf16[256,128]{1,0:T(8,128)(2,1)S(1)}, bf16[256,128]{1,0:T(8,128)(2,1)S(1)}, u32[]{:S(2)}, u32[]{:S(2)}) collective-permute-start(bf16[256,128]{1,0:T(8,128)(2,1)S(1)} %get-tuple-element.29), channel_id=1, source_target_pairs={{0,2},{2,0},{1,3},{3,1},{4,6},{6,4},{5,7},{7,5},{8,10},{10,8},{9,1... | collective-permute-start | bytes 196616 | tf_op jit(solution)/shard_map/ppermute | solution.py:252
  16.0 5.9 %collective-permute-start.7 = (bf16[256,128]{1,0:T(8,128)(2,1)S(1)}, bf16[256,128]{1,0:T(8,128)(2,1)S(1)}, u32[]{:S(2)}, u32[]{:S(2)}) collective-permute-start(bf16[256,128]{1,0:T(8,128)(2,1)S(1)} %get-tuple-element.25), channel_id=1, source_target_pairs={{0,2},{2,0},{1,3},{3,1},{4,6},{6,4},{5,7},{7,5},{8,10},{10,8},{9,1... | collective-permute-start | bytes 196616 | tf_op jit(solution)/shard_map/ppermute | solution.py:252
  17.6 6.2 %collective-permute-start.3 = (bf16[512,128]{1,0:T(8,128)(2,1)S(1)}, bf16[512,128]{1,0:T(8,128)(2,1)S(1)}, u32[]{:S(2)}, u32[]{:S(2)}) collective-permute-start(bf16[512,128]{1,0:T(8,128)(2,1)S(1)} %pad_maximum_fusion), channel_id=1, source_target_pairs={{0,4},{4,0},{8,12},{12,8},{1,5},{5,1},{9,13},{13,9},{2,6},{6,2},{1... | collective-permute-start | bytes 393224 | tf_op jit(solution)/shard_map/ppermute | solution.py:249
  19.9 7.1 %collective-permute-start.5 = (bf16[256,128]{1,0:T(8,128)(2,1)S(1)}, bf16[256,128]{1,0:T(8,128)(2,1)S(1)}, u32[]{:S(2)}, u32[]{:S(2)}) collective-permute-start(bf16[256,128]{1,0:T(8,128)(2,1)S(1)} %get-tuple-element.19.refs_0_), channel_id=1, source_target_pairs={{0,2},{2,0},{1,3},{3,1},{4,6},{6,4},{5,7},{7,5},{8,10},{10,8},{9,1... | collective-permute-start | bytes 196616 | tf_op jit(solution)/shard_map/ppermute | solution.py:252
  21.1 4.3 %collective-permute-start = (bf16[256,128]{1,0:T(8,128)(2,1)S(1)}, bf16[256,128]{1,0:T(8,128)(2,1)S(1)}, u32[]{:S(2)}, u32[]{:S(2)}) collective-permute-start(bf16[256,128]{1,0:T(8,128)(2,1)S(1)} %get-tuple-element.14.refs_0_), channel_id=1, source_target_pairs={{0,2},{2,0},{1,3},{3,1},{4,6},{6,4},{5,7},{7,5},{8,10},{10,8},{9,1... | collective-permute-start | bytes 196616 | tf_op jit(solution)/shard_map/ppermute | solution.py:252
  21.9 5.1 %collective-permute-start.8 = (bf16[512,128]{1,0:T(8,128)(2,1)S(1)}, bf16[512,128]{1,0:T(8,128)(2,1)S(1)}, u32[]{:S(2)}, u32[]{:S(2)}) collective-permute-start(bf16[512,128]{1,0:T(8,128)(2,1)S(1)} %pad_maximum_fusion.1), channel_id=1, source_target_pairs={{0,4},{4,0},{8,12},{12,8},{1,5},{5,1},{9,13},{13,9},{2,6},{6,2},{1... | collective-permute-start | bytes 393224 | tf_op jit(solution)/shard_map/ppermute | solution.py:249
  26.9 2.2 %collective-permute-start.4 = (f32[1,256,128]{2,1,0:T(8,128)S(1)}, f32[1,256,128]{2,1,0:T(8,128)S(1)}, u32[]{:S(2)}, u32[]{:S(2)}) collective-permute-start(f32[1,256,128]{2,1,0:T(8,128)S(1)} %get-tuple-element.17), channel_id=1, source_target_pairs={{0,1},{1,0},{2,3},{3,2},{4,5},{5,4},{6,7},{7,6},{8,9},{9,8},{10,11... | collective-permute-start | bytes 393224 | tf_op jit(solution)/shard_map/ppermute | solution.py:291
  27.0 2.1 %copy-start = (bf16[2,2,128,512]{3,2,1,0:T(8,128)(2,1)S(1)}, bf16[2,2,128,512]{3,2,1,0:T(8,128)(2,1)}, u32[]{:S(2)}) copy-start(bf16[2,2,128,512]{3,2,1,0:T(8,128)(2,1)} %win_ref.7) | copy-start | bytes 1572868
  27.1 2.1 %copy-start.1 = (bf16[2,512,128]{2,1,0:T(8,128)(2,1)S(1)}, bf16[2,512,128]{2,1,0:T(8,128)(2,1)}, u32[]{:S(2)}) copy-start(bf16[2,512,128]{2,1,0:T(8,128)(2,1)} %wout_ref.5) | copy-start | bytes 786436
  27.1 2.1 %copy-start.3 = (f32[8,32,128]{2,1,0:T(8,128)S(1)}, f32[8,32,128]{2,1,0:T(8,128)}, u32[]{:S(2)}) copy-start(f32[8,32,128]{2,1,0:T(8,128)} %param.14) | copy-start | bytes 393220
  27.1 2.1 %copy-start.7 = (f32[2,128]{1,0:T(2,128)S(1)}, f32[2,128]{1,0:T(2,128)}, u32[]{:S(2)}) copy-start(f32[2,128]{1,0:T(2,128)} %g_ref.3) | copy-start | bytes 3076
  28.6 1.9 %collective-permute-start.9 = (f32[1,256,128]{2,1,0:T(8,128)S(1)}, f32[1,256,128]{2,1,0:T(8,128)S(1)}, u32[]{:S(2)}, u32[]{:S(2)}) collective-permute-start(f32[1,256,128]{2,1,0:T(8,128)S(1)} %get-tuple-element.22), channel_id=1, source_target_pairs={{0,1},{1,0},{2,3},{3,2},{4,5},{5,4},{6,7},{7,6},{8,9},{9,8},{10,11... | collective-permute-start | bytes 393224 | tf_op jit(solution)/shard_map/ppermute | solution.py:291
  29.2 0.7 %copy-start.6 = (f32[2,128]{1,0:T(2,128)S(1)}, f32[2,128]{1,0:T(2,128)}, u32[]{:S(2)}) copy-start(f32[2,128]{1,0:T(2,128)} %b_ref.3) | copy-start | bytes 3076

commit v2 on v1

v2 whole, which is shorter than its diff:
```python
import functools

import jax
import jax.numpy as jnp
from jax import lax
from jax.experimental import pallas as pl
from jax.experimental.pallas import tpu as pltpu
from jax.sharding import PartitionSpec as P

NUM_MODULES = 2
LANES = 128
SUB = 8
F32 = jnp.float32
BF16 = jnp.bfloat16
VMEM_LIMIT = 32 * 1024 * 1024


def dot_tn(a, b):
    return lax.dot_general(a, b, (((0,), (0,)), ((), ())), preferred_element_type=F32)


def dot_nt(a, b):
    return lax.dot_general(a, b, (((1,), (1,)), ((), ())), preferred_element_type=F32)


def dot_nn(a, b):
    return lax.dot_general(a, b, (((1,), (0,)), ((), ())), preferred_element_type=F32)


def silu_of_double(x):
    return x * jnp.tanh(x) + x


def norm_rows(m, gain):
    mean = jnp.mean(m, axis=0, keepdims=True)
    centered = m - mean
    var = jnp.mean(centered * centered, axis=0, keepdims=True)
    return centered * lax.rsqrt(var + 1e-05) * gain


def norm_lanes(x, gain):
    mean = jnp.mean(x, axis=1, keepdims=True)
    centered = x - mean
    var = jnp.mean(centered * centered, axis=1, keepdims=True)
    return centered * lax.rsqrt(var + 1e-05) * gain


def msa_module(step, seqs, amino, m_ref, gains, w_in, w_out, w_l, w_r, m_out, left_out, right_out, ls):
    width = w_r.shape[1]
    per = 8
    lanes = per * seqs
    three = len(m_ref.shape) == 3
    gain1 = jnp.concatenate([gains[step, 0]] * per, axis=1)
    gain2 = jnp.concatenate([gains[step, 1]] * per, axis=1)
    for start in range(0, amino, per):
        here = slice(start * seqs, start * seqs + lanes)
        if three:
            m = jnp.concatenate([m_ref[start + k] for k in range(per)], axis=1).astype(F32)
        else:
            m = m_ref[:, here]
        xm = norm_rows(m, gain1).astype(BF16)
        gate = dot_nn(w_in[step, 0], xm)
        upper = dot_nn(w_in[step, 1], xm)
        hidden = (silu_of_double(gate) * upper).astype(BF16)
        m = m + dot_nn(w_out[step], hidden)
        if m_out is not None:
            m_out[:, here] = m
        xo = norm_rows(m, gain2).astype(BF16)
        right = dot_nn(w_r[step], xo)
        if left_out is not None:
            left = dot_nn(w_l[step], xo)
        for k in range(per):
            rows = slice((start + k) * width, (start + k + 1) * width)
            right_out[rows, :] = right[:, k * seqs : (k + 1) * seqs].astype(BF16)
            if left_out is not None:
                ls[rows, :] = left[:, k * seqs : (k + 1) * seqs]
    if left_out is not None:
        for p in range(0, width, 2):
            pair = [ls[pl.ds(p + k, amino, stride=width), :] for k in range(2)]
            left_out[p * amino : (p + 2) * amino, :] = jnp.concatenate(pair, axis=0).astype(BF16)


def own_kernel(seqs, amino, n_first, n_load, *refs):
    srcs, refs = refs[:n_load], refs[n_load:]
    (lefts_out, rights_out, gains, w_in), refs = refs[:4], refs[4:]
    dsts, (m_ref, g1_ref, win_ref, g2_ref, state, ls, sems) = refs[: n_load - 4], refs[n_load - 4 :]
    dsts = (m_ref, g1_ref, win_ref, g2_ref) + tuple(dsts)
    copies = [pltpu.make_async_copy(s, d, sems.at[k]) for k, (s, d) in enumerate(zip(srcs, dsts))]
    for copy in copies:
        copy.start()
    for copy in copies[:n_first]:
        copy.wait()
    w_out, w_l, w_r = dsts[4:7]
    for step in range(NUM_MODULES):
        for k, g_ref in enumerate((g1_ref, g2_ref)):
            row = g_ref[step : step + 1, :]
            gains[step, k] = jnp.broadcast_to(row, (seqs, row.shape[1])).T
        for k in range(2):
            w_in[step, k] = win_ref[step, k].T * (1.0 if k else 0.5)
    for step in range(NUM_MODULES):
        source = state if step else m_ref
        target = None if step == NUM_MODULES - 1 else state
        msa_module(
            step, seqs, amino, source, gains, w_in, w_out, w_l, w_r, target, lefts_out.at[step], rights_out.at[step], ls
        )
    for copy in copies[n_first:]:
        copy.wait()


def own_call(seqs, amino, load, n_first):
    m, g1, win, g2, w_out, w_l, w_r = load[:7]
    width, feats, hidden = w_l.shape[1], win.shape[2], win.shape[3]
    factor = jax.ShapeDtypeStruct((NUM_MODULES, amino * width, seqs), BF16)
    outs = [
        factor,
        factor,
        jax.ShapeDtypeStruct((NUM_MODULES, 2, feats, seqs), F32),
        jax.ShapeDtypeStruct((NUM_MODULES, 2, hidden, feats), BF16),
    ]
    outs += [jax.ShapeDtypeStruct(x.shape, x.dtype) for x in load[4:]]
    load = [pltpu.with_memory_space_constraint(x, pltpu.HBM) for x in load]
    got = pl.pallas_call(
        functools.partial(own_kernel, seqs, amino, n_first, len(load)),
        out_shape=outs,
        in_specs=[pl.BlockSpec(memory_space=pltpu.HBM)] * len(load),
        out_specs=[pl.BlockSpec(memory_space=pltpu.VMEM)] * len(outs),
        scratch_shapes=[pltpu.VMEM(x.shape, x.dtype) for x in load[:4]]
        + [
            pltpu.VMEM((feats, amino * seqs), F32),
            pltpu.VMEM((amino * width, seqs), F32),
            pltpu.SemaphoreType.DMA((len(load),)),
        ],
        compiler_params=pltpu.CompilerParams(vmem_limit_bytes=VMEM_LIMIT),
        cost_estimate=pl.CostEstimate(flops=4_000_000_000, bytes_accessed=500_000, transcendentals=0),
        name="own",
    )(*load)
    return list(got[:4]), list(got[4:])


def far_kernel(seqs, amino, m_ref, gains, w_in, w_out, w_r, right_out, state):
    for step in range(NUM_MODULES):
        source = state if step else m_ref
        target = None if step == NUM_MODULES - 1 else state
        msa_module(
            step, seqs, amino, source, gains, w_in, w_out, None, w_r, target, None, right_out.at[step], None
        )


def far_call(seqs, amino, m, gains, w_in, w_out, w_r):
    return pl.pallas_call(
        functools.partial(far_kernel, seqs, amino),
        out_shape=jax.ShapeDtypeStruct((NUM_MODULES, amino * w_r.shape[1], seqs), BF16),
        in_specs=[pl.BlockSpec(memory_space=pltpu.VMEM)] * 5,
        out_specs=pl.BlockSpec(memory_space=pltpu.VMEM),
        scratch_shapes=[pltpu.VMEM((w_in.shape[3], amino * seqs), F32)],
        compiler_params=pltpu.CompilerParams(vmem_limit_bytes=VMEM_LIMIT),
        cost_estimate=pl.CostEstimate(flops=3_000_000_000, bytes_accessed=500_000, transcendentals=0),
        name="far",
    )(m, gains, w_in, w_out, w_r)


def swap_groups(parts, width):
    n = len(parts)
    lanes = parts[0].shape[1]
    group = lax.broadcasted_iota(jnp.int32, parts[0].shape, 1) // width
    bit = 1
    while bit < n:
        low = (group & bit) == 0
        shift = bit * width
        new = list(parts)
        for a in range(n):
            if a & bit == 0:
                x, y = parts[a], parts[a | bit]
                new[a] = jnp.where(low, x, pltpu.roll(y, shift, 1))
                new[a | bit] = jnp.where(low, pltpu.roll(x, lanes - shift, 1), y)
        parts = new
        bit *= 2
    return parts


def pair_kernel(step, n_row, n_col, n_dep, amino, width, depth, starts, *refs):
    lefts, refs = refs[:n_col], refs[n_col:]
    rights, refs = refs[:n_row], refs[n_row:]
    w_ref, b_ref, keep_ref, send_ref, ls, rs = refs
    ratio = n_row // n_col
    per_dep = n_col // n_dep
    block, seqs = amino * width, rs.shape[1]
    row, col, dep = lax.axis_index("row"), lax.axis_index("col"), lax.axis_index("dep")
    for dc in range(n_col):
        source = lax.rem(col - dc + n_col, n_col)
        slot = lax.rem(source - dep * per_dep + n_col, n_col)
        ls[slot] = lefts[dc][starts[dc], step].astype(F32)
    for dr in range(ratio):
        off = lax.rem(lax.rem(row, ratio) - dr + ratio, ratio)
        for dc in range(n_col):
            source = lax.rem(col - dc + n_col, n_col)
            k = dr * n_col + dc
            rs[pl.ds(pl.multiple_of((off * n_col + source) * block, block), block), :] = rights[k][starts[n_col + k], step]
    pair_ch = w_ref.shape[2]
    groups = LANES // width
    both = 2 * amino
    tiles = n_row * block // LANES
    rows_tile = groups * amino

    def right(t):
        if isinstance(t, int):
            return rs[t * LANES : (t + 1) * LANES, :]
        return rs[pl.ds(pl.multiple_of(t * LANES, LANES), LANES), :]

    def swapped(outer):
        bigs = []
        for big in range(width // groups):
            first = big * groups
            bigs.append(
                swap_groups([outer[(first + k) * both : (first + k + 1) * both] for k in range(groups)], width)
            )
        return jnp.concatenate([jnp.concatenate([x[k] for x in bigs], axis=1) for k in range(groups)], axis=0)

    for u in range(per_dep):
        left = jnp.concatenate(
            [ls[u].reshape(width, amino, seqs), ls[per_dep + u].reshape(width, amino, seqs)], axis=1
        )
        left = left.reshape(width * both, seqs).astype(BF16)

        def multiply(t):
            return dot_nt(left, right(t)).astype(BF16)

        def finish(t, lhs):
            got = (dot_nn(lhs, w_ref[step]) * (1.0 / depth)).reshape(groups, both, pair_ch)
            rows = pl.ds(t * rows_tile, rows_tile)
            keep_ref[u, rows, :] = got[:, :amino].reshape(rows_tile, pair_ch) + b_ref[step : step + 1, :]
            send_ref[u, rows, :] = got[:, amino:].reshape(rows_tile, pair_ch)

        if tiles <= 8:
            outer, lhs = multiply(0), None
            for t in range(tiles + 1):
                after = multiply(t + 1) if t + 1 < tiles else None
                if t >= 1:
                    finish(t - 1, lhs)
                if t < tiles:
                    lhs = swapped(outer)
                outer = after
        else:
            lax.fori_loop(0, tiles, lambda t, _: (finish(t, swapped(multiply(t))), 0)[1], 0)


def pair_call(step, n_row, n_col, n_dep, amino, width, depth, lefts, rights, w, b):
    rows = n_row * amino * amino
    pair_ch = w.shape[2]
    per_dep = n_col // n_dep
    factors, starts = zip(*lefts, *rights)
    seqs = factors[0].shape[-1]
    block = amino * width
    out = jax.ShapeDtypeStruct((per_dep, rows, pair_ch), F32)
    return pl.pallas_call(
        functools.partial(pair_kernel, step, n_row, n_col, n_dep, amino, width, depth, starts),
        out_shape=[out, out],
        in_specs=[pl.BlockSpec(memory_space=pltpu.VMEM)] * (n_col + n_row + 2),
        out_specs=[pl.BlockSpec(memory_space=pltpu.VMEM)] * 2,
        scratch_shapes=[
            pltpu.VMEM((n_col, block, seqs), F32),
            pltpu.VMEM((n_row * block, seqs), BF16),
        ],
        compiler_params=pltpu.CompilerParams(vmem_limit_bytes=VMEM_LIMIT),
        cost_estimate=pl.CostEstimate(flops=1_700_000_000, bytes_accessed=1_500_000, transcendentals=0),
        name="pair" + str(step),
    )(*factors, w, b)


def trans_kernel(step, first, last, amino, cols, z_ref, keep_ref, recv_ref, g_ref, win_ref, wout_ref, out_ref):
    for blk in range(keep_ref.shape[0]):
        base = blk * amino * cols
        if first:
            z = jnp.concatenate([z_ref[pl.ds(base + j, amino, stride=cols), :] for j in range(cols)], axis=0)
        else:
            z = z_ref[blk]
        z = z + (keep_ref[blk] + recv_ref[blk])
        xp = norm_lanes(z, g_ref[step : step + 1, :]).astype(BF16)
        gate = dot_nn(xp, win_ref[step, 0]) * 0.5
        upper = dot_nn(xp, win_ref[step, 1])
        hidden = (silu_of_double(gate) * upper).astype(BF16)
        z = z + dot_nn(hidden, wout_ref[step])
        if last:
            for j in range(cols):
                out_ref[pl.ds(base + j, amino, stride=cols), :] = z[j * amino : (j + 1) * amino, :]
        else:
            out_ref[blk] = z


def trans_call(step, amino, cols, z, keep, recv, g, win, wout):
    first, last = step == 0, step == NUM_MODULES - 1
    per_dep, rows, pair_ch = keep.shape
    shape = (per_dep * rows, pair_ch) if last else keep.shape
    return pl.pallas_call(
        functools.partial(trans_kernel, step, first, last, amino, cols),
        out_shape=jax.ShapeDtypeStruct(shape, F32),
        in_specs=[pl.BlockSpec(memory_space=pltpu.VMEM)] * 6,
        out_specs=pl.BlockSpec(memory_space=pltpu.VMEM),
        compiler_params=pltpu.CompilerParams(vmem_limit_bytes=VMEM_LIMIT),
        cost_estimate=pl.CostEstimate(flops=700_000_000, bytes_accessed=1_500_000, transcendentals=0),
        name="trans" + str(step),
    )(z, keep, recv, g, win, wout)


def per_device(n_row, n_col, n_dep, msa, pair, g_ff, w_in, w_out, g_op, w_l, w_r, w_res, b_res, g_pair, p_in, p_out):
    seqs, amino, feats = msa.shape
    width = w_l.shape[2]
    depth = seqs * n_dep
    ratio = n_row // n_col
    cols = amino * n_row
    row, col = lax.axis_index("row"), lax.axis_index("col")

    def rows_by(k):
        return lambda x: lax.ppermute(x, "row", [(r, (r + k) % n_row) for r in range(n_row)])

    def group_by(k):
        pairs = [(r, r // ratio * ratio + (r % ratio + k) % ratio) for r in range(n_row)]
        return lambda x: lax.ppermute(x, "row", pairs)

    def cols_by(k):
        return lambda x: lax.ppermute(x, "col", [(c, (c + k) % n_col) for c in range(n_col)])

    def pick(items, index):
        got = items[0]
        for k in range(1, len(items)):
            got = jnp.where(index == k, items[k], got)
        return got

    def spread_far(right):
        return [right] + [rows_by(k * ratio)(right) for k in range(1, n_col)]

    def moved(x, dr, dc):
        pairs = []
        for r in range(n_row):
            to = r // ratio * ratio + (r % ratio + dr) % ratio
            pairs += [(r * n_col + c, to * n_col + (c + dc) % n_col) for c in range(n_col)]
        return lax.ppermute(x, ("row", "col"), pairs)

    def spread(items):
        group = row // ratio
        wanted = [pick(items, (group - (col + dc) + 2 * n_col) % n_col) for dc in range(n_col)]
        steps = [(dr, dc) for dr in range(ratio) for dc in range(n_col)]
        got = [moved(wanted[dc], dr, dc) if dr or dc else wanted[0] for dr, dc in steps]
        return [(x[None], 0) for x in got]

    w_out, w_l, w_r = (w.transpose(0, 2, 1) for w in (w_out, w_l, w_r))
    m = msa.transpose(1, 2, 0)
    z = pair.reshape(-1, pair.shape[2])
    far = [rows_by(k * ratio)(m) for k in range(1, n_col)]
    load = [m, g_ff, w_in, g_op, w_out, w_l, w_r, w_res, b_res, g_pair, p_in, p_out, z]
    (left, right, gains, w_in), load = own_call(seqs, amino, load, 7)
    w_out, w_l, w_r, w_res, b_res, g_pair, p_in, p_out, z = load
    lefts = [left] + [cols_by(dc)(left) for dc in range(1, n_col)]
    lefts = [(x[None], 0) for x in lefts]
    rights = spread([right] + [far_call(seqs, amino, x, gains, w_in, w_out, w_r) for x in far])
    for step in range(NUM_MODULES):
        keep, send = pair_call(
            step, n_row, n_col, n_dep, amino, width, depth, lefts, rights, w_res, b_res
        )
        recv = lax.ppermute(send, "dep", [(d, (d + 1) % n_dep) for d in range(n_dep)])
        z = trans_call(step, amino, cols, z, keep, recv, g_pair, p_in, p_out)
    return z.reshape(pair.shape)


def solution(mesh):
    return jax.shard_map(
        functools.partial(per_device, mesh.shape["row"], mesh.shape["col"], mesh.shape["dep"]),
        mesh=mesh,
        in_specs=(
            P(("grp", "dep"), ("row", "col"), None),
            P(("grp", "row", "dep"), "col", None),
        )
        + (P(),) * 11,
        out_specs=P(("grp", "row", "dep"), "col", None),
        check_vma=False,
    )
```

time: 32 us -> 26.5 us (0.83)
  local copies, waits for them, and re-layouts: 3.4 us -> 0 us
  starting transfers between devices: 12.6 us -> 9.78 us
  waiting for transfers between devices: 6.93 us -> 7.64 us
    ppermute x2 -> x3, waiting for transfers between devices: 1.7 us -> 5.75 us  [moved(): return lax.ppermute(x, ('row', 'col'), pairs)]
    ppermute x4 -> x1, starting transfers between devices: 5.34 us -> 1.57 us  [cols_by(): lax.ppermute(x, 'col', [(c, (c + k) % n_col) for c in range(n_col)])]
    unnamed x28 -> x0, local copies, waits for them, and re-layouts: 3.38 us -> none
    ppermute x2 -> x1, waiting for transfers between devices: 3.61 us -> 1.56 us  [rows_by(): lax.ppermute(x, 'row', [(r, (r + k) % n_row) for r in range(n_row)])]
    ppermute x4 -> x1, waiting for transfers between devices: 1.61 us -> 0.01 us  [cols_by(): lax.ppermute(x, 'col', [(c, (c + k) % n_col) for c in range(n_col)])]
    pallas_call x2, Pallas kernels: 3.62 us -> 4.77 us  [the longest x1 3.37 us: own_call(): pl.pallas_call(functools.partial(own_kernel, seqs, amino, n_first, len(lo...]
    ppermute x2 -> x3, starting transfers between devices: 2.42 us -> 3.55 us  [moved(): return lax.ppermute(x, ('row', 'col'), pairs)]
    pallas_call x2, Pallas kernels: 3.05 us -> 2.09 us  [pair_call(): pl.pallas_call(functools.partial(pair_kernel, step, n_row, n_col, n_dep,...]
  transfers between devices with their start and end apart: 10 -> 7, of which waited for: 4 -> 5; matrix products, arithmetic and copies ran while one was open for 0% -> 0% of each run, Pallas kernels for 17% -> 25%
where the time goes in v2:
time: 26.5 us; the launch traced here: 26.3 us
  starting transfers between devices  9.78 us (37%)
  Pallas kernels  8.83 us (33%)
  waiting for transfers between devices  7.64 us (29%)
    ppermute x3, waiting for transfers between devices, moved(): return lax.ppermute(x, ('row', 'col'), pairs)  5.75 us
    ppermute x1, starting transfers between devices, rows_by(): lax.ppermute(x, 'row', [(r, (r + k) % n_row) for r in range(n_row)])  4.04 us
    ppermute x3, starting transfers between devices, moved(): return lax.ppermute(x, ('row', 'col'), pairs)  3.55 us
    pallas_call x1, Pallas kernels, own_call(): pl.pallas_call(functools.partial(own_kernel, seqs, amino, n_first, len(lo...  3.37 us
    pallas_call x2, Pallas kernels, pair_call(): pl.pallas_call(functools.partial(pair_kernel, step, n_row, n_col, n_dep,...  2.09 us
    pallas_call x2, Pallas kernels, trans_call(): pl.pallas_call(functools.partial(trans_kernel, step, first, last, amino,...  1.97 us
    ppermute x1, starting transfers between devices, cols_by(): lax.ppermute(x, 'col', [(c, (c + k) % n_col) for c in range(n_col)])  1.57 us
    ppermute x1, waiting for transfers between devices, rows_by(): lax.ppermute(x, 'row', [(r, (r + k) % n_row) for r in range(n_row)])  1.56 us
  transfers between devices with their start and end apart: 7, of which 5 were waited for; matrix products, arithmetic and copies ran while one was open for 0% of the time, Pallas kernels for 25%

profile of v2, /device:TPU:0, one launch (start us, length us, event | category | flops | bytes accessed | tf_op | source)
XLA Modules:
  0.0 26.3 jit_solution(1262079659687252777)
XLA Ops:
  0.0 4.0 %collective-permute-start.1 = (bf16[8,64,128]{2,1,0:T(8,128)(2,1)}, bf16[8,64,128]{2,1,0:T(8,128)(2,1)S(1)}, u32[]{:S(2)}, u32[]{:S(2)}) collective-permute-start(bf16[8,64,128]{2,1,0:T(8,128)(2,1)} %bitcast.25), channel_id=1, source_target_pairs={{0,8},{4,12},{8,0},{12,4},{1,9},{5,13},{9,1},{13,5},{2,10},{6,14},... | collective-permute-start | bytes 393224 | tf_op jit(solution)/shard_map/ppermute | solution.py:314
  4.0 3.4 %own.1 = (bf16[2,256,128]{2,1,0:T(8,128)(2,1)S(1)}, bf16[2,256,128]{2,1,0:T(8,128)(2,1)S(1)}, f32[2,2,64,128]{3,2,1,0:T(8,128)S(1)}, bf16[2,2,256,64]{3,2,1,0:T(...) custom-call(bf16[8,64,128]{2,1,0:T(8,128)(2,1)} %bitcast.26, ...), custom_call_target="tpu_custom_call" | custom-call | flops 4000000000 | bytes 500000 | tf_op jit(solution)/shard_map/own/pallas_call | solution.py:122
  7.4 1.6 %collective-permute-start = (bf16[2,256,128]{2,1,0:T(8,128)(2,1)S(1)}, bf16[2,256,128]{2,1,0:T(8,128)(2,1)S(1)}, u32[]{:S(2)}, u32[]{:S(2)}) collective-permute-start(bf16[2,256,128]{2,1,0:T(8,128)(2,1)S(1)} %get-tuple-element.22), channel_id=1, source_target_pairs={{0,2},{2,0},{1,3},{3,1},{4,6},{6,4},{5,7},{7,5},{8,10},{10,8},{9,1... | collective-permute-start | bytes 393224 | tf_op jit(solution)/shard_map/ppermute | solution.py:321
  9.0 1.6 %collective-permute-done.1.m_ref = bf16[8,64,128]{2,1,0:T(8,128)(2,1)S(1)} collective-permute-done((bf16[8,64,128]{2,1,0:T(8,128)(2,1)}, bf16[8,64,128]{2,1,0:T(8,128)(2,1)S(1)}, u32[]{:S(2)}, u32[]{:S(2)}) %collective-permute-start.1) | collective-permute-done | bytes 131104 | tf_op jit(solution)/shard_map/ppermute | solution.py:314
  10.6 1.4 %far.1 = bf16[2,256,128]{2,1,0:T(8,128)(2,1)S(1)} custom-call(bf16[8,64,128]{2,1,0:T(8,128)(2,1)S(1)} %collective-permute-done.1.m_ref, f32[2,2,64,128]{3,2,1,0:T(8,128)S(1)} %get-tuple-element.23.gains, bf16[2,2,256,64]{3,2,1,0:T(8,128)(2,1)S(1)} %get-tuple-element.24.w_in, bf16[2,64,256]{2,1,0:T(8,128)(2,1)S(1)} %get-tuple-element.25.w_out, ...), custom_call_target="tpu_custom_call" | custom-call | flops 3000000000 | bytes 500000 | tf_op jit(solution)/shard_map/far/pallas_call | solution.py:150
  12.0 1.6 %collective-permute-start.2 = (bf16[2,256,128]{2,1,0:T(8,128)(2,1)S(1)}, bf16[2,256,128]{2,1,0:T(8,128)(2,1)S(1)}, u32[]{:S(2)}, u32[]{:S(2)}) collective-permute-start(bf16[2,256,128]{2,1,0:T(8,128)(2,1)S(1)} %get-tuple-element.37), channel_id=1, source_target_pairs={{0,2},{2,0},{4,6},{6,4},{8,10},{10,8},{12,14},{14,12},{1,3},{3,1},... | collective-permute-start | bytes 393224 | tf_op jit(solution)/shard_map/ppermute | solution.py:337
  13.6 0.8 %collective-permute-start.3 = (bf16[2,256,128]{2,1,0:T(8,128)(2,1)S(1)}, bf16[2,256,128]{2,1,0:T(8,128)(2,1)S(1)}, u32[]{:S(2)}, u32[]{:S(2)}) collective-permute-start(bf16[2,256,128]{2,1,0:T(8,128)(2,1)S(1)} %get-tuple-element.38), channel_id=1, source_target_pairs={{0,4},{2,6},{4,0},{6,2},{8,12},{10,14},{12,8},{14,10},{1,5},{3,7},... | collective-permute-start | bytes 393224 | tf_op jit(solution)/shard_map/ppermute | solution.py:337
  14.4 1.2 %collective-permute-start.4 = (bf16[2,256,128]{2,1,0:T(8,128)(2,1)S(1)}, bf16[2,256,128]{2,1,0:T(8,128)(2,1)S(1)}, u32[]{:S(2)}, u32[]{:S(2)}) collective-permute-start(bf16[2,256,128]{2,1,0:T(8,128)(2,1)S(1)} %get-tuple-element.37), channel_id=1, source_target_pairs={{0,6},{2,4},{4,2},{6,0},{8,14},{10,12},{12,10},{14,8},{1,7},{3,5},... | collective-permute-start | bytes 393224 | tf_op jit(solution)/shard_map/ppermute | solution.py:337
  15.5 0.0 collective-permute-done
  15.5 1.8 %collective-permute-done.2 = bf16[2,256,128]{2,1,0:T(8,128)(2,1)S(1)} collective-permute-done((bf16[2,256,128]{2,1,0:T(8,128)(2,1)S(1)}, bf16[2,256,128]{2,1,0:T(8,128)(2,1)S(1)}, u32[]{:S(2)}, u32[]{:S(2)}) %collective-permute-start.2) | collective-permute-done | bytes 131104 | tf_op jit(solution)/shard_map/ppermute | solution.py:337
  17.4 1.9 %collective-permute-done.3 = bf16[2,256,128]{2,1,0:T(8,128)(2,1)S(1)} collective-permute-done((bf16[2,256,128]{2,1,0:T(8,128)(2,1)S(1)}, bf16[2,256,128]{2,1,0:T(8,128)(2,1)S(1)}, u32[]{:S(2)}, u32[]{:S(2)}) %collective-permute-start.3) | collective-permute-done | bytes 131104 | tf_op jit(solution)/shard_map/ppermute | solution.py:337
  19.2 2.1 %collective-permute-done.4 = bf16[2,256,128]{2,1,0:T(8,128)(2,1)S(1)} collective-permute-done((bf16[2,256,128]{2,1,0:T(8,128)(2,1)S(1)}, bf16[2,256,128]{2,1,0:T(8,128)(2,1)S(1)}, u32[]{:S(2)}, u32[]{:S(2)}) %collective-permute-start.4) | collective-permute-done | bytes 131104 | tf_op jit(solution)/shard_map/ppermute | solution.py:337
  21.3 1.0 %pair0.1 = (f32[1,256,128]{2,1,0:T(8,128)S(1)}, f32[1,256,128]{2,1,0:T(8,128)S(1)}) custom-call(bf16[1,2,256,128]{3,2,1,0:T(8,128)(2,1)S(1)} %bitcast.14, bf16[1,2,256,128]{3,2,1,0:T(8,128)(2,1)S(1)} %bitcast.16, bf16[1,2,256,128]{3,2,1,0:T(8,128)(2,1)S(1)} %bitcast.12, bf16[1,2,256,128]{3,2,1,0:T(8,128)(2,1)S(1)} %bitcast.18, ...), custom_call_target="tpu_custom_call" | custom-call | flops 1700000000 | bytes 1500000 | tf_op jit(solution)/shard_map/pair0/pallas_call | solution.py:255
  22.3 0.1 collective-permute-start.5
  22.4 1.1 %pair1.1 = (f32[1,256,128]{2,1,0:T(8,128)S(1)}, f32[1,256,128]{2,1,0:T(8,128)S(1)}) custom-call(bf16[1,2,256,128]{3,2,1,0:T(8,128)(2,1)S(1)} %bitcast.15, bf16[1,2,256,128]{3,2,1,0:T(8,128)(2,1)S(1)} %bitcast.17, bf16[1,2,256,128]{3,2,1,0:T(8,128)(2,1)S(1)} %bitcast.13, bf16[1,2,256,128]{3,2,1,0:T(8,128)(2,1)S(1)} %bitcast.19, ...), custom_call_target="tpu_custom_call" | custom-call | flops 1700000000 | bytes 1500000 | tf_op jit(solution)/shard_map/pair1/pallas_call | solution.py:255
  23.5 0.5 %collective-permute-start.6 = (f32[1,256,128]{2,1,0:T(8,128)S(1)}, f32[1,256,128]{2,1,0:T(8,128)S(1)}, u32[]{:S(2)}, u32[]{:S(2)}) collective-permute-start(f32[1,256,128]{2,1,0:T(8,128)S(1)} %get-tuple-element.36), channel_id=1, source_target_pairs={{0,1},{1,0},{2,3},{3,2},{4,5},{5,4},{6,7},{7,6},{8,9},{9,8},{10,11... | collective-permute-start | bytes 393224 | tf_op jit(solution)/shard_map/ppermute | solution.py:360
  24.0 0.0 collective-permute-done.5.recv_ref
  24.0 0.7 %trans0.1.z_ref = f32[1,256,128]{2,1,0:T(8,128)S(1)} custom-call(f32[256,128]{1,0:T(8,128)S(1)} %get-tuple-element.21.z_ref, f32[1,256,128]{2,1,0:T(8,128)S(1)} %get-tuple-element.30.keep_ref, f32[1,256,128]{2,1,0:T(8,128)S(1)} %collective-permute-done.5.recv_ref, f32[2,128]{1,0:T(2,128)S(1)} %get-tuple-element.32.g_ref, ...), custom_call_target="tpu_custom_call" | custom-call | flops 700000000 | bytes 1500000 | tf_op jit(solution)/shard_map/trans0/pallas_call | solution.py:294
  24.7 0.3 %collective-permute-done.6.recv_ref = f32[1,256,128]{2,1,0:T(8,128)S(1)} collective-permute-done((f32[1,256,128]{2,1,0:T(8,128)S(1)}, f32[1,256,128]{2,1,0:T(8,128)S(1)}, u32[]{:S(2)}, u32[]{:S(2)}) %collective-permute-start.6) | collective-permute-done | bytes 131104 | tf_op jit(solution)/shard_map/ppermute | solution.py:360
  25.0 1.3 %trans1.1 = f32[256,128]{1,0:T(8,128)} custom-call(f32[1,256,128]{2,1,0:T(8,128)S(1)} %trans0.1.z_ref, f32[1,256,128]{2,1,0:T(8,128)S(1)} %get-tuple-element.35.keep_ref, f32[1,256,128]{2,1,0:T(8,128)S(1)} %collective-permute-done.6.recv_ref, f32[2,128]{1,0:T(2,128)S(1)} %get-tuple-element.32.g_ref, bf16[2,2,128,512]{3,2,1,0:T(8,128)(2,1)S(1)} %get-tuple-element.33.win_ref, ...), custom_call_target="tpu_custom_call" | custom-call | flops 700000000 | bytes 1500000 | tf_op jit(solution)/shard_map/trans1/pallas_call | solution.py:294
  (1 shorter events, 0.0 us)
Async XLA Ops:
  0.0 10.5 %collective-permute-start.1 = (bf16[8,64,128]{2,1,0:T(8,128)(2,1)}, bf16[8,64,128]{2,1,0:T(8,128)(2,1)S(1)}, u32[]{:S(2)}, u32[]{:S(2)}) collective-permute-start(bf16[8,64,128]{2,1,0:T(8,128)(2,1)} %bitcast.25), channel_id=1, source_target_pairs={{0,8},{4,12},{8,0},{12,4},{1,9},{5,13},{9,1},{13,5},{2,10},{6,14},... | collective-permute-start | bytes 393224 | tf_op jit(solution)/shard_map/ppermute | solution.py:314
  7.4 8.1 %collective-permute-start = (bf16[2,256,128]{2,1,0:T(8,128)(2,1)S(1)}, bf16[2,256,128]{2,1,0:T(8,128)(2,1)S(1)}, u32[]{:S(2)}, u32[]{:S(2)}) collective-permute-start(bf16[2,256,128]{2,1,0:T(8,128)(2,1)S(1)} %get-tuple-element.22), channel_id=1, source_target_pairs={{0,2},{2,0},{1,3},{3,1},{4,6},{6,4},{5,7},{7,5},{8,10},{10,8},{9,1... | collective-permute-start | bytes 393224 | tf_op jit(solution)/shard_map/ppermute | solution.py:321
  12.0 5.4 %collective-permute-start.2 = (bf16[2,256,128]{2,1,0:T(8,128)(2,1)S(1)}, bf16[2,256,128]{2,1,0:T(8,128)(2,1)S(1)}, u32[]{:S(2)}, u32[]{:S(2)}) collective-permute-start(bf16[2,256,128]{2,1,0:T(8,128)(2,1)S(1)} %get-tuple-element.37), channel_id=1, source_target_pairs={{0,2},{2,0},{4,6},{6,4},{8,10},{10,8},{12,14},{14,12},{1,3},{3,1},... | collective-permute-start | bytes 393224 | tf_op jit(solution)/shard_map/ppermute | solution.py:337
  13.6 5.6 %collective-permute-start.3 = (bf16[2,256,128]{2,1,0:T(8,128)(2,1)S(1)}, bf16[2,256,128]{2,1,0:T(8,128)(2,1)S(1)}, u32[]{:S(2)}, u32[]{:S(2)}) collective-permute-start(bf16[2,256,128]{2,1,0:T(8,128)(2,1)S(1)} %get-tuple-element.38), channel_id=1, source_target_pairs={{0,4},{2,6},{4,0},{6,2},{8,12},{10,14},{12,8},{14,10},{1,5},{3,7},... | collective-permute-start | bytes 393224 | tf_op jit(solution)/shard_map/ppermute | solution.py:337
  14.4 6.9 %collective-permute-start.4 = (bf16[2,256,128]{2,1,0:T(8,128)(2,1)S(1)}, bf16[2,256,128]{2,1,0:T(8,128)(2,1)S(1)}, u32[]{:S(2)}, u32[]{:S(2)}) collective-permute-start(bf16[2,256,128]{2,1,0:T(8,128)(2,1)S(1)} %get-tuple-element.37), channel_id=1, source_target_pairs={{0,6},{2,4},{4,2},{6,0},{8,14},{10,12},{12,10},{14,8},{1,7},{3,5},... | collective-permute-start | bytes 393224 | tf_op jit(solution)/shard_map/ppermute | solution.py:337
  22.3 1.7 %collective-permute-start.5 = (f32[1,256,128]{2,1,0:T(8,128)S(1)}, f32[1,256,128]{2,1,0:T(8,128)S(1)}, u32[]{:S(2)}, u32[]{:S(2)}) collective-permute-start(f32[1,256,128]{2,1,0:T(8,128)S(1)} %get-tuple-element.31), channel_id=1, source_target_pairs={{0,1},{1,0},{2,3},{3,2},{4,5},{5,4},{6,7},{7,6},{8,9},{9,8},{10,11... | collective-permute-start | bytes 393224 | tf_op jit(solution)/shard_map/ppermute | solution.py:360
  23.5 1.5 %collective-permute-start.6 = (f32[1,256,128]{2,1,0:T(8,128)S(1)}, f32[1,256,128]{2,1,0:T(8,128)S(1)}, u32[]{:S(2)}, u32[]{:S(2)}) collective-permute-start(f32[1,256,128]{2,1,0:T(8,128)S(1)} %get-tuple-element.36), channel_id=1, source_target_pairs={{0,1},{1,0},{2,3},{3,2},{4,5},{5,4},{6,7},{7,6},{8,9},{9,8},{10,11... | collective-permute-start | bytes 393224 | tf_op jit(solution)/shard_map/ppermute | solution.py:360

commit v3 on v2

--- a/solution.py
+++ b/solution.py
@@ -178,34 +178,30 @@
     return parts
 
 
-def pair_kernel(step, n_row, n_col, n_dep, amino, width, depth, starts, *refs):
+def pair_kernel(n_col, n_dep, amino, width, depth, starts, *refs):
+    n_right = len(starts) - n_col
     lefts, refs = refs[:n_col], refs[n_col:]
-    rights, refs = refs[:n_row], refs[n_row:]
-    w_ref, b_ref, keep_ref, send_ref, ls, rs = refs
-    ratio = n_row // n_col
+    rights, refs = refs[:n_right], refs[n_right:]
+    w_ref, b_ref, keep_ref, send_ref, ls = refs
     per_dep = n_col // n_dep
-    block, seqs = amino * width, rs.shape[1]
-    row, col, dep = lax.axis_index("row"), lax.axis_index("col"), lax.axis_index("dep")
+    block, seqs = ls.shape[2:]
+    pair_ch = w_ref.shape[2]
+    groups = LANES // width
+    both = 2 * amino
+    tiles = block // LANES
+    rows_tile = groups * amino
+    col, dep = lax.axis_index("col"), lax.axis_index("dep")
     for dc in range(n_col):
         source = lax.rem(col - dc + n_col, n_col)
         slot = lax.rem(source - dep * per_dep + n_col, n_col)
-        ls[slot] = lefts[dc][starts[dc], step].astype(F32)
-    for dr in range(ratio):
-        off = lax.rem(lax.rem(row, ratio) - dr + ratio, ratio)
-        for dc in range(n_col):
-            source = lax.rem(col - dc + n_col, n_col)
-            k = dr * n_col + dc
-            rs[pl.ds(pl.multiple_of((off * n_col + source) * block, block), block), :] = rights[k][starts[n_col + k], step]
-    pair_ch = w_ref.shape[2]
-    groups = LANES // width
-    both = 2 * amino
-    tiles = n_row * block // LANES
-    rows_tile = groups * amino
-
-    def right(t):
-        if isinstance(t, int):
-            return rs[t * LANES : (t + 1) * LANES, :]
-        return rs[pl.ds(pl.multiple_of(t * LANES, LANES), LANES), :]
+        for step in range(NUM_MODULES):
+            ls[slot, step] = lefts[dc][starts[dc], step].astype(F32)
+
+    def rows_of(step, u):
+        left = jnp.concatenate(
+            [ls[u, step].reshape(width, amino, seqs), ls[per_dep + u, step].reshape(width, amino, seqs)], axis=1
+        )
+        return left.reshape(width * both, seqs).astype(BF16)
 
     def swapped(outer):
         bigs = []
@@ -216,90 +212,115 @@
             )
         return jnp.concatenate([jnp.concatenate([x[k] for x in bigs], axis=1) for k in range(groups)], axis=0)
 
-    for u in range(per_dep):
-        left = jnp.concatenate(
-            [ls[u].reshape(width, amino, seqs), ls[per_dep + u].reshape(width, amino, seqs)], axis=1
-        )
-        left = left.reshape(width * both, seqs).astype(BF16)
-
-        def multiply(t):
-            return dot_nt(left, right(t)).astype(BF16)
-
-        def finish(t, lhs):
-            got = (dot_nn(lhs, w_ref[step]) * (1.0 / depth)).reshape(groups, both, pair_ch)
-            rows = pl.ds(t * rows_tile, rows_tile)
-            keep_ref[u, rows, :] = got[:, :amino].reshape(rows_tile, pair_ch) + b_ref[step : step + 1, :]
-            send_ref[u, rows, :] = got[:, amino:].reshape(rows_tile, pair_ch)
-
-        if tiles <= 8:
-            outer, lhs = multiply(0), None
-            for t in range(tiles + 1):
-                after = multiply(t + 1) if t + 1 < tiles else None
-                if t >= 1:
-                    finish(t - 1, lhs)
-                if t < tiles:
-                    lhs = swapped(outer)
-                outer = after
-        else:
-            lax.fori_loop(0, tiles, lambda t, _: (finish(t, swapped(multiply(t))), 0)[1], 0)
-
-
-def pair_call(step, n_row, n_col, n_dep, amino, width, depth, lefts, rights, w, b):
-    rows = n_row * amino * amino
+    left = {(step, u): rows_of(step, u) for step in range(NUM_MODULES) for u in range(per_dep)}
+    items = [
+        (step, u, k, t)
+        for step in range(NUM_MODULES)
+        for u in range(per_dep)
+        for k in range(n_right)
+        for t in range(tiles)
+    ]
+
+    def multiply(step, u, k, t):
+        tile = rights[k][starts[n_col + k], step, t * LANES : (t + 1) * LANES, :]
+        return dot_nt(left[step, u], tile).astype(BF16)
+
+    def finish(step, u, k, t, lhs):
+        got = (dot_nn(lhs, w_ref[step]) * (1.0 / depth)).reshape(groups, both, pair_ch)
+        rows = slice(t * rows_tile, (t + 1) * rows_tile)
+        keep_ref[step, u, k, rows, :] = got[:, :amino].reshape(rows_tile, pair_ch) + b_ref[step : step + 1, :]
+        send_ref[step, u, k, rows, :] = got[:, amino:].reshape(rows_tile, pair_ch)
+
+    outer, lhs = multiply(*items[0]), None
+    for n in range(len(items) + 1):
+        after = multiply(*items[n + 1]) if n + 1 < len(items) else None
+        if n >= 1:
+            finish(*items[n - 1], lhs)
+        if n < len(items):
+            lhs = swapped(outer)
+        outer = after
+
+
+def pair_call(name, n_col, n_dep, amino, width, depth, lefts, rights, w, b):
     pair_ch = w.shape[2]
     per_dep = n_col // n_dep
     factors, starts = zip(*lefts, *rights)
     seqs = factors[0].shape[-1]
-    block = amino * width
-    out = jax.ShapeDtypeStruct((per_dep, rows, pair_ch), F32)
+    out = jax.ShapeDtypeStruct((NUM_MODULES, per_dep, len(rights), amino * amino, pair_ch), F32)
     return pl.pallas_call(
-        functools.partial(pair_kernel, step, n_row, n_col, n_dep, amino, width, depth, starts),
+        functools.partial(pair_kernel, n_col, n_dep, amino, width, depth, starts),
         out_shape=[out, out],
-        in_specs=[pl.BlockSpec(memory_space=pltpu.VMEM)] * (n_col + n_row + 2),
+        in_specs=[pl.BlockSpec(memory_space=pltpu.VMEM)] * (len(factors) + 2),
         out_specs=[pl.BlockSpec(memory_space=pltpu.VMEM)] * 2,
-        scratch_shapes=[
-            pltpu.VMEM((n_col, block, seqs), F32),
-            pltpu.VMEM((n_row * block, seqs), BF16),
-        ],
+        scratch_shapes=[pltpu.VMEM((n_col, NUM_MODULES, amino * width, seqs), F32)],
         compiler_params=pltpu.CompilerParams(vmem_limit_bytes=VMEM_LIMIT),
-        cost_estimate=pl.CostEstimate(flops=1_700_000_000, bytes_accessed=1_500_000, transcendentals=0),
-        name="pair" + str(step),
+        cost_estimate=pl.CostEstimate(
+            flops=600_000_000 * len(rights), bytes_accessed=1_500_000, transcendentals=0
+        ),
+        name="pair" + name,
     )(*factors, w, b)
 
 
-def trans_kernel(step, first, last, amino, cols, z_ref, keep_ref, recv_ref, g_ref, win_ref, wout_ref, out_ref):
-    for blk in range(keep_ref.shape[0]):
-        base = blk * amino * cols
-        if first:
-            z = jnp.concatenate([z_ref[pl.ds(base + j, amino, stride=cols), :] for j in range(cols)], axis=0)
-        else:
-            z = z_ref[blk]
-        z = z + (keep_ref[blk] + recv_ref[blk])
+def trans_kernel(last, n_row, n_col, amino, cols, steps, done_steps, *refs):
+    n = sum(len(group) for group in steps)
+    parts, refs = refs[: 2 * len(steps)], refs[2 * len(steps) :]
+    done, refs = refs[: len(done_steps)], refs[len(done_steps) :]
+    z_ref, g_ref, win_ref, wout_ref, out_ref = refs
+    ratio = n_row // n_col
+    row, col = lax.axis_index("row"), lax.axis_index("col")
+    per_dep, size = parts[0].shape[1], amino * amino
+
+    def first_column(step):
+        off = lax.rem(lax.rem(row, ratio) - step[0] + ratio, ratio)
+        return (off * n_col + lax.rem(col - step[1] + n_col, n_col)) * amino
+
+    def places(steps):
+        return [
+            u * amino * cols + first_column(step) + j
+            for u in range(per_dep)
+            for step in steps
+            for j in range(amino)
+        ]
+
+    flat = [step for group in steps for step in group]
+    here = places(flat)
+    z = jnp.concatenate([z_ref[pl.ds(at, amino, stride=cols), :] for at in here], axis=0)
+    for step in range(NUM_MODULES):
+        moved = [
+            parts[2 * k][step, u, i] + parts[2 * k + 1][step, u, i]
+            for u in range(per_dep)
+            for k, group in enumerate(steps)
+            for i in range(len(group))
+        ]
+        z = z + jnp.concatenate(moved, axis=0)
         xp = norm_lanes(z, g_ref[step : step + 1, :]).astype(BF16)
         gate = dot_nn(xp, win_ref[step, 0]) * 0.5
         upper = dot_nn(xp, win_ref[step, 1])
         hidden = (silu_of_double(gate) * upper).astype(BF16)
         z = z + dot_nn(hidden, wout_ref[step])
-        if last:
-            for j in range(cols):
-                out_ref[pl.ds(base + j, amino, stride=cols), :] = z[j * amino : (j + 1) * amino, :]
-        else:
-            out_ref[blk] = z
-
-
-def trans_call(step, amino, cols, z, keep, recv, g, win, wout):
-    first, last = step == 0, step == NUM_MODULES - 1
-    per_dep, rows, pair_ch = keep.shape
-    shape = (per_dep * rows, pair_ch) if last else keep.shape
+    if last:
+        for k, at in enumerate(here):
+            out_ref[pl.ds(at, amino, stride=cols), :] = z[k * amino : (k + 1) * amino, :]
+        for x, group in zip(done, done_steps):
+            for k, at in enumerate(places([step for part in group for step in part])):
+                out_ref[pl.ds(at, amino, stride=cols), :] = x[k * amino : (k + 1) * amino, :]
+    else:
+        out_ref[...] = z
+
+
+def trans_call(name, last, n_row, n_col, amino, cols, steps, parts, done_steps, done, z, g, win, wout):
+    per_dep, pair_ch = parts[0].shape[1], z.shape[1]
+    n = sum(len(group) for group in steps)
+    shape = z.shape if last else (per_dep * n * amino * amino, pair_ch)
     return pl.pallas_call(
-        functools.partial(trans_kernel, step, first, last, amino, cols),
+        functools.partial(trans_kernel, last, n_row, n_col, amino, cols, steps, done_steps),
         out_shape=jax.ShapeDtypeStruct(shape, F32),
-        in_specs=[pl.BlockSpec(memory_space=pltpu.VMEM)] * 6,
+        in_specs=[pl.BlockSpec(memory_space=pltpu.VMEM)] * (len(parts) + len(done) + 4),
         out_specs=pl.BlockSpec(memory_space=pltpu.VMEM),
         compiler_params=pltpu.CompilerParams(vmem_limit_bytes=VMEM_LIMIT),
-        cost_estimate=pl.CostEstimate(flops=700_000_000, bytes_accessed=1_500_000, transcendentals=0),
-        name="trans" + str(step),
-    )(z, keep, recv, g, win, wout)
+        cost_estimate=pl.CostEstimate(flops=1_400_000_000, bytes_accessed=1_500_000, transcendentals=0),
+        name="trans" + name,
+    )(*parts, *done, z, g, win, wout)
 
 
 def per_device(n_row, n_col, n_dep, msa, pair, g_ff, w_in, w_out, g_op, w_l, w_r, w_res, b_res, g_pair, p_in, p_out):
@@ -339,9 +360,7 @@
     def spread(items):
         group = row // ratio
         wanted = [pick(items, (group - (col + dc) + 2 * n_col) % n_col) for dc in range(n_col)]
-        steps = [(dr, dc) for dr in range(ratio) for dc in range(n_col)]
-        got = [moved(wanted[dc], dr, dc) if dr or dc else wanted[0] for dr, dc in steps]
-        return [(x[None], 0) for x in got]
+        return lambda dr, dc: moved(wanted[dc], dr, dc) if dr or dc else wanted[0]
 
     w_out, w_l, w_r = (w.transpose(0, 2, 1) for w in (w_out, w_l, w_r))
     m = msa.transpose(1, 2, 0)
@@ -352,13 +371,21 @@
     w_out, w_l, w_r, w_res, b_res, g_pair, p_in, p_out, z = load
     lefts = [left] + [cols_by(dc)(left) for dc in range(1, n_col)]
     lefts = [(x[None], 0) for x in lefts]
-    rights = spread([right] + [far_call(seqs, amino, x, gains, w_in, w_out, w_r) for x in far])
-    for step in range(NUM_MODULES):
-        keep, send = pair_call(
-            step, n_row, n_col, n_dep, amino, width, depth, lefts, rights, w_res, b_res
-        )
-        recv = lax.ppermute(send, "dep", [(d, (d + 1) % n_dep) for d in range(n_dep)])
-        z = trans_call(step, amino, cols, z, keep, recv, g_pair, p_in, p_out)
+    take = spread([right] + [far_call(seqs, amino, x, gains, w_in, w_out, w_r) for x in far])
+    steps = [[(0, dc) for dc in range(n_col)]]
+    for dr in range(1, ratio):
+        group = [(dr, dc) for dc in range(n_col)]
+        steps += [[step] for step in group] if ratio <= 2 else [group]
+    got = [[(take(*step)[None], 0) for step in group] for group in steps]
+    parts = []
+    for k, rights in enumerate(got):
+        keep, send = pair_call(str(k), n_col, n_dep, amino, width, depth, lefts, rights, w_res, b_res)
+        parts += [keep, lax.ppermute(send, "dep", [(d, (d + 1) % n_dep) for d in range(n_dep)])]
+    call = lambda name, last, *args: trans_call(
+        name, last, n_row, n_col, amino, cols, *args, z, g_pair, p_in, p_out
+    )
+    most = call("0", False, steps[:-1], parts[:-2], [], [])
+    z = call("1", True, steps[-1:], parts[-2:], [steps[:-1]], [most])
     return z.reshape(pair.shape)
 
 

time: 26.5 us -> 25.2 us (0.951)
  waiting for transfers between devices: 7.64 us -> 5.41 us
  Pallas kernels: 8.83 us -> 10.1 us
  starting transfers between devices: 9.78 us -> 9.37 us
    ppermute x3, waiting for transfers between devices: 5.75 us -> 3.73 us  [moved(): return lax.ppermute(x, ('row', 'col'), pairs)]
    pallas_call x4 -> x5, Pallas kernels: 4.06 us -> 5.38 us  [the longest x2 2.8 us: trans_call(): pl.pallas_call(functools.partial(trans_kernel, last, n_row, n_col, amino,...]
    ppermute x2 -> x3, starting transfers between devices: 0.62 us -> 0.21 us  [per_device(): lax.ppermute(send, 'dep', [(d, (d + 1) % n_dep) for d in range(n_dep)])]
  transfers between devices with their start and end apart: 7 -> 8, of which waited for: 5 -> 5; matrix products, arithmetic and copies ran while one was open for 0% -> 0% of each run, Pallas kernels for 25% -> 34%
where the time goes in v3:
time: 25.2 us; the launch traced here: 25 us
  Pallas kernels  10.1 us (40%)
  starting transfers between devices  9.37 us (37%)
  waiting for transfers between devices  5.41 us (21%)
    ppermute x1, starting transfers between devices, rows_by(): lax.ppermute(x, 'row', [(r, (r + k) % n_row) for r in range(n_row)])  4.04 us
    ppermute x3, waiting for transfers between devices, moved(): return lax.ppermute(x, ('row', 'col'), pairs)  3.73 us
    ppermute x3, starting transfers between devices, moved(): return lax.ppermute(x, ('row', 'col'), pairs)  3.55 us
    pallas_call x1, Pallas kernels, own_call(): pl.pallas_call(functools.partial(own_kernel, seqs, amino, n_first, len(lo...  3.37 us
    pallas_call x2, Pallas kernels, trans_call(): pl.pallas_call(functools.partial(trans_kernel, last, n_row, n_col, amino,...  2.8 us
    pallas_call x3, Pallas kernels, pair_call(): pl.pallas_call(functools.partial(pair_kernel, n_col, n_dep, amino, width,...  2.58 us
    ppermute x1, waiting for transfers between devices, rows_by(): lax.ppermute(x, 'row', [(r, (r + k) % n_row) for r in range(n_row)])  1.57 us
    ppermute x1, starting transfers between devices, cols_by(): lax.ppermute(x, 'col', [(c, (c + k) % n_col) for c in range(n_col)])  1.57 us
  transfers between devices with their start and end apart: 8, of which 5 were waited for; matrix products, arithmetic and copies ran while one was open for 0% of the time, Pallas kernels for 34%

profile of v3, /device:TPU:0, one launch (start us, length us, event | category | flops | bytes accessed | tf_op | source)
XLA Modules:
  0.0 25.0 jit_solution(1192190874716245343)
XLA Ops:
  0.0 4.0 %collective-permute-start.1 = (bf16[8,64,128]{2,1,0:T(8,128)(2,1)}, bf16[8,64,128]{2,1,0:T(8,128)(2,1)S(1)}, u32[]{:S(2)}, u32[]{:S(2)}) collective-permute-start(bf16[8,64,128]{2,1,0:T(8,128)(2,1)} %bitcast.23), channel_id=1, source_target_pairs={{0,8},{4,12},{8,0},{12,4},{1,9},{5,13},{9,1},{13,5},{2,10},{6,14},... | collective-permute-start | bytes 393224 | tf_op jit(solution)/shard_map/ppermute | solution.py:335
  4.0 3.4 %own.1 = (bf16[2,256,128]{2,1,0:T(8,128)(2,1)S(1)}, bf16[2,256,128]{2,1,0:T(8,128)(2,1)S(1)}, f32[2,2,64,128]{3,2,1,0:T(8,128)S(1)}, bf16[2,2,256,64]{3,2,1,0:T(...) custom-call(bf16[8,64,128]{2,1,0:T(8,128)(2,1)} %bitcast.24, ...), custom_call_target="tpu_custom_call" | custom-call | flops 4000000000 | bytes 500000 | tf_op jit(solution)/shard_map/own/pallas_call | solution.py:122
  7.4 1.6 %collective-permute-start = (bf16[2,256,128]{2,1,0:T(8,128)(2,1)S(1)}, bf16[2,256,128]{2,1,0:T(8,128)(2,1)S(1)}, u32[]{:S(2)}, u32[]{:S(2)}) collective-permute-start(bf16[2,256,128]{2,1,0:T(8,128)(2,1)S(1)} %get-tuple-element.23), channel_id=1, source_target_pairs={{0,2},{2,0},{1,3},{3,1},{4,6},{6,4},{5,7},{7,5},{8,10},{10,8},{9,1... | collective-permute-start | bytes 393224 | tf_op jit(solution)/shard_map/ppermute | solution.py:342
  9.0 1.6 %collective-permute-done.1.m_ref = bf16[8,64,128]{2,1,0:T(8,128)(2,1)S(1)} collective-permute-done((bf16[8,64,128]{2,1,0:T(8,128)(2,1)}, bf16[8,64,128]{2,1,0:T(8,128)(2,1)S(1)}, u32[]{:S(2)}, u32[]{:S(2)}) %collective-permute-start.1) | collective-permute-done | bytes 131104 | tf_op jit(solution)/shard_map/ppermute | solution.py:335
  10.6 1.4 %far.1 = bf16[2,256,128]{2,1,0:T(8,128)(2,1)S(1)} custom-call(bf16[8,64,128]{2,1,0:T(8,128)(2,1)S(1)} %collective-permute-done.1.m_ref, f32[2,2,64,128]{3,2,1,0:T(8,128)S(1)} %get-tuple-element.24.gains, bf16[2,2,256,64]{3,2,1,0:T(8,128)(2,1)S(1)} %get-tuple-element.25.w_in, bf16[2,64,256]{2,1,0:T(8,128)(2,1)S(1)} %get-tuple-element.26.w_out, ...), custom_call_target="tpu_custom_call" | custom-call | flops 3000000000 | bytes 500000 | tf_op jit(solution)/shard_map/far/pallas_call | solution.py:150
  12.0 1.6 %collective-permute-start.4 = (bf16[2,256,128]{2,1,0:T(8,128)(2,1)S(1)}, bf16[2,256,128]{2,1,0:T(8,128)(2,1)S(1)}, u32[]{:S(2)}, u32[]{:S(2)}) collective-permute-start(bf16[2,256,128]{2,1,0:T(8,128)(2,1)S(1)} %get-tuple-element.42), channel_id=1, source_target_pairs={{0,2},{2,0},{4,6},{6,4},{8,10},{10,8},{12,14},{14,12},{1,3},{3,1},... | collective-permute-start | bytes 393224 | tf_op jit(solution)/shard_map/ppermute | solution.py:358
  13.6 0.8 %collective-permute-start.6 = (bf16[2,256,128]{2,1,0:T(8,128)(2,1)S(1)}, bf16[2,256,128]{2,1,0:T(8,128)(2,1)S(1)}, u32[]{:S(2)}, u32[]{:S(2)}) collective-permute-start(bf16[2,256,128]{2,1,0:T(8,128)(2,1)S(1)} %get-tuple-element.41), channel_id=1, source_target_pairs={{0,4},{2,6},{4,0},{6,2},{8,12},{10,14},{12,8},{14,10},{1,5},{3,7},... | collective-permute-start | bytes 393224 | tf_op jit(solution)/shard_map/ppermute | solution.py:358
  14.4 1.2 %collective-permute-start.2 = (bf16[2,256,128]{2,1,0:T(8,128)(2,1)S(1)}, bf16[2,256,128]{2,1,0:T(8,128)(2,1)S(1)}, u32[]{:S(2)}, u32[]{:S(2)}) collective-permute-start(bf16[2,256,128]{2,1,0:T(8,128)(2,1)S(1)} %get-tuple-element.42), channel_id=1, source_target_pairs={{0,6},{2,4},{4,2},{6,0},{8,14},{10,12},{12,10},{14,8},{1,7},{3,5},... | collective-permute-start | bytes 393224 | tf_op jit(solution)/shard_map/ppermute | solution.py:358
  15.5 0.0 collective-permute-done
  15.5 1.8 %collective-permute-done.4 = bf16[2,256,128]{2,1,0:T(8,128)(2,1)S(1)} collective-permute-done((bf16[2,256,128]{2,1,0:T(8,128)(2,1)S(1)}, bf16[2,256,128]{2,1,0:T(8,128)(2,1)S(1)}, u32[]{:S(2)}, u32[]{:S(2)}) %collective-permute-start.4) | collective-permute-done | bytes 131104 | tf_op jit(solution)/shard_map/ppermute | solution.py:358
  17.4 1.1 %pair0.1 = (f32[2,1,2,64,128]{4,3,2,1,0:T(8,128)S(1)}, f32[2,1,2,64,128]{4,3,2,1,0:T(8,128)S(1)}) custom-call(bf16[1,2,256,128]{3,2,1,0:T(8,128)(2,1)S(1)} %bitcast.13, bf16[1,2,256,128]{3,2,1,0:T(8,128)(2,1)S(1)} %bitcast.16, bf16[1,2,256,128]{3,2,1,0:T(8,128)(2,1)S(1)} %bitcast.12, bf16[1,2,256,128]{3,2,1,0:T(8,128)(2,1)S(1)} %bitcast.21, ...), custom_call_target="tpu_custom_call" | custom-call | flops 1200000000 | bytes 1500000 | tf_op jit(solution)/shard_map/pair0/pallas_call | solution.py:250
  18.5 0.1 collective-permute-start.5
  18.5 0.7 %collective-permute-done.6 = bf16[2,256,128]{2,1,0:T(8,128)(2,1)S(1)} collective-permute-done((bf16[2,256,128]{2,1,0:T(8,128)(2,1)S(1)}, bf16[2,256,128]{2,1,0:T(8,128)(2,1)S(1)}, u32[]{:S(2)}, u32[]{:S(2)}) %collective-permute-start.6) | collective-permute-done | bytes 131104 | tf_op jit(solution)/shard_map/ppermute | solution.py:358
  19.2 0.7 %pair1.1 = (f32[2,1,1,64,128]{4,3,2,1,0:T(8,128)S(1)}, f32[2,1,1,64,128]{4,3,2,1,0:T(8,128)S(1)}) custom-call(bf16[1,2,256,128]{3,2,1,0:T(8,128)(2,1)S(1)} %bitcast.14, bf16[1,2,256,128]{3,2,1,0:T(8,128)(2,1)S(1)} %bitcast.17, bf16[1,2,256,128]{3,2,1,0:T(8,128)(2,1)S(1)} %bitcast.20, bf16[2,1024,128]{2,1,0:T(8,128)(2,1)S(1)} %get-tuple-element.29.refs_3_.refs_4_, ...), custom_call_target="tpu_custom_call" | custom-call | flops 600000000 | bytes 1500000 | tf_op jit(solution)/shard_map/pair1/pallas_call | solution.py:250
  19.9 0.1 collective-permute-start.7
  20.0 1.3 %collective-permute-done.2 = bf16[2,256,128]{2,1,0:T(8,128)(2,1)S(1)} collective-permute-done((bf16[2,256,128]{2,1,0:T(8,128)(2,1)S(1)}, bf16[2,256,128]{2,1,0:T(8,128)(2,1)S(1)}, u32[]{:S(2)}, u32[]{:S(2)}) %collective-permute-start.2) | collective-permute-done | bytes 131104 | tf_op jit(solution)/shard_map/ppermute | solution.py:358
  21.3 0.7 %pair2.1 = (f32[2,1,1,64,128]{4,3,2,1,0:T(8,128)S(1)}, f32[2,1,1,64,128]{4,3,2,1,0:T(8,128)S(1)}) custom-call(bf16[1,2,256,128]{3,2,1,0:T(8,128)(2,1)S(1)} %bitcast.15, bf16[1,2,256,128]{3,2,1,0:T(8,128)(2,1)S(1)} %bitcast.18, bf16[1,2,256,128]{3,2,1,0:T(8,128)(2,1)S(1)} %bitcast.19, bf16[2,1024,128]{2,1,0:T(8,128)(2,1)S(1)} %get-tuple-element.29.refs_3_.refs_4_, ...), custom_call_target="tpu_custom_call" | custom-call | flops 600000000 | bytes 1500000 | tf_op jit(solution)/shard_map/pair2/pallas_call | solution.py:250
  22.0 0.1 collective-permute-start.3
  22.1 0.0 collective-permute-done.7.refs_3_
  22.1 0.0 collective-permute-done.5.refs_1_
  22.1 1.1 %trans0.1.refs_2_ = f32[192,128]{1,0:T(8,128)S(1)} custom-call(f32[2,1,2,64,128]{4,3,2,1,0:T(8,128)S(1)} %get-tuple-element.33.refs_0_, f32[2,1,2,64,128]{4,3,2,1,0:T(8,128)S(1)} %collective-permute-done.5.refs_1_, f32[2,1,1,64,128]{4,3,2,1,0:T(8,128)S(1)} %get-tuple-element.35.refs_2_, f32[2,1,1,64,128]{4,3,2,1,0:T(8,128)S(1)} %collective-permute-done.7.refs_3_, ...), custom_call_target="tpu_custom_call" | custom-call | flops 1400000000 | bytes 1500000 | tf_op jit(solution)/shard_map/trans0/pallas_call | solution.py:315
  23.3 0.1 collective-permute-done.3.refs_1_
  23.4 1.7 %trans1.1 = f32[256,128]{1,0:T(8,128)} custom-call(f32[2,1,1,64,128]{4,3,2,1,0:T(8,128)S(1)} %get-tuple-element.31.refs_0_, f32[2,1,1,64,128]{4,3,2,1,0:T(8,128)S(1)} %collective-permute-done.3.refs_1_, f32[192,128]{1,0:T(8,128)S(1)} %trans0.1.refs_2_, f32[256,128]{1,0:T(8,128)S(1)} %get-tuple-element.37.refs_4_.refs_3_, ...), custom_call_target="tpu_custom_call" | custom-call | flops 1400000000 | bytes 1500000 | tf_op jit(solution)/shard_map/trans1/pallas_call | solution.py:315
  (1 shorter events, 0.0 us)
Async XLA Ops:
  0.0 10.5 %collective-permute-start.1 = (bf16[8,64,128]{2,1,0:T(8,128)(2,1)}, bf16[8,64,128]{2,1,0:T(8,128)(2,1)S(1)}, u32[]{:S(2)}, u32[]{:S(2)}) collective-permute-start(bf16[8,64,128]{2,1,0:T(8,128)(2,1)} %bitcast.23), channel_id=1, source_target_pairs={{0,8},{4,12},{8,0},{12,4},{1,9},{5,13},{9,1},{13,5},{2,10},{6,14},... | collective-permute-start | bytes 393224 | tf_op jit(solution)/shard_map/ppermute | solution.py:335
  7.4 8.1 %collective-permute-start = (bf16[2,256,128]{2,1,0:T(8,128)(2,1)S(1)}, bf16[2,256,128]{2,1,0:T(8,128)(2,1)S(1)}, u32[]{:S(2)}, u32[]{:S(2)}) collective-permute-start(bf16[2,256,128]{2,1,0:T(8,128)(2,1)S(1)} %get-tuple-element.23), channel_id=1, source_target_pairs={{0,2},{2,0},{1,3},{3,1},{4,6},{6,4},{5,7},{7,5},{8,10},{10,8},{9,1... | collective-permute-start | bytes 393224 | tf_op jit(solution)/shard_map/ppermute | solution.py:342
  12.0 5.4 %collective-permute-start.4 = (bf16[2,256,128]{2,1,0:T(8,128)(2,1)S(1)}, bf16[2,256,128]{2,1,0:T(8,128)(2,1)S(1)}, u32[]{:S(2)}, u32[]{:S(2)}) collective-permute-start(bf16[2,256,128]{2,1,0:T(8,128)(2,1)S(1)} %get-tuple-element.42), channel_id=1, source_target_pairs={{0,2},{2,0},{4,6},{6,4},{8,10},{10,8},{12,14},{14,12},{1,3},{3,1},... | collective-permute-start | bytes 393224 | tf_op jit(solution)/shard_map/ppermute | solution.py:358
  13.6 5.6 %collective-permute-start.6 = (bf16[2,256,128]{2,1,0:T(8,128)(2,1)S(1)}, bf16[2,256,128]{2,1,0:T(8,128)(2,1)S(1)}, u32[]{:S(2)}, u32[]{:S(2)}) collective-permute-start(bf16[2,256,128]{2,1,0:T(8,128)(2,1)S(1)} %get-tuple-element.41), channel_id=1, source_target_pairs={{0,4},{2,6},{4,0},{6,2},{8,12},{10,14},{12,8},{14,10},{1,5},{3,7},... | collective-permute-start | bytes 393224 | tf_op jit(solution)/shard_map/ppermute | solution.py:358
  14.4 6.9 %collective-permute-start.2 = (bf16[2,256,128]{2,1,0:T(8,128)(2,1)S(1)}, bf16[2,256,128]{2,1,0:T(8,128)(2,1)S(1)}, u32[]{:S(2)}, u32[]{:S(2)}) collective-permute-start(bf16[2,256,128]{2,1,0:T(8,128)(2,1)S(1)} %get-tuple-element.42), channel_id=1, source_target_pairs={{0,6},{2,4},{4,2},{6,0},{8,14},{10,12},{12,10},{14,8},{1,7},{3,5},... | collective-permute-start | bytes 393224 | tf_op jit(solution)/shard_map/ppermute | solution.py:358
  18.5 3.7 %collective-permute-start.5 = (f32[2,1,2,64,128]{4,3,2,1,0:T(8,128)S(1)}, f32[2,1,2,64,128]{4,3,2,1,0:T(8,128)S(1)}, u32[]{:S(2)}, u32[]{:S(2)}) collective-permute-start(f32[2,1,2,64,128]{4,3,2,1,0:T(8,128)S(1)} %get-tuple-element.34), channel_id=1, source_target_pairs={{0,1},{1,0},{2,3},{3,2},{4,5},{5,4},{6,7},{7,6},{8,9},{9,8},{10,11... | collective-permute-start | bytes 393224 | tf_op jit(solution)/shard_map/ppermute | solution.py:383
  19.9 2.2 %collective-permute-start.7 = (f32[2,1,1,64,128]{4,3,2,1,0:T(8,128)S(1)}, f32[2,1,1,64,128]{4,3,2,1,0:T(8,128)S(1)}, u32[]{:S(2)}, u32[]{:S(2)}) collective-permute-start(f32[2,1,1,64,128]{4,3,2,1,0:T(8,128)S(1)} %get-tuple-element.36), channel_id=1, source_target_pairs={{0,1},{1,0},{2,3},{3,2},{4,5},{5,4},{6,7},{7,6},{8,9},{9,8},{10,11... | collective-permute-start | bytes 196616 | tf_op jit(solution)/shard_map/ppermute | solution.py:383
  22.0 1.3 %collective-permute-start.3 = (f32[2,1,1,64,128]{4,3,2,1,0:T(8,128)S(1)}, f32[2,1,1,64,128]{4,3,2,1,0:T(8,128)S(1)}, u32[]{:S(2)}, u32[]{:S(2)}) collective-permute-start(f32[2,1,1,64,128]{4,3,2,1,0:T(8,128)S(1)} %get-tuple-element.32), channel_id=1, source_target_pairs={{0,1},{1,0},{2,3},{3,2},{4,5},{5,4},{6,7},{7,6},{8,9},{9,8},{10,11... | collective-permute-start | bytes 196616 | tf_op jit(solution)/shard_map/ppermute | solution.py:383

commit v4 on v3

--- a/solution.py
+++ b/solution.py
@@ -83,14 +83,14 @@
 def own_kernel(seqs, amino, n_first, n_load, *refs):
     srcs, refs = refs[:n_load], refs[n_load:]
     (lefts_out, rights_out, gains, w_in), refs = refs[:4], refs[4:]
-    dsts, (m_ref, g1_ref, win_ref, g2_ref, state, ls, sems) = refs[: n_load - 4], refs[n_load - 4 :]
-    dsts = (m_ref, g1_ref, win_ref, g2_ref) + tuple(dsts)
+    dsts, (g1_ref, win_ref, g2_ref, state, ls, sems) = refs[: n_load - 3], refs[n_load - 3 :]
+    dsts = (g1_ref, win_ref, g2_ref) + tuple(dsts)
     copies = [pltpu.make_async_copy(s, d, sems.at[k]) for k, (s, d) in enumerate(zip(srcs, dsts))]
     for copy in copies:
         copy.start()
     for copy in copies[:n_first]:
         copy.wait()
-    w_out, w_l, w_r = dsts[4:7]
+    m_ref, w_out, w_l, w_r = dsts[3:7]
     for step in range(NUM_MODULES):
         for k, g_ref in enumerate((g1_ref, g2_ref)):
             row = g_ref[step : step + 1, :]
@@ -108,7 +108,7 @@
 
 
 def own_call(seqs, amino, load, n_first):
-    m, g1, win, g2, w_out, w_l, w_r = load[:7]
+    g1, win, g2, m, w_out, w_l, w_r = load[:7]
     width, feats, hidden = w_l.shape[1], win.shape[2], win.shape[3]
     factor = jax.ShapeDtypeStruct((NUM_MODULES, amino * width, seqs), BF16)
     outs = [
@@ -117,14 +117,14 @@
         jax.ShapeDtypeStruct((NUM_MODULES, 2, feats, seqs), F32),
         jax.ShapeDtypeStruct((NUM_MODULES, 2, hidden, feats), BF16),
     ]
-    outs += [jax.ShapeDtypeStruct(x.shape, x.dtype) for x in load[4:]]
+    outs += [jax.ShapeDtypeStruct(x.shape, x.dtype) for x in load[3:]]
     load = [pltpu.with_memory_space_constraint(x, pltpu.HBM) for x in load]
     got = pl.pallas_call(
         functools.partial(own_kernel, seqs, amino, n_first, len(load)),
         out_shape=outs,
         in_specs=[pl.BlockSpec(memory_space=pltpu.HBM)] * len(load),
         out_specs=[pl.BlockSpec(memory_space=pltpu.VMEM)] * len(outs),
-        scratch_shapes=[pltpu.VMEM(x.shape, x.dtype) for x in load[:4]]
+        scratch_shapes=[pltpu.VMEM(x.shape, x.dtype) for x in load[:3]]
         + [
             pltpu.VMEM((feats, amino * seqs), F32),
             pltpu.VMEM((amino * width, seqs), F32),
@@ -178,30 +178,41 @@
     return parts
 
 
-def pair_kernel(n_col, n_dep, amino, width, depth, starts, *refs):
-    n_right = len(starts) - n_col
-    lefts, refs = refs[:n_col], refs[n_col:]
-    rights, refs = refs[:n_right], refs[n_right:]
-    w_ref, b_ref, keep_ref, send_ref, ls = refs
+def pair_kernel(first, n_raw, n_col, n_dep, amino, width, depth, n_left, starts, *refs):
+    raw, refs = refs[:n_raw], refs[n_raw:]
+    lefts, refs = refs[:n_left], refs[n_left:]
+    rights, refs = refs[: len(starts)], refs[len(starts) :]
+    w_ref, b_ref, keep_ref, send_ref = refs[:4]
+    n_right = len(starts)
     per_dep = n_col // n_dep
-    block, seqs = ls.shape[2:]
     pair_ch = w_ref.shape[2]
     groups = LANES // width
     both = 2 * amino
-    tiles = block // LANES
+    tiles = amino * width // LANES
     rows_tile = groups * amino
-    col, dep = lax.axis_index("col"), lax.axis_index("dep")
-    for dc in range(n_col):
-        source = lax.rem(col - dc + n_col, n_col)
-        slot = lax.rem(source - dep * per_dep + n_col, n_col)
+    if first:
+        left, ls = refs[4:]
+        seqs = ls.shape[3]
+        col, dep = lax.axis_index("col"), lax.axis_index("dep")
+        for dc in range(n_col):
+            source = lax.rem(col - dc + n_col, n_col)
+            slot = lax.rem(source - dep * per_dep + n_col, n_col)
+            for step in range(NUM_MODULES):
+                ls[slot, step] = lefts[dc][step].astype(F32)
         for step in range(NUM_MODULES):
-            ls[slot, step] = lefts[dc][starts[dc], step].astype(F32)
-
-    def rows_of(step, u):
-        left = jnp.concatenate(
-            [ls[u, step].reshape(width, amino, seqs), ls[per_dep + u, step].reshape(width, amino, seqs)], axis=1
-        )
-        return left.reshape(width * both, seqs).astype(BF16)
+            for u in range(per_dep):
+                rows = jnp.concatenate(
+                    [ls[u, step].reshape(width, amino, seqs), ls[per_dep + u, step].reshape(width, amino, seqs)],
+                    axis=1,
+                )
+                left[step, u] = rows.reshape(width * both, seqs).astype(BF16)
+    else:
+        (left,) = lefts
+    if raw:
+        right, state = refs[4:]
+        far_kernel(left.shape[3], amino, *raw, right.at[0], state)
+        rights, starts = [right], (0,)
+        n_right = 1
 
     def swapped(outer):
         bigs = []
@@ -212,7 +223,6 @@
             )
         return jnp.concatenate([jnp.concatenate([x[k] for x in bigs], axis=1) for k in range(groups)], axis=0)
 
-    left = {(step, u): rows_of(step, u) for step in range(NUM_MODULES) for u in range(per_dep)}
     items = [
         (step, u, k, t)
         for step in range(NUM_MODULES)
@@ -222,7 +232,7 @@
     ]
 
     def multiply(step, u, k, t):
-        tile = rights[k][starts[n_col + k], step, t * LANES : (t + 1) * LANES, :]
+        tile = rights[k][starts[k], step, t * LANES : (t + 1) * LANES, :]
         return dot_nt(left[step, u], tile).astype(BF16)
 
     def finish(step, u, k, t, lhs):
@@ -241,24 +251,35 @@
         outer = after
 
 
-def pair_call(name, n_col, n_dep, amino, width, depth, lefts, rights, w, b):
+def pair_call(name, n_col, n_dep, amino, width, depth, lefts, rights, w, b, raw=()):
+    first = len(lefts) > 1
     pair_ch = w.shape[2]
     per_dep = n_col // n_dep
-    factors, starts = zip(*lefts, *rights)
-    seqs = factors[0].shape[-1]
-    out = jax.ShapeDtypeStruct((NUM_MODULES, per_dep, len(rights), amino * amino, pair_ch), F32)
+    factors, starts = zip(*rights) if rights else ((), ())
+    seqs = lefts[0].shape[-1]
+    n_right = max(len(rights), 1)
+    out = jax.ShapeDtypeStruct((NUM_MODULES, per_dep, n_right, amino * amino, pair_ch), F32)
+    outs, scratch = [out, out], []
+    if raw:
+        scratch += [
+            pltpu.VMEM((1, NUM_MODULES, amino * width, seqs), BF16),
+            pltpu.VMEM((raw[2].shape[3], amino * seqs), F32),
+        ]
+    if first:
+        outs.append(jax.ShapeDtypeStruct((NUM_MODULES, per_dep, 2 * amino * width, seqs), BF16))
+        scratch.append(pltpu.VMEM((n_col, NUM_MODULES, amino * width, seqs), F32))
     return pl.pallas_call(
-        functools.partial(pair_kernel, n_col, n_dep, amino, width, depth, starts),
-        out_shape=[out, out],
-        in_specs=[pl.BlockSpec(memory_space=pltpu.VMEM)] * (len(factors) + 2),
-        out_specs=[pl.BlockSpec(memory_space=pltpu.VMEM)] * 2,
-        scratch_shapes=[pltpu.VMEM((n_col, NUM_MODULES, amino * width, seqs), F32)],
+        functools.partial(pair_kernel, first, len(raw), n_col, n_dep, amino, width, depth, len(lefts), starts),
+        out_shape=outs,
+        in_specs=[pl.BlockSpec(memory_space=pltpu.VMEM)] * (len(raw) + len(lefts) + len(factors) + 2),
+        out_specs=[pl.BlockSpec(memory_space=pltpu.VMEM)] * len(outs),
+        scratch_shapes=scratch,
         compiler_params=pltpu.CompilerParams(vmem_limit_bytes=VMEM_LIMIT),
         cost_estimate=pl.CostEstimate(
-            flops=600_000_000 * len(rights), bytes_accessed=1_500_000, transcendentals=0
+            flops=600_000_000 * n_right + (3_000_000_000 if raw else 0), bytes_accessed=1_500_000, transcendentals=0
         ),
         name="pair" + name,
-    )(*factors, w, b)
+    )(*raw, *lefts, *factors, w, b)
 
 
 def trans_kernel(last, n_row, n_col, amino, cols, steps, done_steps, *refs):
@@ -366,20 +387,25 @@
     m = msa.transpose(1, 2, 0)
     z = pair.reshape(-1, pair.shape[2])
     far = [rows_by(k * ratio)(m) for k in range(1, n_col)]
-    load = [m, g_ff, w_in, g_op, w_out, w_l, w_r, w_res, b_res, g_pair, p_in, p_out, z]
+    load = [g_ff, w_in, g_op, m, w_out, w_l, w_r, w_res, b_res, g_pair, p_in, p_out, z]
     (left, right, gains, w_in), load = own_call(seqs, amino, load, 7)
-    w_out, w_l, w_r, w_res, b_res, g_pair, p_in, p_out, z = load
+    m, w_out, w_l, w_r, w_res, b_res, g_pair, p_in, p_out, z = load
     lefts = [left] + [cols_by(dc)(left) for dc in range(1, n_col)]
-    lefts = [(x[None], 0) for x in lefts]
-    take = spread([right] + [far_call(seqs, amino, x, gains, w_in, w_out, w_r) for x in far])
-    steps = [[(0, dc) for dc in range(n_col)]]
-    for dr in range(1, ratio):
-        group = [(dr, dc) for dc in range(n_col)]
-        steps += [[step] for step in group] if ratio <= 2 else [group]
-    got = [[(take(*step)[None], 0) for step in group] for group in steps]
+    others = [(dr, dc) for dr in range(ratio) for dc in range(n_col) if dr or dc]
+    others.sort(key=lambda step: (min(step[0], ratio - step[0]) + min(step[1], n_col - step[1])), reverse=True)
+    tools = (gains, w_in, w_out, w_r)
+    first = (spread([m] + far)(*others[0]), *tools)
+    take = spread([right] + [far_call(seqs, amino, x, *tools) for x in far])
+    per = -(-(len(others) - 1) // 2)
+    steps = [[(0, 0)], others[:1]] + [others[k : k + per] for k in range(1, len(others), per)]
     parts = []
-    for k, rights in enumerate(got):
-        keep, send = pair_call(str(k), n_col, n_dep, amino, width, depth, lefts, rights, w_res, b_res)
+    for k, group in enumerate(steps):
+        raw = first if k == 1 else ()
+        rights = [] if raw else [(take(*step)[None], 0) for step in group]
+        if k > 1:
+            lefts, parts[-2] = lax.optimization_barrier((lefts, parts[-2]))
+        keep, send, *lead = pair_call(str(k), n_col, n_dep, amino, width, depth, lefts, rights, w_res, b_res, raw)
+        lefts = lead or lefts
         parts += [keep, lax.ppermute(send, "dep", [(d, (d + 1) % n_dep) for d in range(n_dep)])]
     call = lambda name, last, *args: trans_call(
         name, last, n_row, n_col, amino, cols, *args, z, g_pair, p_in, p_out

time: 25.2 us -> 24.5 us (0.972)
  waiting for transfers between devices: 5.41 us -> 2.45 us
  Pallas kernels: 10.1 us -> 11.8 us
  starting transfers between devices: 9.37 us -> 10 us
    ppermute x3, waiting for transfers between devices: 3.73 us -> 0.81 us  [moved(): return lax.ppermute(x, ('row', 'col'), pairs)]
    pallas_call x3 -> x4, Pallas kernels: 2.58 us -> 4.22 us  [pair_call(): pl.pallas_call(functools.partial(pair_kernel, first, len(raw), n_col, n_d...]
    ppermute x3 -> x4, starting transfers between devices: 0.21 us -> 0.78 us  [per_device(): lax.ppermute(send, 'dep', [(d, (d + 1) % n_dep) for d in range(n_dep)])]
  transfers between devices with their start and end apart: 8 -> 9, of which waited for: 5 -> 2; matrix products, arithmetic and copies ran while one was open for 0% -> 0% of each run, Pallas kernels for 34% -> 42%
where the time goes in v4:
time: 24.5 us; the launch traced here: 24.3 us
  Pallas kernels  11.8 us (48%)
  starting transfers between devices  10 us (41%)
  waiting for transfers between devices  2.45 us (10%)
    pallas_call x4, Pallas kernels, pair_call(): pl.pallas_call(functools.partial(pair_kernel, first, len(raw), n_col, n_d...  4.22 us
    ppermute x1, starting transfers between devices, rows_by(): lax.ppermute(x, 'row', [(r, (r + k) % n_row) for r in range(n_row)])  4.04 us
    ppermute x3, starting transfers between devices, moved(): return lax.ppermute(x, ('row', 'col'), pairs)  3.62 us
    pallas_call x1, Pallas kernels, own_call(): pl.pallas_call(functools.partial(own_kernel, seqs, amino, n_first, len(lo...  3.38 us
    pallas_call x2, Pallas kernels, trans_call(): pl.pallas_call(functools.partial(trans_kernel, last, n_row, n_col, amino,...  2.79 us
    ppermute x1, waiting for transfers between devices, rows_by(): lax.ppermute(x, 'row', [(r, (r + k) % n_row) for r in range(n_row)])  1.57 us
    ppermute x1, starting transfers between devices, cols_by(): lax.ppermute(x, 'col', [(c, (c + k) % n_col) for c in range(n_col)])  1.56 us
    pallas_call x1, Pallas kernels, far_call(): pl.pallas_call(functools.partial(far_kernel, seqs, amino), out_shape=jax....  1.39 us
  transfers between devices with their start and end apart: 9, of which 2 were waited for; matrix products, arithmetic and copies ran while one was open for 0% of the time, Pallas kernels for 42%

profile of v4, /device:TPU:0, one launch (start us, length us, event | category | flops | bytes accessed | tf_op | source)
XLA Modules:
  0.0 24.3 jit_solution(9884232113887168179)
XLA Ops:
  0.0 4.0 %collective-permute-start.1 = (bf16[8,64,128]{2,1,0:T(8,128)(2,1)}, bf16[8,64,128]{2,1,0:T(8,128)(2,1)S(1)}, u32[]{:S(2)}, u32[]{:S(2)}) collective-permute-start(bf16[8,64,128]{2,1,0:T(8,128)(2,1)} %bitcast.13), channel_id=1, source_target_pairs={{0,8},{4,12},{8,0},{12,4},{1,9},{5,13},{9,1},{13,5},{2,10},{6,14},... | collective-permute-start | bytes 393224 | tf_op jit(solution)/shard_map/ppermute | solution.py:356
  4.0 3.4 %own.1 = (bf16[2,256,128]{2,1,0:T(8,128)(2,1)S(1)}, bf16[2,256,128]{2,1,0:T(8,128)(2,1)S(1)}, f32[2,2,64,128]{3,2,1,0:T(8,128)S(1)}, bf16[2,2,256,64]{3,2,1,0:T(...) custom-call(f32[2,64]{1,0:T(2,128)} %refs_0_.1, ...), custom_call_target="tpu_custom_call" | custom-call | flops 4000000000 | bytes 500000 | tf_op jit(solution)/shard_map/own/pallas_call | solution.py:122
  7.4 1.6 %collective-permute-start = (bf16[2,256,128]{2,1,0:T(8,128)(2,1)S(1)}, bf16[2,256,128]{2,1,0:T(8,128)(2,1)S(1)}, u32[]{:S(2)}, u32[]{:S(2)}) collective-permute-start(bf16[2,256,128]{2,1,0:T(8,128)(2,1)S(1)} %get-tuple-element.31.refs_0_), channel_id=1, source_target_pairs={{0,2},{2,0},{1,3},{3,1},{4,6},{6,4},{5,7},{7,5},{8,10},{10,8},{9,1... | collective-permute-start | bytes 393224 | tf_op jit(solution)/shard_map/ppermute | solution.py:363
  9.0 1.6 %collective-permute-done.1.m_ref = bf16[8,64,128]{2,1,0:T(8,128)(2,1)S(1)} collective-permute-done((bf16[8,64,128]{2,1,0:T(8,128)(2,1)}, bf16[8,64,128]{2,1,0:T(8,128)(2,1)S(1)}, u32[]{:S(2)}, u32[]{:S(2)}) %collective-permute-start.1) | collective-permute-done | bytes 131104 | tf_op jit(solution)/shard_map/ppermute | solution.py:356
  10.6 1.8 %collective-permute-start.2 = (bf16[8,64,128]{2,1,0:T(8,128)(2,1)S(1)}, bf16[8,64,128]{2,1,0:T(8,128)(2,1)S(1)}, u32[]{:S(2)}, u32[]{:S(2)}) collective-permute-start(bf16[8,64,128]{2,1,0:T(8,128)(2,1)S(1)} %broadcast_select_fusion.1), channel_id=1, source_target_pairs={{0,6},{2,4},{4,2},{6,0},{8,14},{10,12},{12,10},{14,8},{1,7},{3,5},... | collective-permute-start | bytes 393224 | tf_op jit(solution)/shard_map/ppermute | solution.py:379
  12.4 1.4 %far.1 = bf16[2,256,128]{2,1,0:T(8,128)(2,1)S(1)} custom-call(bf16[8,64,128]{2,1,0:T(8,128)(2,1)S(1)} %collective-permute-done.1.m_ref, f32[2,2,64,128]{3,2,1,0:T(8,128)S(1)} %get-tuple-element.32.gains.refs_1_, bf16[2,2,256,64]{3,2,1,0:T(8,128)(2,1)S(1)} %get-tuple-element.33.w_in.refs_2_, bf16[2,64,256]{2,1,0:T(8,128)(2,1)S(1)} %get-tuple-element.34.w_out.refs_3_, ...), custom_call_target="tpu_custom_call" | custom-call | flops 3000000000 | bytes 500000 | tf_op jit(solution)/shard_map/far/pallas_call | solution.py:150
  13.8 0.6 %collective-permute-start.3 = (bf16[2,256,128]{2,1,0:T(8,128)(2,1)S(1)}, bf16[2,256,128]{2,1,0:T(8,128)(2,1)S(1)}, u32[]{:S(2)}, u32[]{:S(2)}) collective-permute-start(bf16[2,256,128]{2,1,0:T(8,128)(2,1)S(1)} %get-tuple-element.57), channel_id=1, source_target_pairs={{0,2},{2,0},{4,6},{6,4},{8,10},{10,8},{12,14},{14,12},{1,3},{3,1},... | collective-permute-start | bytes 393224 | tf_op jit(solution)/shard_map/ppermute | solution.py:379
  14.4 1.2 %collective-permute-start.4 = (bf16[2,256,128]{2,1,0:T(8,128)(2,1)S(1)}, bf16[2,256,128]{2,1,0:T(8,128)(2,1)S(1)}, u32[]{:S(2)}, u32[]{:S(2)}) collective-permute-start(bf16[2,256,128]{2,1,0:T(8,128)(2,1)S(1)} %get-tuple-element.58), channel_id=1, source_target_pairs={{0,4},{2,6},{4,0},{6,2},{8,12},{10,14},{12,8},{14,10},{1,5},{3,7},... | collective-permute-start | bytes 393224 | tf_op jit(solution)/shard_map/ppermute | solution.py:379
  15.6 0.0 collective-permute-done.refs_1_
  15.6 0.8 %pair0.1 = (f32[2,1,1,64,128]{4,3,2,1,0:T(8,128)S(1)}, f32[2,1,1,64,128]{4,3,2,1,0:T(8,128)S(1)}, bf16[2,1,512,128]{3,2,1,0:T(8,128)(2,1)S(1)}) custom-call(bf16[2,256,128]{2,1,0:T(8,128)(2,1)S(1)} %get-tuple-element.31.refs_0_, bf16[2,256,128]{2,1,0:T(8,128)(2,1)S(1)} %collective-permute-done.refs_1_, bf16[1,2,256,128]{3,2,1,0:T(8,128)(2,1)S(1)} %bitcast.9, ...), custom_call_target="tpu_custom_call" | custom-call | flops 600000000 | bytes 1500000 | tf_op jit(solution)/shard_map/pair0/pallas_call | solution.py:271
  16.4 0.1 collective-permute-start.6
  16.5 0.0 collective-permute-done.2.refs_0_
  16.5 2.0 %pair1.1 = (f32[2,1,1,64,128]{4,3,2,1,0:T(8,128)S(1)}, f32[2,1,1,64,128]{4,3,2,1,0:T(8,128)S(1)}) custom-call(bf16[8,64,128]{2,1,0:T(8,128)(2,1)S(1)} %collective-permute-done.2.refs_0_, f32[2,2,64,128]{3,2,1,0:T(8,128)S(1)} %get-tuple-element.32.gains.refs_1_, bf16[2,2,256,64]{3,2,1,0:T(8,128)(2,1)S(1)} %get-tuple-element.33.w_in.refs_2_, ...), custom_call_target="tpu_custom_call" | custom-call | flops 3600000000 | bytes 1500000 | tf_op jit(solution)/shard_map/pair1/pallas_call | solution.py:271
  18.5 0.8 %collective-permute-done.3 = bf16[2,256,128]{2,1,0:T(8,128)(2,1)S(1)} collective-permute-done((bf16[2,256,128]{2,1,0:T(8,128)(2,1)S(1)}, bf16[2,256,128]{2,1,0:T(8,128)(2,1)S(1)}, u32[]{:S(2)}, u32[]{:S(2)}) %collective-permute-start.3) | collective-permute-done | bytes 131104 | tf_op jit(solution)/shard_map/ppermute | solution.py:379
  19.3 0.7 %pair2.1 = (f32[2,1,1,64,128]{4,3,2,1,0:T(8,128)S(1)}, f32[2,1,1,64,128]{4,3,2,1,0:T(8,128)S(1)}) custom-call(bf16[2,1,512,128]{3,2,1,0:T(8,128)(2,1)S(1)} %get-tuple-element.44.refs_5_.refs_0_, bf16[1,2,256,128]{3,2,1,0:T(8,128)(2,1)S(1)} %bitcast.11, bf16[2,1024,128]{2,1,0:T(8,128)(2,1)S(1)} %get-tuple-element.37.refs_3_.refs_6_.refs_2_, ...), custom_call_target="tpu_custom_call" | custom-call | flops 600000000 | bytes 1500000 | tf_op jit(solution)/shard_map/pair2/pallas_call | solution.py:271
  20.0 0.1 collective-permute-start.8
  20.1 0.5 %collective-permute-start.7 = (f32[2,1,1,64,128]{4,3,2,1,0:T(8,128)S(1)}, f32[2,1,1,64,128]{4,3,2,1,0:T(8,128)S(1)}, u32[]{:S(2)}, u32[]{:S(2)}) collective-permute-start(f32[2,1,1,64,128]{4,3,2,1,0:T(8,128)S(1)} %get-tuple-element.50), channel_id=1, source_target_pairs={{0,1},{1,0},{2,3},{3,2},{4,5},{5,4},{6,7},{7,6},{8,9},{9,8},{10,11... | collective-permute-start | bytes 196616 | tf_op jit(solution)/shard_map/ppermute | solution.py:409
  20.6 0.0 collective-permute-done.4
  20.6 0.7 %pair3.1 = (f32[2,1,1,64,128]{4,3,2,1,0:T(8,128)S(1)}, f32[2,1,1,64,128]{4,3,2,1,0:T(8,128)S(1)}) custom-call(bf16[2,1,512,128]{3,2,1,0:T(8,128)(2,1)S(1)} %get-tuple-element.44.refs_5_.refs_0_, bf16[1,2,256,128]{3,2,1,0:T(8,128)(2,1)S(1)} %bitcast.10, bf16[2,1024,128]{2,1,0:T(8,128)(2,1)S(1)} %get-tuple-element.37.refs_3_.refs_6_.refs_2_, ...), custom_call_target="tpu_custom_call" | custom-call | flops 600000000 | bytes 1500000 | tf_op jit(solution)/shard_map/pair3/pallas_call | solution.py:271
  21.3 0.1 collective-permute-start.5
  21.5 0.0 collective-permute-done.6.refs_1_
  21.5 0.0 collective-permute-done.8.refs_5_
  21.5 0.0 collective-permute-done.7.refs_3_
  21.5 1.1 %trans0.1.refs_2_ = f32[192,128]{1,0:T(8,128)S(1)} custom-call(f32[2,1,1,64,128]{4,3,2,1,0:T(8,128)S(1)} %get-tuple-element.47.refs_0_, f32[2,1,1,64,128]{4,3,2,1,0:T(8,128)S(1)} %collective-permute-done.6.refs_1_, f32[2,1,1,64,128]{4,3,2,1,0:T(8,128)S(1)} %get-tuple-element.49.refs_2_, f32[2,1,1,64,128]{4,3,2,1,0:T(8,128)S(1)} %collective-permute-done.7.refs_3_, ...), custom_call_target="tpu_custom_call" | custom-call | flops 1400000000 | bytes 1500000 | tf_op jit(solution)/shard_map/trans0/pallas_call | solution.py:336
  22.6 0.0 collective-permute-done.5.refs_1_
  22.7 1.7 %trans1.1 = f32[256,128]{1,0:T(8,128)} custom-call(f32[2,1,1,64,128]{4,3,2,1,0:T(8,128)S(1)} %get-tuple-element.45.refs_0_, f32[2,1,1,64,128]{4,3,2,1,0:T(8,128)S(1)} %collective-permute-done.5.refs_1_, f32[192,128]{1,0:T(8,128)S(1)} %trans0.1.refs_2_, f32[256,128]{1,0:T(8,128)S(1)} %get-tuple-element.53.refs_6_.refs_3_, ...), custom_call_target="tpu_custom_call" | custom-call | flops 1400000000 | bytes 1500000 | tf_op jit(solution)/shard_map/trans1/pallas_call | solution.py:336
  (2 shorter events, 0.0 us)
Async XLA Ops:
  0.0 10.5 %collective-permute-start.1 = (bf16[8,64,128]{2,1,0:T(8,128)(2,1)}, bf16[8,64,128]{2,1,0:T(8,128)(2,1)S(1)}, u32[]{:S(2)}, u32[]{:S(2)}) collective-permute-start(bf16[8,64,128]{2,1,0:T(8,128)(2,1)} %bitcast.13), channel_id=1, source_target_pairs={{0,8},{4,12},{8,0},{12,4},{1,9},{5,13},{9,1},{13,5},{2,10},{6,14},... | collective-permute-start | bytes 393224 | tf_op jit(solution)/shard_map/ppermute | solution.py:356
  7.4 8.2 %collective-permute-start = (bf16[2,256,128]{2,1,0:T(8,128)(2,1)S(1)}, bf16[2,256,128]{2,1,0:T(8,128)(2,1)S(1)}, u32[]{:S(2)}, u32[]{:S(2)}) collective-permute-start(bf16[2,256,128]{2,1,0:T(8,128)(2,1)S(1)} %get-tuple-element.31.refs_0_), channel_id=1, source_target_pairs={{0,2},{2,0},{1,3},{3,1},{4,6},{6,4},{5,7},{7,5},{8,10},{10,8},{9,1... | collective-permute-start | bytes 393224 | tf_op jit(solution)/shard_map/ppermute | solution.py:363
  10.6 6.0 %collective-permute-start.2 = (bf16[8,64,128]{2,1,0:T(8,128)(2,1)S(1)}, bf16[8,64,128]{2,1,0:T(8,128)(2,1)S(1)}, u32[]{:S(2)}, u32[]{:S(2)}) collective-permute-start(bf16[8,64,128]{2,1,0:T(8,128)(2,1)S(1)} %broadcast_select_fusion.1), channel_id=1, source_target_pairs={{0,6},{2,4},{4,2},{6,0},{8,14},{10,12},{12,10},{14,8},{1,7},{3,5},... | collective-permute-start | bytes 393224 | tf_op jit(solution)/shard_map/ppermute | solution.py:379
  13.8 5.5 %collective-permute-start.3 = (bf16[2,256,128]{2,1,0:T(8,128)(2,1)S(1)}, bf16[2,256,128]{2,1,0:T(8,128)(2,1)S(1)}, u32[]{:S(2)}, u32[]{:S(2)}) collective-permute-start(bf16[2,256,128]{2,1,0:T(8,128)(2,1)S(1)} %get-tuple-element.57), channel_id=1, source_target_pairs={{0,2},{2,0},{4,6},{6,4},{8,10},{10,8},{12,14},{14,12},{1,3},{3,1},... | collective-permute-start | bytes 393224 | tf_op jit(solution)/shard_map/ppermute | solution.py:379
  14.4 6.2 %collective-permute-start.4 = (bf16[2,256,128]{2,1,0:T(8,128)(2,1)S(1)}, bf16[2,256,128]{2,1,0:T(8,128)(2,1)S(1)}, u32[]{:S(2)}, u32[]{:S(2)}) collective-permute-start(bf16[2,256,128]{2,1,0:T(8,128)(2,1)S(1)} %get-tuple-element.58), channel_id=1, source_target_pairs={{0,4},{2,6},{4,0},{6,2},{8,12},{10,14},{12,8},{14,10},{1,5},{3,7},... | collective-permute-start | bytes 393224 | tf_op jit(solution)/shard_map/ppermute | solution.py:379
  16.4 5.1 %collective-permute-start.6 = (f32[2,1,1,64,128]{4,3,2,1,0:T(8,128)S(1)}, f32[2,1,1,64,128]{4,3,2,1,0:T(8,128)S(1)}, u32[]{:S(2)}, u32[]{:S(2)}) collective-permute-start(f32[2,1,1,64,128]{4,3,2,1,0:T(8,128)S(1)} %get-tuple-element.48), channel_id=1, source_target_pairs={{0,1},{1,0},{2,3},{3,2},{4,5},{5,4},{6,7},{7,6},{8,9},{9,8},{10,11... | collective-permute-start | bytes 196616 | tf_op jit(solution)/shard_map/ppermute | solution.py:409
  20.0 1.5 %collective-permute-start.8 = (f32[2,1,1,64,128]{4,3,2,1,0:T(8,128)S(1)}, f32[2,1,1,64,128]{4,3,2,1,0:T(8,128)S(1)}, u32[]{:S(2)}, u32[]{:S(2)}) collective-permute-start(f32[2,1,1,64,128]{4,3,2,1,0:T(8,128)S(1)} %get-tuple-element.52), channel_id=1, source_target_pairs={{0,1},{1,0},{2,3},{3,2},{4,5},{5,4},{6,7},{7,6},{8,9},{9,8},{10,11... | collective-permute-start | bytes 196616 | tf_op jit(solution)/shard_map/ppermute | solution.py:409
  20.1 1.4 %collective-permute-start.7 = (f32[2,1,1,64,128]{4,3,2,1,0:T(8,128)S(1)}, f32[2,1,1,64,128]{4,3,2,1,0:T(8,128)S(1)}, u32[]{:S(2)}, u32[]{:S(2)}) collective-permute-start(f32[2,1,1,64,128]{4,3,2,1,0:T(8,128)S(1)} %get-tuple-element.50), channel_id=1, source_target_pairs={{0,1},{1,0},{2,3},{3,2},{4,5},{5,4},{6,7},{7,6},{8,9},{9,8},{10,11... | collective-permute-start | bytes 196616 | tf_op jit(solution)/shard_map/ppermute | solution.py:409
  21.3 1.3 %collective-permute-start.5 = (f32[2,1,1,64,128]{4,3,2,1,0:T(8,128)S(1)}, f32[2,1,1,64,128]{4,3,2,1,0:T(8,128)S(1)}, u32[]{:S(2)}, u32[]{:S(2)}) collective-permute-start(f32[2,1,1,64,128]{4,3,2,1,0:T(8,128)S(1)} %get-tuple-element.46), channel_id=1, source_target_pairs={{0,1},{1,0},{2,3},{3,2},{4,5},{5,4},{6,7},{7,6},{8,9},{9,8},{10,11... | collective-permute-start | bytes 196616 | tf_op jit(solution)/shard_map/ppermute | solution.py:409

commit v5 on v4

--- a/solution.py
+++ b/solution.py
@@ -276,7 +276,7 @@
         scratch_shapes=scratch,
         compiler_params=pltpu.CompilerParams(vmem_limit_bytes=VMEM_LIMIT),
         cost_estimate=pl.CostEstimate(
-            flops=600_000_000 * n_right + (3_000_000_000 if raw else 0), bytes_accessed=1_500_000, transcendentals=0
+            flops=1_000_000, bytes_accessed=1000, transcendentals=0
         ),
         name="pair" + name,
     )(*raw, *lefts, *factors, w, b)
@@ -396,7 +396,7 @@
     tools = (gains, w_in, w_out, w_r)
     first = (spread([m] + far)(*others[0]), *tools)
     take = spread([right] + [far_call(seqs, amino, x, *tools) for x in far])
-    per = -(-(len(others) - 1) // 2)
+    per = len(others) - 1 if ratio * n_col <= 4 else n_col
     steps = [[(0, 0)], others[:1]] + [others[k : k + per] for k in range(1, len(others), per)]
     parts = []
     for k, group in enumerate(steps):

time: 24.5 us -> 23.7 us (0.967)
  Pallas kernels: 11.8 us -> 11.3 us
    pallas_call x4 -> x3, Pallas kernels: 4.22 us -> 3.79 us  [pair_call(): pl.pallas_call(functools.partial(pair_kernel, first, len(raw), n_col, n_d...]
    ppermute x3, waiting for transfers between devices: 0.81 us -> 0.39 us  [moved(): return lax.ppermute(x, ('row', 'col'), pairs)]
    ppermute x4 -> x3, waiting for transfers between devices: 0.06 us -> 0.31 us  [per_device(): lax.ppermute(send, 'dep', [(d, (d + 1) % n_dep) for d in range(n_dep)])]
    ppermute x4 -> x3, starting transfers between devices: 0.78 us -> 0.65 us  [per_device(): lax.ppermute(send, 'dep', [(d, (d + 1) % n_dep) for d in range(n_dep)])]
  transfers between devices with their start and end apart: 9 -> 8, of which waited for: 2 -> 5; matrix products, arithmetic and copies ran while one was open for 0% -> 0% of each run, Pallas kernels for 42% -> 41%
where the time goes in v5:
time: 23.7 us; the launch traced here: 23.6 us
  Pallas kernels  11.3 us (48%)
  starting transfers between devices  9.86 us (42%)
  waiting for transfers between devices  2.28 us (10%)
    ppermute x1, starting transfers between devices, rows_by(): lax.ppermute(x, 'row', [(r, (r + k) % n_row) for r in range(n_row)])  4.04 us
    pallas_call x3, Pallas kernels, pair_call(): pl.pallas_call(functools.partial(pair_kernel, first, len(raw), n_col, n_d...  3.79 us
    ppermute x3, starting transfers between devices, moved(): return lax.ppermute(x, ('row', 'col'), pairs)  3.62 us
    pallas_call x1, Pallas kernels, own_call(): pl.pallas_call(functools.partial(own_kernel, seqs, amino, n_first, len(lo...  3.38 us
    pallas_call x2, Pallas kernels, trans_call(): pl.pallas_call(functools.partial(trans_kernel, last, n_row, n_col, amino,...  2.74 us
    ppermute x1, waiting for transfers between devices, rows_by(): lax.ppermute(x, 'row', [(r, (r + k) % n_row) for r in range(n_row)])  1.57 us
    ppermute x1, starting transfers between devices, cols_by(): lax.ppermute(x, 'col', [(c, (c + k) % n_col) for c in range(n_col)])  1.55 us
    pallas_call x1, Pallas kernels, far_call(): pl.pallas_call(functools.partial(far_kernel, seqs, amino), out_shape=jax....  1.39 us
  transfers between devices with their start and end apart: 8, of which 5 were waited for; matrix products, arithmetic and copies ran while one was open for 0% of the time, Pallas kernels for 41%

profile of v5, /device:TPU:0, one launch (start us, length us, event | category | flops | bytes accessed | tf_op | source)
XLA Modules:
  0.0 23.6 jit_solution(10141956696758832198)
XLA Ops:
  0.0 4.0 %collective-permute-start.1 = (bf16[8,64,128]{2,1,0:T(8,128)(2,1)}, bf16[8,64,128]{2,1,0:T(8,128)(2,1)S(1)}, u32[]{:S(2)}, u32[]{:S(2)}) collective-permute-start(bf16[8,64,128]{2,1,0:T(8,128)(2,1)} %bitcast.13), channel_id=1, source_target_pairs={{0,8},{4,12},{8,0},{12,4},{1,9},{5,13},{9,1},{13,5},{2,10},{6,14},... | collective-permute-start | bytes 393224 | tf_op jit(solution)/shard_map/ppermute | solution.py:356
  4.0 3.4 %own.1 = (bf16[2,256,128]{2,1,0:T(8,128)(2,1)S(1)}, bf16[2,256,128]{2,1,0:T(8,128)(2,1)S(1)}, f32[2,2,64,128]{3,2,1,0:T(8,128)S(1)}, bf16[2,2,256,64]{3,2,1,0:T(...) custom-call(f32[2,64]{1,0:T(2,128)} %refs_0_.1, ...), custom_call_target="tpu_custom_call" | custom-call | flops 4000000000 | bytes 500000 | tf_op jit(solution)/shard_map/own/pallas_call | solution.py:122
  7.4 1.6 %collective-permute-start = (bf16[2,256,128]{2,1,0:T(8,128)(2,1)S(1)}, bf16[2,256,128]{2,1,0:T(8,128)(2,1)S(1)}, u32[]{:S(2)}, u32[]{:S(2)}) collective-permute-start(bf16[2,256,128]{2,1,0:T(8,128)(2,1)S(1)} %get-tuple-element.27.refs_0_), channel_id=1, source_target_pairs={{0,2},{2,0},{1,3},{3,1},{4,6},{6,4},{5,7},{7,5},{8,10},{10,8},{9,1... | collective-permute-start | bytes 393224 | tf_op jit(solution)/shard_map/ppermute | solution.py:363
  9.0 1.6 %collective-permute-done.1.m_ref = bf16[8,64,128]{2,1,0:T(8,128)(2,1)S(1)} collective-permute-done((bf16[8,64,128]{2,1,0:T(8,128)(2,1)}, bf16[8,64,128]{2,1,0:T(8,128)(2,1)S(1)}, u32[]{:S(2)}, u32[]{:S(2)}) %collective-permute-start.1) | collective-permute-done | bytes 131104 | tf_op jit(solution)/shard_map/ppermute | solution.py:356
  10.6 1.8 %collective-permute-start.2 = (bf16[8,64,128]{2,1,0:T(8,128)(2,1)S(1)}, bf16[8,64,128]{2,1,0:T(8,128)(2,1)S(1)}, u32[]{:S(2)}, u32[]{:S(2)}) collective-permute-start(bf16[8,64,128]{2,1,0:T(8,128)(2,1)S(1)} %broadcast_select_fusion.1), channel_id=1, source_target_pairs={{0,6},{2,4},{4,2},{6,0},{8,14},{10,12},{12,10},{14,8},{1,7},{3,5},... | collective-permute-start | bytes 393224 | tf_op jit(solution)/shard_map/ppermute | solution.py:379
  12.4 1.4 %far.1 = bf16[2,256,128]{2,1,0:T(8,128)(2,1)S(1)} custom-call(bf16[8,64,128]{2,1,0:T(8,128)(2,1)S(1)} %collective-permute-done.1.m_ref, f32[2,2,64,128]{3,2,1,0:T(8,128)S(1)} %get-tuple-element.28.gains.refs_1_, bf16[2,2,256,64]{3,2,1,0:T(8,128)(2,1)S(1)} %get-tuple-element.29.w_in.refs_2_, bf16[2,64,256]{2,1,0:T(8,128)(2,1)S(1)} %get-tuple-element.30.w_out.refs_3_, ...), custom_call_target="tpu_custom_call" | custom-call | flops 3000000000 | bytes 500000 | tf_op jit(solution)/shard_map/far/pallas_call | solution.py:150
  13.8 0.6 %collective-permute-start.3 = (bf16[2,256,128]{2,1,0:T(8,128)(2,1)S(1)}, bf16[2,256,128]{2,1,0:T(8,128)(2,1)S(1)}, u32[]{:S(2)}, u32[]{:S(2)}) collective-permute-start(bf16[2,256,128]{2,1,0:T(8,128)(2,1)S(1)} %get-tuple-element.49), channel_id=1, source_target_pairs={{0,2},{2,0},{4,6},{6,4},{8,10},{10,8},{12,14},{14,12},{1,3},{3,1},... | collective-permute-start | bytes 393224 | tf_op jit(solution)/shard_map/ppermute | solution.py:379
  14.4 1.2 %collective-permute-start.4 = (bf16[2,256,128]{2,1,0:T(8,128)(2,1)S(1)}, bf16[2,256,128]{2,1,0:T(8,128)(2,1)S(1)}, u32[]{:S(2)}, u32[]{:S(2)}) collective-permute-start(bf16[2,256,128]{2,1,0:T(8,128)(2,1)S(1)} %get-tuple-element.50), channel_id=1, source_target_pairs={{0,4},{2,6},{4,0},{6,2},{8,12},{10,14},{12,8},{14,10},{1,5},{3,7},... | collective-permute-start | bytes 393224 | tf_op jit(solution)/shard_map/ppermute | solution.py:379
  15.6 0.0 collective-permute-done.refs_1_
  15.6 0.8 %pair0.1 = (f32[2,1,1,64,128]{4,3,2,1,0:T(8,128)S(1)}, f32[2,1,1,64,128]{4,3,2,1,0:T(8,128)S(1)}, bf16[2,1,512,128]{3,2,1,0:T(8,128)(2,1)S(1)}) custom-call(bf16[2,256,128]{2,1,0:T(8,128)(2,1)S(1)} %get-tuple-element.27.refs_0_, bf16[2,256,128]{2,1,0:T(8,128)(2,1)S(1)} %collective-permute-done.refs_1_, bf16[1,2,256,128]{3,2,1,0:T(8,128)(2,1)S(1)} %bitcast.9, ...), custom_call_target="tpu_custom_call" | custom-call | flops 1000000 | bytes 1000 | tf_op jit(solution)/shard_map/pair0/pallas_call | solution.py:271
  16.4 0.1 collective-permute-start.6
  16.5 0.1 collective-permute-done.2.refs_0_
  16.5 2.0 %pair1.1 = (f32[2,1,1,64,128]{4,3,2,1,0:T(8,128)S(1)}, f32[2,1,1,64,128]{4,3,2,1,0:T(8,128)S(1)}) custom-call(bf16[8,64,128]{2,1,0:T(8,128)(2,1)S(1)} %collective-permute-done.2.refs_0_, f32[2,2,64,128]{3,2,1,0:T(8,128)S(1)} %get-tuple-element.28.gains.refs_1_, bf16[2,2,256,64]{3,2,1,0:T(8,128)(2,1)S(1)} %get-tuple-element.29.w_in.refs_2_, ...), custom_call_target="tpu_custom_call" | custom-call | flops 1000000 | bytes 1000 | tf_op jit(solution)/shard_map/pair1/pallas_call | solution.py:271
  18.5 0.5 %collective-permute-start.7 = (f32[2,1,1,64,128]{4,3,2,1,0:T(8,128)S(1)}, f32[2,1,1,64,128]{4,3,2,1,0:T(8,128)S(1)}, u32[]{:S(2)}, u32[]{:S(2)}) collective-permute-start(f32[2,1,1,64,128]{4,3,2,1,0:T(8,128)S(1)} %get-tuple-element.44), channel_id=1, source_target_pairs={{0,1},{1,0},{2,3},{3,2},{4,5},{5,4},{6,7},{7,6},{8,9},{9,8},{10,11... | collective-permute-start | bytes 196616 | tf_op jit(solution)/shard_map/ppermute | solution.py:409
  19.1 0.3 %collective-permute-done.3 = bf16[2,256,128]{2,1,0:T(8,128)(2,1)S(1)} collective-permute-done((bf16[2,256,128]{2,1,0:T(8,128)(2,1)S(1)}, bf16[2,256,128]{2,1,0:T(8,128)(2,1)S(1)}, u32[]{:S(2)}, u32[]{:S(2)}) %collective-permute-start.3) | collective-permute-done | bytes 131104 | tf_op jit(solution)/shard_map/ppermute | solution.py:379
  19.3 0.1 collective-permute-done.4
  19.4 1.0 %pair2.1 = (f32[2,1,2,64,128]{4,3,2,1,0:T(8,128)S(1)}, f32[2,1,2,64,128]{4,3,2,1,0:T(8,128)S(1)}) custom-call(bf16[2,1,512,128]{3,2,1,0:T(8,128)(2,1)S(1)} %get-tuple-element.38.refs_5_.refs_0_, bf16[1,2,256,128]{3,2,1,0:T(8,128)(2,1)S(1)} %bitcast.10, bf16[1,2,256,128]{3,2,1,0:T(8,128)(2,1)S(1)} %bitcast.11, ...), custom_call_target="tpu_custom_call" | custom-call | flops 1000000 | bytes 1000 | tf_op jit(solution)/shard_map/pair2/pallas_call | solution.py:271
  20.4 0.1 collective-permute-start.5
  20.5 0.0 collective-permute-done.6.refs_1_
  20.5 0.0 collective-permute-done.7.refs_3_
  20.5 1.0 %trans0.1.refs_2_ = f32[128,128]{1,0:T(8,128)S(1)} custom-call(f32[2,1,1,64,128]{4,3,2,1,0:T(8,128)S(1)} %get-tuple-element.41.refs_0_, f32[2,1,1,64,128]{4,3,2,1,0:T(8,128)S(1)} %collective-permute-done.6.refs_1_, f32[2,1,1,64,128]{4,3,2,1,0:T(8,128)S(1)} %get-tuple-element.43.refs_2_, f32[2,1,1,64,128]{4,3,2,1,0:T(8,128)S(1)} %collective-permute-done.7.refs_3_, ...), custom_call_target="tpu_custom_call" | custom-call | flops 1400000000 | bytes 1500000 | tf_op jit(solution)/shard_map/trans0/pallas_call | solution.py:336
  21.5 0.3 %collective-permute-done.5.refs_1_ = f32[2,1,2,64,128]{4,3,2,1,0:T(8,128)S(1)} collective-permute-done((f32[2,1,2,64,128]{4,3,2,1,0:T(8,128)S(1)}, f32[2,1,2,64,128]{4,3,2,1,0:T(8,128)S(1)}, u32[]{:S(2)}, u32[]{:S(2)}) %collective-permute-start.5) | collective-permute-done | bytes 131104 | tf_op jit(solution)/shard_map/ppermute | solution.py:409
  21.8 1.7 %trans1.1 = f32[256,128]{1,0:T(8,128)} custom-call(f32[2,1,2,64,128]{4,3,2,1,0:T(8,128)S(1)} %get-tuple-element.39.refs_0_, f32[2,1,2,64,128]{4,3,2,1,0:T(8,128)S(1)} %collective-permute-done.5.refs_1_, f32[128,128]{1,0:T(8,128)S(1)} %trans0.1.refs_2_, f32[256,128]{1,0:T(8,128)S(1)} %get-tuple-element.45.refs_4_.refs_3_, ...), custom_call_target="tpu_custom_call" | custom-call | flops 1400000000 | bytes 1500000 | tf_op jit(solution)/shard_map/trans1/pallas_call | solution.py:336
  (2 shorter events, 0.0 us)
Async XLA Ops:
  0.0 10.5 %collective-permute-start.1 = (bf16[8,64,128]{2,1,0:T(8,128)(2,1)}, bf16[8,64,128]{2,1,0:T(8,128)(2,1)S(1)}, u32[]{:S(2)}, u32[]{:S(2)}) collective-permute-start(bf16[8,64,128]{2,1,0:T(8,128)(2,1)} %bitcast.13), channel_id=1, source_target_pairs={{0,8},{4,12},{8,0},{12,4},{1,9},{5,13},{9,1},{13,5},{2,10},{6,14},... | collective-permute-start | bytes 393224 | tf_op jit(solution)/shard_map/ppermute | solution.py:356
  7.4 8.2 %collective-permute-start = (bf16[2,256,128]{2,1,0:T(8,128)(2,1)S(1)}, bf16[2,256,128]{2,1,0:T(8,128)(2,1)S(1)}, u32[]{:S(2)}, u32[]{:S(2)}) collective-permute-start(bf16[2,256,128]{2,1,0:T(8,128)(2,1)S(1)} %get-tuple-element.27.refs_0_), channel_id=1, source_target_pairs={{0,2},{2,0},{1,3},{3,1},{4,6},{6,4},{5,7},{7,5},{8,10},{10,8},{9,1... | collective-permute-start | bytes 393224 | tf_op jit(solution)/shard_map/ppermute | solution.py:363
  10.6 6.0 %collective-permute-start.2 = (bf16[8,64,128]{2,1,0:T(8,128)(2,1)S(1)}, bf16[8,64,128]{2,1,0:T(8,128)(2,1)S(1)}, u32[]{:S(2)}, u32[]{:S(2)}) collective-permute-start(bf16[8,64,128]{2,1,0:T(8,128)(2,1)S(1)} %broadcast_select_fusion.1), channel_id=1, source_target_pairs={{0,6},{2,4},{4,2},{6,0},{8,14},{10,12},{12,10},{14,8},{1,7},{3,5},... | collective-permute-start | bytes 393224 | tf_op jit(solution)/shard_map/ppermute | solution.py:379
  13.8 5.5 %collective-permute-start.3 = (bf16[2,256,128]{2,1,0:T(8,128)(2,1)S(1)}, bf16[2,256,128]{2,1,0:T(8,128)(2,1)S(1)}, u32[]{:S(2)}, u32[]{:S(2)}) collective-permute-start(bf16[2,256,128]{2,1,0:T(8,128)(2,1)S(1)} %get-tuple-element.49), channel_id=1, source_target_pairs={{0,2},{2,0},{4,6},{6,4},{8,10},{10,8},{12,14},{14,12},{1,3},{3,1},... | collective-permute-start | bytes 393224 | tf_op jit(solution)/shard_map/ppermute | solution.py:379
  14.4 5.0 %collective-permute-start.4 = (bf16[2,256,128]{2,1,0:T(8,128)(2,1)S(1)}, bf16[2,256,128]{2,1,0:T(8,128)(2,1)S(1)}, u32[]{:S(2)}, u32[]{:S(2)}) collective-permute-start(bf16[2,256,128]{2,1,0:T(8,128)(2,1)S(1)} %get-tuple-element.50), channel_id=1, source_target_pairs={{0,4},{2,6},{4,0},{6,2},{8,12},{10,14},{12,8},{14,10},{1,5},{3,7},... | collective-permute-start | bytes 393224 | tf_op jit(solution)/shard_map/ppermute | solution.py:379
  16.4 4.1 %collective-permute-start.6 = (f32[2,1,1,64,128]{4,3,2,1,0:T(8,128)S(1)}, f32[2,1,1,64,128]{4,3,2,1,0:T(8,128)S(1)}, u32[]{:S(2)}, u32[]{:S(2)}) collective-permute-start(f32[2,1,1,64,128]{4,3,2,1,0:T(8,128)S(1)} %get-tuple-element.42), channel_id=1, source_target_pairs={{0,1},{1,0},{2,3},{3,2},{4,5},{5,4},{6,7},{7,6},{8,9},{9,8},{10,11... | collective-permute-start | bytes 196616 | tf_op jit(solution)/shard_map/ppermute | solution.py:409
  18.5 2.0 %collective-permute-start.7 = (f32[2,1,1,64,128]{4,3,2,1,0:T(8,128)S(1)}, f32[2,1,1,64,128]{4,3,2,1,0:T(8,128)S(1)}, u32[]{:S(2)}, u32[]{:S(2)}) collective-permute-start(f32[2,1,1,64,128]{4,3,2,1,0:T(8,128)S(1)} %get-tuple-element.44), channel_id=1, source_target_pairs={{0,1},{1,0},{2,3},{3,2},{4,5},{5,4},{6,7},{7,6},{8,9},{9,8},{10,11... | collective-permute-start | bytes 196616 | tf_op jit(solution)/shard_map/ppermute | solution.py:409
  20.4 1.4 %collective-permute-start.5 = (f32[2,1,2,64,128]{4,3,2,1,0:T(8,128)S(1)}, f32[2,1,2,64,128]{4,3,2,1,0:T(8,128)S(1)}, u32[]{:S(2)}, u32[]{:S(2)}) collective-permute-start(f32[2,1,2,64,128]{4,3,2,1,0:T(8,128)S(1)} %get-tuple-element.40), channel_id=1, source_target_pairs={{0,1},{1,0},{2,3},{3,2},{4,5},{5,4},{6,7},{7,6},{8,9},{9,8},{10,11... | collective-permute-start | bytes 393224 | tf_op jit(solution)/shard_map/ppermute | solution.py:409

commit v6 on v5

--- a/solution.py
+++ b/solution.py
@@ -282,66 +282,74 @@
     )(*raw, *lefts, *factors, w, b)
 
 
-def trans_kernel(last, n_row, n_col, amino, cols, steps, done_steps, *refs):
-    n = sum(len(group) for group in steps)
+def trans_kernel(last, n_row, n_col, amino, cols, steps, next_steps, *refs):
     parts, refs = refs[: 2 * len(steps)], refs[2 * len(steps) :]
-    done, refs = refs[: len(done_steps)], refs[len(done_steps) :]
-    z_ref, g_ref, win_ref, wout_ref, out_ref = refs
+    if last:
+        start_ref, done_ref, g_ref, win_ref, wout_ref, out_ref = refs
+    else:
+        next_ref, z_ref, g_ref, win_ref, wout_ref, out_ref, after_ref = refs
     ratio = n_row // n_col
     row, col = lax.axis_index("row"), lax.axis_index("col")
-    per_dep, size = parts[0].shape[1], amino * amino
-
-    def first_column(step):
-        off = lax.rem(lax.rem(row, ratio) - step[0] + ratio, ratio)
-        return (off * n_col + lax.rem(col - step[1] + n_col, n_col)) * amino
+    per_dep = parts[0].shape[1]
 
     def places(steps):
-        return [
-            u * amino * cols + first_column(step) + j
-            for u in range(per_dep)
-            for step in steps
-            for j in range(amino)
-        ]
+        found = []
+        for u in range(per_dep):
+            for dr, dc in steps:
+                off = lax.rem(lax.rem(row, ratio) - dr + ratio, ratio)
+                first = (off * n_col + lax.rem(col - dc + n_col, n_col)) * amino
+                found += [u * amino * cols + first + j for j in range(amino)]
+        return found
+
+    def gather(steps):
+        return jnp.concatenate([z_ref[pl.ds(at, amino, stride=cols), :] for at in places(steps)], axis=0)
+
+    def blocks(step, refs):
+        return jnp.concatenate(
+            [
+                functools.reduce(jnp.add, [ref[step, u, i] for ref in group])
+                for u in range(per_dep)
+                for group in refs
+                for i in range(group[0].shape[2])
+            ],
+            axis=0,
+        )
 
     flat = [step for group in steps for step in group]
-    here = places(flat)
-    z = jnp.concatenate([z_ref[pl.ds(at, amino, stride=cols), :] for at in here], axis=0)
+    if last:
+        z = start_ref[...]
+        out_ref[...] = done_ref[...]
+    else:
+        z = gather(flat)
+        after_ref[...] = gather(next_steps) + blocks(0, [(next_ref,)])
     for step in range(NUM_MODULES):
-        moved = [
-            parts[2 * k][step, u, i] + parts[2 * k + 1][step, u, i]
-            for u in range(per_dep)
-            for k, group in enumerate(steps)
-            for i in range(len(group))
-        ]
-        z = z + jnp.concatenate(moved, axis=0)
+        pairs = [(parts[2 * k], parts[2 * k + 1]) for k in range(len(steps))]
+        if last and step == 0:
+            pairs = [x[1:] for x in pairs]
+        z = z + blocks(step, pairs)
         xp = norm_lanes(z, g_ref[step : step + 1, :]).astype(BF16)
         gate = dot_nn(xp, win_ref[step, 0]) * 0.5
         upper = dot_nn(xp, win_ref[step, 1])
         hidden = (silu_of_double(gate) * upper).astype(BF16)
         z = z + dot_nn(hidden, wout_ref[step])
-    if last:
-        for k, at in enumerate(here):
-            out_ref[pl.ds(at, amino, stride=cols), :] = z[k * amino : (k + 1) * amino, :]
-        for x, group in zip(done, done_steps):
-            for k, at in enumerate(places([step for part in group for step in part])):
-                out_ref[pl.ds(at, amino, stride=cols), :] = x[k * amino : (k + 1) * amino, :]
-    else:
-        out_ref[...] = z
-
-
-def trans_call(name, last, n_row, n_col, amino, cols, steps, parts, done_steps, done, z, g, win, wout):
-    per_dep, pair_ch = parts[0].shape[1], z.shape[1]
-    n = sum(len(group) for group in steps)
-    shape = z.shape if last else (per_dep * n * amino * amino, pair_ch)
+    for k, at in enumerate(places(flat)):
+        out_ref[pl.ds(at, amino, stride=cols), :] = z[k * amino : (k + 1) * amino, :]
+
+
+def trans_call(name, last, n_row, n_col, amino, cols, steps, parts, next_steps, ins, g, win, wout):
+    per_dep, pair_ch = parts[0].shape[1], g.shape[1]
+    outs = [jax.ShapeDtypeStruct((per_dep * amino * cols, pair_ch), F32)]
+    if not last:
+        outs.append(jax.ShapeDtypeStruct((per_dep * len(next_steps) * amino * amino, pair_ch), F32))
     return pl.pallas_call(
-        functools.partial(trans_kernel, last, n_row, n_col, amino, cols, steps, done_steps),
-        out_shape=jax.ShapeDtypeStruct(shape, F32),
-        in_specs=[pl.BlockSpec(memory_space=pltpu.VMEM)] * (len(parts) + len(done) + 4),
-        out_specs=pl.BlockSpec(memory_space=pltpu.VMEM),
+        functools.partial(trans_kernel, last, n_row, n_col, amino, cols, steps, next_steps),
+        out_shape=outs,
+        in_specs=[pl.BlockSpec(memory_space=pltpu.VMEM)] * (len(parts) + len(ins) + 3),
+        out_specs=[pl.BlockSpec(memory_space=pltpu.VMEM)] * len(outs),
         compiler_params=pltpu.CompilerParams(vmem_limit_bytes=VMEM_LIMIT),
         cost_estimate=pl.CostEstimate(flops=1_400_000_000, bytes_accessed=1_500_000, transcendentals=0),
         name="trans" + name,
-    )(*parts, *done, z, g, win, wout)
+    )(*parts, *ins, g, win, wout)
 
 
 def per_device(n_row, n_col, n_dep, msa, pair, g_ff, w_in, w_out, g_op, w_l, w_r, w_res, b_res, g_pair, p_in, p_out):
@@ -408,10 +416,10 @@
         lefts = lead or lefts
         parts += [keep, lax.ppermute(send, "dep", [(d, (d + 1) % n_dep) for d in range(n_dep)])]
     call = lambda name, last, *args: trans_call(
-        name, last, n_row, n_col, amino, cols, *args, z, g_pair, p_in, p_out
+        name, last, n_row, n_col, amino, cols, *args, g_pair, p_in, p_out
     )
-    most = call("0", False, steps[:-1], parts[:-2], [], [])
-    z = call("1", True, steps[-1:], parts[-2:], [steps[:-1]], [most])
+    most, start = call("0", False, steps[:-1], parts[:-2], steps[-1], [parts[-2], z])
+    (z,) = call("1", True, steps[-1:], parts[-2:], [], [start, most])
     return z.reshape(pair.shape)
 
 

time: 23.7 us -> 23.6 us (level)
  no operation moved by 1% of the time
where the time goes in v6:
time: 23.6 us; the launch traced here: 23.5 us
  Pallas kernels  11.2 us (47%)
  starting transfers between devices  9.86 us (42%)
  waiting for transfers between devices  2.24 us (9%)
    ppermute x1, starting transfers between devices, rows_by(): lax.ppermute(x, 'row', [(r, (r + k) % n_row) for r in range(n_row)])  4.04 us
    pallas_call x3, Pallas kernels, pair_call(): pl.pallas_call(functools.partial(pair_kernel, first, len(raw), n_col, n_d...  3.79 us
    ppermute x3, starting transfers between devices, moved(): return lax.ppermute(x, ('row', 'col'), pairs)  3.62 us
    pallas_call x1, Pallas kernels, own_call(): pl.pallas_call(functools.partial(own_kernel, seqs, amino, n_first, len(lo...  3.38 us
    pallas_call x2, Pallas kernels, trans_call(): pl.pallas_call(functools.partial(trans_kernel, last, n_row, n_col, amino,...  2.69 us
    ppermute x1, waiting for transfers between devices, rows_by(): lax.ppermute(x, 'row', [(r, (r + k) % n_row) for r in range(n_row)])  1.57 us
    ppermute x1, starting transfers between devices, cols_by(): lax.ppermute(x, 'col', [(c, (c + k) % n_col) for c in range(n_col)])  1.55 us
    pallas_call x1, Pallas kernels, far_call(): pl.pallas_call(functools.partial(far_kernel, seqs, amino), out_shape=jax....  1.39 us
  transfers between devices with their start and end apart: 8, of which 5 were waited for; matrix products, arithmetic and copies ran while one was open for 0% of the time, Pallas kernels for 41%

profile of v6, /device:TPU:0, one launch (start us, length us, event | category | flops | bytes accessed | tf_op | source)
XLA Modules:
  0.0 23.5 jit_solution(7224294605707678316)
XLA Ops:
  0.0 4.0 %collective-permute-start.1 = (bf16[8,64,128]{2,1,0:T(8,128)(2,1)}, bf16[8,64,128]{2,1,0:T(8,128)(2,1)S(1)}, u32[]{:S(2)}, u32[]{:S(2)}) collective-permute-start(bf16[8,64,128]{2,1,0:T(8,128)(2,1)} %bitcast.13), channel_id=1, source_target_pairs={{0,8},{4,12},{8,0},{12,4},{1,9},{5,13},{9,1},{13,5},{2,10},{6,14},... | collective-permute-start | bytes 393224 | tf_op jit(solution)/shard_map/ppermute | solution.py:364
  4.0 3.4 %own.1 = (bf16[2,256,128]{2,1,0:T(8,128)(2,1)S(1)}, bf16[2,256,128]{2,1,0:T(8,128)(2,1)S(1)}, f32[2,2,64,128]{3,2,1,0:T(8,128)S(1)}, bf16[2,2,256,64]{3,2,1,0:T(...) custom-call(f32[2,64]{1,0:T(2,128)} %refs_0_.1, ...), custom_call_target="tpu_custom_call" | custom-call | flops 4000000000 | bytes 500000 | tf_op jit(solution)/shard_map/own/pallas_call | solution.py:122
  7.4 1.6 %collective-permute-start = (bf16[2,256,128]{2,1,0:T(8,128)(2,1)S(1)}, bf16[2,256,128]{2,1,0:T(8,128)(2,1)S(1)}, u32[]{:S(2)}, u32[]{:S(2)}) collective-permute-start(bf16[2,256,128]{2,1,0:T(8,128)(2,1)S(1)} %get-tuple-element.29.refs_0_), channel_id=1, source_target_pairs={{0,2},{2,0},{1,3},{3,1},{4,6},{6,4},{5,7},{7,5},{8,10},{10,8},{9,1... | collective-permute-start | bytes 393224 | tf_op jit(solution)/shard_map/ppermute | solution.py:371
  9.0 1.6 %collective-permute-done.1.m_ref = bf16[8,64,128]{2,1,0:T(8,128)(2,1)S(1)} collective-permute-done((bf16[8,64,128]{2,1,0:T(8,128)(2,1)}, bf16[8,64,128]{2,1,0:T(8,128)(2,1)S(1)}, u32[]{:S(2)}, u32[]{:S(2)}) %collective-permute-start.1) | collective-permute-done | bytes 131104 | tf_op jit(solution)/shard_map/ppermute | solution.py:364
  10.6 1.8 %collective-permute-start.2 = (bf16[8,64,128]{2,1,0:T(8,128)(2,1)S(1)}, bf16[8,64,128]{2,1,0:T(8,128)(2,1)S(1)}, u32[]{:S(2)}, u32[]{:S(2)}) collective-permute-start(bf16[8,64,128]{2,1,0:T(8,128)(2,1)S(1)} %broadcast_select_fusion.1), channel_id=1, source_target_pairs={{0,6},{2,4},{4,2},{6,0},{8,14},{10,12},{12,10},{14,8},{1,7},{3,5},... | collective-permute-start | bytes 393224 | tf_op jit(solution)/shard_map/ppermute | solution.py:387
  12.4 1.4 %far.1 = bf16[2,256,128]{2,1,0:T(8,128)(2,1)S(1)} custom-call(bf16[8,64,128]{2,1,0:T(8,128)(2,1)S(1)} %collective-permute-done.1.m_ref, f32[2,2,64,128]{3,2,1,0:T(8,128)S(1)} %get-tuple-element.30.gains.refs_1_, bf16[2,2,256,64]{3,2,1,0:T(8,128)(2,1)S(1)} %get-tuple-element.31.w_in.refs_2_, bf16[2,64,256]{2,1,0:T(8,128)(2,1)S(1)} %get-tuple-element.32.w_out.refs_3_, ...), custom_call_target="tpu_custom_call" | custom-call | flops 3000000000 | bytes 500000 | tf_op jit(solution)/shard_map/far/pallas_call | solution.py:150
  13.8 0.6 %collective-permute-start.3 = (bf16[2,256,128]{2,1,0:T(8,128)(2,1)S(1)}, bf16[2,256,128]{2,1,0:T(8,128)(2,1)S(1)}, u32[]{:S(2)}, u32[]{:S(2)}) collective-permute-start(bf16[2,256,128]{2,1,0:T(8,128)(2,1)S(1)} %get-tuple-element.53), channel_id=1, source_target_pairs={{0,2},{2,0},{4,6},{6,4},{8,10},{10,8},{12,14},{14,12},{1,3},{3,1},... | collective-permute-start | bytes 393224 | tf_op jit(solution)/shard_map/ppermute | solution.py:387
  14.4 1.2 %collective-permute-start.4 = (bf16[2,256,128]{2,1,0:T(8,128)(2,1)S(1)}, bf16[2,256,128]{2,1,0:T(8,128)(2,1)S(1)}, u32[]{:S(2)}, u32[]{:S(2)}) collective-permute-start(bf16[2,256,128]{2,1,0:T(8,128)(2,1)S(1)} %get-tuple-element.54), channel_id=1, source_target_pairs={{0,4},{2,6},{4,0},{6,2},{8,12},{10,14},{12,8},{14,10},{1,5},{3,7},... | collective-permute-start | bytes 393224 | tf_op jit(solution)/shard_map/ppermute | solution.py:387
  15.6 0.0 collective-permute-done.refs_1_
  15.6 0.8 %pair0.1 = (f32[2,1,1,64,128]{4,3,2,1,0:T(8,128)S(1)}, f32[2,1,1,64,128]{4,3,2,1,0:T(8,128)S(1)}, bf16[2,1,512,128]{3,2,1,0:T(8,128)(2,1)S(1)}) custom-call(bf16[2,256,128]{2,1,0:T(8,128)(2,1)S(1)} %get-tuple-element.29.refs_0_, bf16[2,256,128]{2,1,0:T(8,128)(2,1)S(1)} %collective-permute-done.refs_1_, bf16[1,2,256,128]{3,2,1,0:T(8,128)(2,1)S(1)} %bitcast.9, ...), custom_call_target="tpu_custom_call" | custom-call | flops 1000000 | bytes 1000 | tf_op jit(solution)/shard_map/pair0/pallas_call | solution.py:271
  16.4 0.1 collective-permute-start.6
  16.5 0.1 collective-permute-done.2.refs_0_
  16.5 2.0 %pair1.1 = (f32[2,1,1,64,128]{4,3,2,1,0:T(8,128)S(1)}, f32[2,1,1,64,128]{4,3,2,1,0:T(8,128)S(1)}) custom-call(bf16[8,64,128]{2,1,0:T(8,128)(2,1)S(1)} %collective-permute-done.2.refs_0_, f32[2,2,64,128]{3,2,1,0:T(8,128)S(1)} %get-tuple-element.30.gains.refs_1_, bf16[2,2,256,64]{3,2,1,0:T(8,128)(2,1)S(1)} %get-tuple-element.31.w_in.refs_2_, ...), custom_call_target="tpu_custom_call" | custom-call | flops 1000000 | bytes 1000 | tf_op jit(solution)/shard_map/pair1/pallas_call | solution.py:271
  18.5 0.5 %collective-permute-start.7 = (f32[2,1,1,64,128]{4,3,2,1,0:T(8,128)S(1)}, f32[2,1,1,64,128]{4,3,2,1,0:T(8,128)S(1)}, u32[]{:S(2)}, u32[]{:S(2)}) collective-permute-start(f32[2,1,1,64,128]{4,3,2,1,0:T(8,128)S(1)} %get-tuple-element.46), channel_id=1, source_target_pairs={{0,1},{1,0},{2,3},{3,2},{4,5},{5,4},{6,7},{7,6},{8,9},{9,8},{10,11... | collective-permute-start | bytes 196616 | tf_op jit(solution)/shard_map/ppermute | solution.py:417
  19.1 0.3 %collective-permute-done.3 = bf16[2,256,128]{2,1,0:T(8,128)(2,1)S(1)} collective-permute-done((bf16[2,256,128]{2,1,0:T(8,128)(2,1)S(1)}, bf16[2,256,128]{2,1,0:T(8,128)(2,1)S(1)}, u32[]{:S(2)}, u32[]{:S(2)}) %collective-permute-start.3) | collective-permute-done | bytes 131104 | tf_op jit(solution)/shard_map/ppermute | solution.py:387
  19.3 0.1 collective-permute-done.4
  19.4 1.0 %pair2.1 = (f32[2,1,2,64,128]{4,3,2,1,0:T(8,128)S(1)}, f32[2,1,2,64,128]{4,3,2,1,0:T(8,128)S(1)}) custom-call(bf16[2,1,512,128]{3,2,1,0:T(8,128)(2,1)S(1)} %get-tuple-element.40.refs_5_.refs_0_, bf16[1,2,256,128]{3,2,1,0:T(8,128)(2,1)S(1)} %bitcast.10, bf16[1,2,256,128]{3,2,1,0:T(8,128)(2,1)S(1)} %bitcast.11, ...), custom_call_target="tpu_custom_call" | custom-call | flops 1000000 | bytes 1000 | tf_op jit(solution)/shard_map/pair2/pallas_call | solution.py:271
  20.4 0.1 collective-permute-start.5
  20.5 0.0 collective-permute-done.6.refs_1_
  20.5 0.0 collective-permute-done.7.refs_3_
  20.5 1.0 %trans0.1 = (f32[256,128]{1,0:T(8,128)S(1)}, f32[128,128]{1,0:T(8,128)S(1)}) custom-call(f32[2,1,1,64,128]{4,3,2,1,0:T(8,128)S(1)} %get-tuple-element.43.refs_0_, f32[2,1,1,64,128]{4,3,2,1,0:T(8,128)S(1)} %collective-permute-done.6.refs_1_, f32[2,1,1,64,128]{4,3,2,1,0:T(8,128)S(1)} %get-tuple-element.45.refs_2_, ...), custom_call_target="tpu_custom_call" | custom-call | flops 1400000000 | bytes 1500000 | tf_op jit(solution)/shard_map/trans0/pallas_call | solution.py:344
  21.6 0.3 %collective-permute-done.5.refs_1_ = f32[2,1,2,64,128]{4,3,2,1,0:T(8,128)S(1)} collective-permute-done((f32[2,1,2,64,128]{4,3,2,1,0:T(8,128)S(1)}, f32[2,1,2,64,128]{4,3,2,1,0:T(8,128)S(1)}, u32[]{:S(2)}, u32[]{:S(2)}) %collective-permute-start.5) | collective-permute-done | bytes 131104 | tf_op jit(solution)/shard_map/ppermute | solution.py:417
  21.8 1.6 %trans1.1 = f32[256,128]{1,0:T(8,128)} custom-call(f32[2,1,2,64,128]{4,3,2,1,0:T(8,128)S(1)} %get-tuple-element.41.refs_4_.refs_0_, f32[2,1,2,64,128]{4,3,2,1,0:T(8,128)S(1)} %collective-permute-done.5.refs_1_, f32[128,128]{1,0:T(8,128)S(1)} %get-tuple-element.51.refs_2_, f32[256,128]{1,0:T(8,128)S(1)} %get-tuple-element.52.refs_3_, ...), custom_call_target="tpu_custom_call" | custom-call | flops 1400000000 | bytes 1500000 | tf_op jit(solution)/shard_map/trans1/pallas_call | solution.py:344
  (2 shorter events, 0.0 us)
Async XLA Ops:
  0.0 10.5 %collective-permute-start.1 = (bf16[8,64,128]{2,1,0:T(8,128)(2,1)}, bf16[8,64,128]{2,1,0:T(8,128)(2,1)S(1)}, u32[]{:S(2)}, u32[]{:S(2)}) collective-permute-start(bf16[8,64,128]{2,1,0:T(8,128)(2,1)} %bitcast.13), channel_id=1, source_target_pairs={{0,8},{4,12},{8,0},{12,4},{1,9},{5,13},{9,1},{13,5},{2,10},{6,14},... | collective-permute-start | bytes 393224 | tf_op jit(solution)/shard_map/ppermute | solution.py:364
  7.4 8.2 %collective-permute-start = (bf16[2,256,128]{2,1,0:T(8,128)(2,1)S(1)}, bf16[2,256,128]{2,1,0:T(8,128)(2,1)S(1)}, u32[]{:S(2)}, u32[]{:S(2)}) collective-permute-start(bf16[2,256,128]{2,1,0:T(8,128)(2,1)S(1)} %get-tuple-element.29.refs_0_), channel_id=1, source_target_pairs={{0,2},{2,0},{1,3},{3,1},{4,6},{6,4},{5,7},{7,5},{8,10},{10,8},{9,1... | collective-permute-start | bytes 393224 | tf_op jit(solution)/shard_map/ppermute | solution.py:371
  10.6 6.0 %collective-permute-start.2 = (bf16[8,64,128]{2,1,0:T(8,128)(2,1)S(1)}, bf16[8,64,128]{2,1,0:T(8,128)(2,1)S(1)}, u32[]{:S(2)}, u32[]{:S(2)}) collective-permute-start(bf16[8,64,128]{2,1,0:T(8,128)(2,1)S(1)} %broadcast_select_fusion.1), channel_id=1, source_target_pairs={{0,6},{2,4},{4,2},{6,0},{8,14},{10,12},{12,10},{14,8},{1,7},{3,5},... | collective-permute-start | bytes 393224 | tf_op jit(solution)/shard_map/ppermute | solution.py:387
  13.8 5.5 %collective-permute-start.3 = (bf16[2,256,128]{2,1,0:T(8,128)(2,1)S(1)}, bf16[2,256,128]{2,1,0:T(8,128)(2,1)S(1)}, u32[]{:S(2)}, u32[]{:S(2)}) collective-permute-start(bf16[2,256,128]{2,1,0:T(8,128)(2,1)S(1)} %get-tuple-element.53), channel_id=1, source_target_pairs={{0,2},{2,0},{4,6},{6,4},{8,10},{10,8},{12,14},{14,12},{1,3},{3,1},... | collective-permute-start | bytes 393224 | tf_op jit(solution)/shard_map/ppermute | solution.py:387
  14.4 5.0 %collective-permute-start.4 = (bf16[2,256,128]{2,1,0:T(8,128)(2,1)S(1)}, bf16[2,256,128]{2,1,0:T(8,128)(2,1)S(1)}, u32[]{:S(2)}, u32[]{:S(2)}) collective-permute-start(bf16[2,256,128]{2,1,0:T(8,128)(2,1)S(1)} %get-tuple-element.54), channel_id=1, source_target_pairs={{0,4},{2,6},{4,0},{6,2},{8,12},{10,14},{12,8},{14,10},{1,5},{3,7},... | collective-permute-start | bytes 393224 | tf_op jit(solution)/shard_map/ppermute | solution.py:387
  16.4 4.1 %collective-permute-start.6 = (f32[2,1,1,64,128]{4,3,2,1,0:T(8,128)S(1)}, f32[2,1,1,64,128]{4,3,2,1,0:T(8,128)S(1)}, u32[]{:S(2)}, u32[]{:S(2)}) collective-permute-start(f32[2,1,1,64,128]{4,3,2,1,0:T(8,128)S(1)} %get-tuple-element.44), channel_id=1, source_target_pairs={{0,1},{1,0},{2,3},{3,2},{4,5},{5,4},{6,7},{7,6},{8,9},{9,8},{10,11... | collective-permute-start | bytes 196616 | tf_op jit(solution)/shard_map/ppermute | solution.py:417
  18.5 2.0 %collective-permute-start.7 = (f32[2,1,1,64,128]{4,3,2,1,0:T(8,128)S(1)}, f32[2,1,1,64,128]{4,3,2,1,0:T(8,128)S(1)}, u32[]{:S(2)}, u32[]{:S(2)}) collective-permute-start(f32[2,1,1,64,128]{4,3,2,1,0:T(8,128)S(1)} %get-tuple-element.46), channel_id=1, source_target_pairs={{0,1},{1,0},{2,3},{3,2},{4,5},{5,4},{6,7},{7,6},{8,9},{9,8},{10,11... | collective-permute-start | bytes 196616 | tf_op jit(solution)/shard_map/ppermute | solution.py:417
  20.4 1.4 %collective-permute-start.5 = (f32[2,1,2,64,128]{4,3,2,1,0:T(8,128)S(1)}, f32[2,1,2,64,128]{4,3,2,1,0:T(8,128)S(1)}, u32[]{:S(2)}, u32[]{:S(2)}) collective-permute-start(f32[2,1,2,64,128]{4,3,2,1,0:T(8,128)S(1)} %get-tuple-element.42), channel_id=1, source_target_pairs={{0,1},{1,0},{2,3},{3,2},{4,5},{5,4},{6,7},{7,6},{8,9},{9,8},{10,11... | collective-permute-start | bytes 393224 | tf_op jit(solution)/shard_map/ppermute | solution.py:417

commit v7 on v6

--- a/solution.py
+++ b/solution.py
@@ -328,9 +328,9 @@
             pairs = [x[1:] for x in pairs]
         z = z + blocks(step, pairs)
         xp = norm_lanes(z, g_ref[step : step + 1, :]).astype(BF16)
-        gate = dot_nn(xp, win_ref[step, 0]) * 0.5
-        upper = dot_nn(xp, win_ref[step, 1])
-        hidden = (silu_of_double(gate) * upper).astype(BF16)
+        wide = dot_nn(xp, jnp.concatenate([win_ref[step, 0], win_ref[step, 1]], axis=1))
+        half = wide.shape[1] // 2
+        hidden = (silu_of_double(wide[:, :half] * 0.5) * wide[:, half:]).astype(BF16)
         z = z + dot_nn(hidden, wout_ref[step])
     for k, at in enumerate(places(flat)):
         out_ref[pl.ds(at, amino, stride=cols), :] = z[k * amino : (k + 1) * amino, :]

time: 23.6 us -> 23.6 us (level)
  no operation moved by 1% of the time
where the time goes in v7:
time: 23.6 us; the launch traced here: 23.5 us
  Pallas kernels  11.2 us (47%)
  starting transfers between devices  9.86 us (42%)
  waiting for transfers between devices  2.24 us (9%)
    ppermute x1, starting transfers between devices, rows_by(): lax.ppermute(x, 'row', [(r, (r + k) % n_row) for r in range(n_row)])  4.04 us
    pallas_call x3, Pallas kernels, pair_call(): pl.pallas_call(functools.partial(pair_kernel, first, len(raw), n_col, n_d...  3.79 us
    ppermute x3, starting transfers between devices, moved(): return lax.ppermute(x, ('row', 'col'), pairs)  3.62 us
    pallas_call x1, Pallas kernels, own_call(): pl.pallas_call(functools.partial(own_kernel, seqs, amino, n_first, len(lo...  3.38 us
    pallas_call x2, Pallas kernels, trans_call(): pl.pallas_call(functools.partial(trans_kernel, last, n_row, n_col, amino,...  2.69 us
    ppermute x1, waiting for transfers between devices, rows_by(): lax.ppermute(x, 'row', [(r, (r + k) % n_row) for r in range(n_row)])  1.57 us
    ppermute x1, starting transfers between devices, cols_by(): lax.ppermute(x, 'col', [(c, (c + k) % n_col) for c in range(n_col)])  1.55 us
    pallas_call x1, Pallas kernels, far_call(): pl.pallas_call(functools.partial(far_kernel, seqs, amino), out_shape=jax....  1.39 us
  transfers between devices with their start and end apart: 8, of which 5 were waited for; matrix products, arithmetic and copies ran while one was open for 0% of the time, Pallas kernels for 41%

profile of v7, /device:TPU:0, one launch (start us, length us, event | category | flops | bytes accessed | tf_op | source)
XLA Modules:
  0.0 23.5 jit_solution(7224294605707678316)
XLA Ops:
  0.0 4.0 %collective-permute-start.1 = (bf16[8,64,128]{2,1,0:T(8,128)(2,1)}, bf16[8,64,128]{2,1,0:T(8,128)(2,1)S(1)}, u32[]{:S(2)}, u32[]{:S(2)}) collective-permute-start(bf16[8,64,128]{2,1,0:T(8,128)(2,1)} %bitcast.13), channel_id=1, source_target_pairs={{0,8},{4,12},{8,0},{12,4},{1,9},{5,13},{9,1},{13,5},{2,10},{6,14},... | collective-permute-start | bytes 393224 | tf_op jit(solution)/shard_map/ppermute | solution.py:364
  4.0 3.4 %own.1 = (bf16[2,256,128]{2,1,0:T(8,128)(2,1)S(1)}, bf16[2,256,128]{2,1,0:T(8,128)(2,1)S(1)}, f32[2,2,64,128]{3,2,1,0:T(8,128)S(1)}, bf16[2,2,256,64]{3,2,1,0:T(...) custom-call(f32[2,64]{1,0:T(2,128)} %refs_0_.1, ...), custom_call_target="tpu_custom_call" | custom-call | flops 4000000000 | bytes 500000 | tf_op jit(solution)/shard_map/own/pallas_call | solution.py:122
  7.4 1.6 %collective-permute-start = (bf16[2,256,128]{2,1,0:T(8,128)(2,1)S(1)}, bf16[2,256,128]{2,1,0:T(8,128)(2,1)S(1)}, u32[]{:S(2)}, u32[]{:S(2)}) collective-permute-start(bf16[2,256,128]{2,1,0:T(8,128)(2,1)S(1)} %get-tuple-element.29.refs_0_), channel_id=1, source_target_pairs={{0,2},{2,0},{1,3},{3,1},{4,6},{6,4},{5,7},{7,5},{8,10},{10,8},{9,1... | collective-permute-start | bytes 393224 | tf_op jit(solution)/shard_map/ppermute | solution.py:371
  9.0 1.6 %collective-permute-done.1.m_ref = bf16[8,64,128]{2,1,0:T(8,128)(2,1)S(1)} collective-permute-done((bf16[8,64,128]{2,1,0:T(8,128)(2,1)}, bf16[8,64,128]{2,1,0:T(8,128)(2,1)S(1)}, u32[]{:S(2)}, u32[]{:S(2)}) %collective-permute-start.1) | collective-permute-done | bytes 131104 | tf_op jit(solution)/shard_map/ppermute | solution.py:364
  10.6 1.8 %collective-permute-start.2 = (bf16[8,64,128]{2,1,0:T(8,128)(2,1)S(1)}, bf16[8,64,128]{2,1,0:T(8,128)(2,1)S(1)}, u32[]{:S(2)}, u32[]{:S(2)}) collective-permute-start(bf16[8,64,128]{2,1,0:T(8,128)(2,1)S(1)} %broadcast_select_fusion.1), channel_id=1, source_target_pairs={{0,6},{2,4},{4,2},{6,0},{8,14},{10,12},{12,10},{14,8},{1,7},{3,5},... | collective-permute-start | bytes 393224 | tf_op jit(solution)/shard_map/ppermute | solution.py:387
  12.4 1.4 %far.1 = bf16[2,256,128]{2,1,0:T(8,128)(2,1)S(1)} custom-call(bf16[8,64,128]{2,1,0:T(8,128)(2,1)S(1)} %collective-permute-done.1.m_ref, f32[2,2,64,128]{3,2,1,0:T(8,128)S(1)} %get-tuple-element.30.gains.refs_1_, bf16[2,2,256,64]{3,2,1,0:T(8,128)(2,1)S(1)} %get-tuple-element.31.w_in.refs_2_, bf16[2,64,256]{2,1,0:T(8,128)(2,1)S(1)} %get-tuple-element.32.w_out.refs_3_, ...), custom_call_target="tpu_custom_call" | custom-call | flops 3000000000 | bytes 500000 | tf_op jit(solution)/shard_map/far/pallas_call | solution.py:150
  13.8 0.6 %collective-permute-start.3 = (bf16[2,256,128]{2,1,0:T(8,128)(2,1)S(1)}, bf16[2,256,128]{2,1,0:T(8,128)(2,1)S(1)}, u32[]{:S(2)}, u32[]{:S(2)}) collective-permute-start(bf16[2,256,128]{2,1,0:T(8,128)(2,1)S(1)} %get-tuple-element.53), channel_id=1, source_target_pairs={{0,2},{2,0},{4,6},{6,4},{8,10},{10,8},{12,14},{14,12},{1,3},{3,1},... | collective-permute-start | bytes 393224 | tf_op jit(solution)/shard_map/ppermute | solution.py:387
  14.4 1.2 %collective-permute-start.4 = (bf16[2,256,128]{2,1,0:T(8,128)(2,1)S(1)}, bf16[2,256,128]{2,1,0:T(8,128)(2,1)S(1)}, u32[]{:S(2)}, u32[]{:S(2)}) collective-permute-start(bf16[2,256,128]{2,1,0:T(8,128)(2,1)S(1)} %get-tuple-element.54), channel_id=1, source_target_pairs={{0,4},{2,6},{4,0},{6,2},{8,12},{10,14},{12,8},{14,10},{1,5},{3,7},... | collective-permute-start | bytes 393224 | tf_op jit(solution)/shard_map/ppermute | solution.py:387
  15.6 0.0 collective-permute-done.refs_1_
  15.6 0.8 %pair0.1 = (f32[2,1,1,64,128]{4,3,2,1,0:T(8,128)S(1)}, f32[2,1,1,64,128]{4,3,2,1,0:T(8,128)S(1)}, bf16[2,1,512,128]{3,2,1,0:T(8,128)(2,1)S(1)}) custom-call(bf16[2,256,128]{2,1,0:T(8,128)(2,1)S(1)} %get-tuple-element.29.refs_0_, bf16[2,256,128]{2,1,0:T(8,128)(2,1)S(1)} %collective-permute-done.refs_1_, bf16[1,2,256,128]{3,2,1,0:T(8,128)(2,1)S(1)} %bitcast.9, ...), custom_call_target="tpu_custom_call" | custom-call | flops 1000000 | bytes 1000 | tf_op jit(solution)/shard_map/pair0/pallas_call | solution.py:271
  16.4 0.1 collective-permute-start.6
  16.5 0.1 collective-permute-done.2.refs_0_
  16.5 2.0 %pair1.1 = (f32[2,1,1,64,128]{4,3,2,1,0:T(8,128)S(1)}, f32[2,1,1,64,128]{4,3,2,1,0:T(8,128)S(1)}) custom-call(bf16[8,64,128]{2,1,0:T(8,128)(2,1)S(1)} %collective-permute-done.2.refs_0_, f32[2,2,64,128]{3,2,1,0:T(8,128)S(1)} %get-tuple-element.30.gains.refs_1_, bf16[2,2,256,64]{3,2,1,0:T(8,128)(2,1)S(1)} %get-tuple-element.31.w_in.refs_2_, ...), custom_call_target="tpu_custom_call" | custom-call | flops 1000000 | bytes 1000 | tf_op jit(solution)/shard_map/pair1/pallas_call | solution.py:271
  18.5 0.5 %collective-permute-start.7 = (f32[2,1,1,64,128]{4,3,2,1,0:T(8,128)S(1)}, f32[2,1,1,64,128]{4,3,2,1,0:T(8,128)S(1)}, u32[]{:S(2)}, u32[]{:S(2)}) collective-permute-start(f32[2,1,1,64,128]{4,3,2,1,0:T(8,128)S(1)} %get-tuple-element.46), channel_id=1, source_target_pairs={{0,1},{1,0},{2,3},{3,2},{4,5},{5,4},{6,7},{7,6},{8,9},{9,8},{10,11... | collective-permute-start | bytes 196616 | tf_op jit(solution)/shard_map/ppermute | solution.py:417
  19.1 0.3 %collective-permute-done.3 = bf16[2,256,128]{2,1,0:T(8,128)(2,1)S(1)} collective-permute-done((bf16[2,256,128]{2,1,0:T(8,128)(2,1)S(1)}, bf16[2,256,128]{2,1,0:T(8,128)(2,1)S(1)}, u32[]{:S(2)}, u32[]{:S(2)}) %collective-permute-start.3) | collective-permute-done | bytes 131104 | tf_op jit(solution)/shard_map/ppermute | solution.py:387
  19.3 0.1 collective-permute-done.4
  19.4 1.0 %pair2.1 = (f32[2,1,2,64,128]{4,3,2,1,0:T(8,128)S(1)}, f32[2,1,2,64,128]{4,3,2,1,0:T(8,128)S(1)}) custom-call(bf16[2,1,512,128]{3,2,1,0:T(8,128)(2,1)S(1)} %get-tuple-element.40.refs_5_.refs_0_, bf16[1,2,256,128]{3,2,1,0:T(8,128)(2,1)S(1)} %bitcast.10, bf16[1,2,256,128]{3,2,1,0:T(8,128)(2,1)S(1)} %bitcast.11, ...), custom_call_target="tpu_custom_call" | custom-call | flops 1000000 | bytes 1000 | tf_op jit(solution)/shard_map/pair2/pallas_call | solution.py:271
  20.4 0.1 collective-permute-start.5
  20.5 0.0 collective-permute-done.6.refs_1_
  20.5 0.0 collective-permute-done.7.refs_3_
  20.5 1.0 %trans0.1 = (f32[256,128]{1,0:T(8,128)S(1)}, f32[128,128]{1,0:T(8,128)S(1)}) custom-call(f32[2,1,1,64,128]{4,3,2,1,0:T(8,128)S(1)} %get-tuple-element.43.refs_0_, f32[2,1,1,64,128]{4,3,2,1,0:T(8,128)S(1)} %collective-permute-done.6.refs_1_, f32[2,1,1,64,128]{4,3,2,1,0:T(8,128)S(1)} %get-tuple-element.45.refs_2_, ...), custom_call_target="tpu_custom_call" | custom-call | flops 1400000000 | bytes 1500000 | tf_op jit(solution)/shard_map/trans0/pallas_call | solution.py:344
  21.6 0.3 %collective-permute-done.5.refs_1_ = f32[2,1,2,64,128]{4,3,2,1,0:T(8,128)S(1)} collective-permute-done((f32[2,1,2,64,128]{4,3,2,1,0:T(8,128)S(1)}, f32[2,1,2,64,128]{4,3,2,1,0:T(8,128)S(1)}, u32[]{:S(2)}, u32[]{:S(2)}) %collective-permute-start.5) | collective-permute-done | bytes 131104 | tf_op jit(solution)/shard_map/ppermute | solution.py:417
  21.8 1.6 %trans1.1 = f32[256,128]{1,0:T(8,128)} custom-call(f32[2,1,2,64,128]{4,3,2,1,0:T(8,128)S(1)} %get-tuple-element.41.refs_4_.refs_0_, f32[2,1,2,64,128]{4,3,2,1,0:T(8,128)S(1)} %collective-permute-done.5.refs_1_, f32[128,128]{1,0:T(8,128)S(1)} %get-tuple-element.51.refs_2_, f32[256,128]{1,0:T(8,128)S(1)} %get-tuple-element.52.refs_3_, ...), custom_call_target="tpu_custom_call" | custom-call | flops 1400000000 | bytes 1500000 | tf_op jit(solution)/shard_map/trans1/pallas_call | solution.py:344
  (2 shorter events, 0.0 us)
Async XLA Ops:
  0.0 10.5 %collective-permute-start.1 = (bf16[8,64,128]{2,1,0:T(8,128)(2,1)}, bf16[8,64,128]{2,1,0:T(8,128)(2,1)S(1)}, u32[]{:S(2)}, u32[]{:S(2)}) collective-permute-start(bf16[8,64,128]{2,1,0:T(8,128)(2,1)} %bitcast.13), channel_id=1, source_target_pairs={{0,8},{4,12},{8,0},{12,4},{1,9},{5,13},{9,1},{13,5},{2,10},{6,14},... | collective-permute-start | bytes 393224 | tf_op jit(solution)/shard_map/ppermute | solution.py:364
  7.4 8.2 %collective-permute-start = (bf16[2,256,128]{2,1,0:T(8,128)(2,1)S(1)}, bf16[2,256,128]{2,1,0:T(8,128)(2,1)S(1)}, u32[]{:S(2)}, u32[]{:S(2)}) collective-permute-start(bf16[2,256,128]{2,1,0:T(8,128)(2,1)S(1)} %get-tuple-element.29.refs_0_), channel_id=1, source_target_pairs={{0,2},{2,0},{1,3},{3,1},{4,6},{6,4},{5,7},{7,5},{8,10},{10,8},{9,1... | collective-permute-start | bytes 393224 | tf_op jit(solution)/shard_map/ppermute | solution.py:371
  10.6 6.0 %collective-permute-start.2 = (bf16[8,64,128]{2,1,0:T(8,128)(2,1)S(1)}, bf16[8,64,128]{2,1,0:T(8,128)(2,1)S(1)}, u32[]{:S(2)}, u32[]{:S(2)}) collective-permute-start(bf16[8,64,128]{2,1,0:T(8,128)(2,1)S(1)} %broadcast_select_fusion.1), channel_id=1, source_target_pairs={{0,6},{2,4},{4,2},{6,0},{8,14},{10,12},{12,10},{14,8},{1,7},{3,5},... | collective-permute-start | bytes 393224 | tf_op jit(solution)/shard_map/ppermute | solution.py:387
  13.8 5.5 %collective-permute-start.3 = (bf16[2,256,128]{2,1,0:T(8,128)(2,1)S(1)}, bf16[2,256,128]{2,1,0:T(8,128)(2,1)S(1)}, u32[]{:S(2)}, u32[]{:S(2)}) collective-permute-start(bf16[2,256,128]{2,1,0:T(8,128)(2,1)S(1)} %get-tuple-element.53), channel_id=1, source_target_pairs={{0,2},{2,0},{4,6},{6,4},{8,10},{10,8},{12,14},{14,12},{1,3},{3,1},... | collective-permute-start | bytes 393224 | tf_op jit(solution)/shard_map/ppermute | solution.py:387
  14.4 5.0 %collective-permute-start.4 = (bf16[2,256,128]{2,1,0:T(8,128)(2,1)S(1)}, bf16[2,256,128]{2,1,0:T(8,128)(2,1)S(1)}, u32[]{:S(2)}, u32[]{:S(2)}) collective-permute-start(bf16[2,256,128]{2,1,0:T(8,128)(2,1)S(1)} %get-tuple-element.54), channel_id=1, source_target_pairs={{0,4},{2,6},{4,0},{6,2},{8,12},{10,14},{12,8},{14,10},{1,5},{3,7},... | collective-permute-start | bytes 393224 | tf_op jit(solution)/shard_map/ppermute | solution.py:387
  16.4 4.1 %collective-permute-start.6 = (f32[2,1,1,64,128]{4,3,2,1,0:T(8,128)S(1)}, f32[2,1,1,64,128]{4,3,2,1,0:T(8,128)S(1)}, u32[]{:S(2)}, u32[]{:S(2)}) collective-permute-start(f32[2,1,1,64,128]{4,3,2,1,0:T(8,128)S(1)} %get-tuple-element.44), channel_id=1, source_target_pairs={{0,1},{1,0},{2,3},{3,2},{4,5},{5,4},{6,7},{7,6},{8,9},{9,8},{10,11... | collective-permute-start | bytes 196616 | tf_op jit(solution)/shard_map/ppermute | solution.py:417
  18.5 2.0 %collective-permute-start.7 = (f32[2,1,1,64,128]{4,3,2,1,0:T(8,128)S(1)}, f32[2,1,1,64,128]{4,3,2,1,0:T(8,128)S(1)}, u32[]{:S(2)}, u32[]{:S(2)}) collective-permute-start(f32[2,1,1,64,128]{4,3,2,1,0:T(8,128)S(1)} %get-tuple-element.46), channel_id=1, source_target_pairs={{0,1},{1,0},{2,3},{3,2},{4,5},{5,4},{6,7},{7,6},{8,9},{9,8},{10,11... | collective-permute-start | bytes 196616 | tf_op jit(solution)/shard_map/ppermute | solution.py:417
  20.4 1.4 %collective-permute-start.5 = (f32[2,1,2,64,128]{4,3,2,1,0:T(8,128)S(1)}, f32[2,1,2,64,128]{4,3,2,1,0:T(8,128)S(1)}, u32[]{:S(2)}, u32[]{:S(2)}) collective-permute-start(f32[2,1,2,64,128]{4,3,2,1,0:T(8,128)S(1)} %get-tuple-element.42), channel_id=1, source_target_pairs={{0,1},{1,0},{2,3},{3,2},{4,5},{5,4},{6,7},{7,6},{8,9},{9,8},{10,11... | collective-permute-start | bytes 393224 | tf_op jit(solution)/shard_map/ppermute | solution.py:417

commit v8 on v6

--- a/solution.py
+++ b/solution.py
@@ -154,7 +154,7 @@
         out_specs=pl.BlockSpec(memory_space=pltpu.VMEM),
         scratch_shapes=[pltpu.VMEM((w_in.shape[3], amino * seqs), F32)],
         compiler_params=pltpu.CompilerParams(vmem_limit_bytes=VMEM_LIMIT),
-        cost_estimate=pl.CostEstimate(flops=3_000_000_000, bytes_accessed=500_000, transcendentals=0),
+        cost_estimate=pl.CostEstimate(flops=1_000_000, bytes_accessed=500_000, transcendentals=0),
         name="far",
     )(m, gains, w_in, w_out, w_r)
 

time: 23.6 us -> 23.6 us (level)
  no operation moved by 1% of the time
where the time goes in v8:
time: 23.6 us; the launch traced here: 23.5 us
  Pallas kernels  11.2 us (47%)
  starting transfers between devices  9.85 us (42%)
  waiting for transfers between devices  2.26 us (10%)
    ppermute x1, starting transfers between devices, rows_by(): lax.ppermute(x, 'row', [(r, (r + k) % n_row) for r in range(n_row)])  4.04 us
    pallas_call x3, Pallas kernels, pair_call(): pl.pallas_call(functools.partial(pair_kernel, first, len(raw), n_col, n_d...  3.77 us
    ppermute x3, starting transfers between devices, moved(): return lax.ppermute(x, ('row', 'col'), pairs)  3.62 us
    pallas_call x1, Pallas kernels, own_call(): pl.pallas_call(functools.partial(own_kernel, seqs, amino, n_first, len(lo...  3.38 us
    pallas_call x2, Pallas kernels, trans_call(): pl.pallas_call(functools.partial(trans_kernel, last, n_row, n_col, amino,...  2.69 us
    ppermute x1, waiting for transfers between devices, rows_by(): lax.ppermute(x, 'row', [(r, (r + k) % n_row) for r in range(n_row)])  1.57 us
    ppermute x1, starting transfers between devices, cols_by(): lax.ppermute(x, 'col', [(c, (c + k) % n_col) for c in range(n_col)])  1.55 us
    pallas_call x1, Pallas kernels, far_call(): pl.pallas_call(functools.partial(far_kernel, seqs, amino), out_shape=jax....  1.39 us
  transfers between devices with their start and end apart: 8, of which 5 were waited for; matrix products, arithmetic and copies ran while one was open for 0% of the time, Pallas kernels for 41%

profile of v8, /device:TPU:0, one launch (start us, length us, event | category | flops | bytes accessed | tf_op | source)
XLA Modules:
  0.0 23.5 jit_solution(2988262195697821710)
XLA Ops:
  0.0 4.0 %collective-permute-start.1 = (bf16[8,64,128]{2,1,0:T(8,128)(2,1)}, bf16[8,64,128]{2,1,0:T(8,128)(2,1)S(1)}, u32[]{:S(2)}, u32[]{:S(2)}) collective-permute-start(bf16[8,64,128]{2,1,0:T(8,128)(2,1)} %bitcast.13), channel_id=1, source_target_pairs={{0,8},{4,12},{8,0},{12,4},{1,9},{5,13},{9,1},{13,5},{2,10},{6,14},... | collective-permute-start | bytes 393224 | tf_op jit(solution)/shard_map/ppermute | solution.py:364
  4.0 3.4 %own.1 = (bf16[2,256,128]{2,1,0:T(8,128)(2,1)S(1)}, bf16[2,256,128]{2,1,0:T(8,128)(2,1)S(1)}, f32[2,2,64,128]{3,2,1,0:T(8,128)S(1)}, bf16[2,2,256,64]{3,2,1,0:T(...) custom-call(f32[2,64]{1,0:T(2,128)} %refs_0_.1, ...), custom_call_target="tpu_custom_call" | custom-call | flops 4000000000 | bytes 500000 | tf_op jit(solution)/shard_map/own/pallas_call | solution.py:122
  7.4 1.6 %collective-permute-start = (bf16[2,256,128]{2,1,0:T(8,128)(2,1)S(1)}, bf16[2,256,128]{2,1,0:T(8,128)(2,1)S(1)}, u32[]{:S(2)}, u32[]{:S(2)}) collective-permute-start(bf16[2,256,128]{2,1,0:T(8,128)(2,1)S(1)} %get-tuple-element.29.refs_0_), channel_id=1, source_target_pairs={{0,2},{2,0},{1,3},{3,1},{4,6},{6,4},{5,7},{7,5},{8,10},{10,8},{9,1... | collective-permute-start | bytes 393224 | tf_op jit(solution)/shard_map/ppermute | solution.py:371
  9.0 1.6 %collective-permute-done.1.m_ref = bf16[8,64,128]{2,1,0:T(8,128)(2,1)S(1)} collective-permute-done((bf16[8,64,128]{2,1,0:T(8,128)(2,1)}, bf16[8,64,128]{2,1,0:T(8,128)(2,1)S(1)}, u32[]{:S(2)}, u32[]{:S(2)}) %collective-permute-start.1) | collective-permute-done | bytes 131104 | tf_op jit(solution)/shard_map/ppermute | solution.py:364
  10.6 1.8 %collective-permute-start.2 = (bf16[8,64,128]{2,1,0:T(8,128)(2,1)S(1)}, bf16[8,64,128]{2,1,0:T(8,128)(2,1)S(1)}, u32[]{:S(2)}, u32[]{:S(2)}) collective-permute-start(bf16[8,64,128]{2,1,0:T(8,128)(2,1)S(1)} %broadcast_select_fusion.1), channel_id=1, source_target_pairs={{0,6},{2,4},{4,2},{6,0},{8,14},{10,12},{12,10},{14,8},{1,7},{3,5},... | collective-permute-start | bytes 393224 | tf_op jit(solution)/shard_map/ppermute | solution.py:387
  12.4 1.4 %far.1 = bf16[2,256,128]{2,1,0:T(8,128)(2,1)S(1)} custom-call(bf16[8,64,128]{2,1,0:T(8,128)(2,1)S(1)} %collective-permute-done.1.m_ref, f32[2,2,64,128]{3,2,1,0:T(8,128)S(1)} %get-tuple-element.30.gains.refs_1_, bf16[2,2,256,64]{3,2,1,0:T(8,128)(2,1)S(1)} %get-tuple-element.31.w_in.refs_2_, bf16[2,64,256]{2,1,0:T(8,128)(2,1)S(1)} %get-tuple-element.32.w_out.refs_3_, ...), custom_call_target="tpu_custom_call" | custom-call | flops 1000000 | bytes 500000 | tf_op jit(solution)/shard_map/far/pallas_call | solution.py:150
  13.8 0.6 %collective-permute-start.3 = (bf16[2,256,128]{2,1,0:T(8,128)(2,1)S(1)}, bf16[2,256,128]{2,1,0:T(8,128)(2,1)S(1)}, u32[]{:S(2)}, u32[]{:S(2)}) collective-permute-start(bf16[2,256,128]{2,1,0:T(8,128)(2,1)S(1)} %get-tuple-element.53), channel_id=1, source_target_pairs={{0,2},{2,0},{4,6},{6,4},{8,10},{10,8},{12,14},{14,12},{1,3},{3,1},... | collective-permute-start | bytes 393224 | tf_op jit(solution)/shard_map/ppermute | solution.py:387
  14.4 1.2 %collective-permute-start.4 = (bf16[2,256,128]{2,1,0:T(8,128)(2,1)S(1)}, bf16[2,256,128]{2,1,0:T(8,128)(2,1)S(1)}, u32[]{:S(2)}, u32[]{:S(2)}) collective-permute-start(bf16[2,256,128]{2,1,0:T(8,128)(2,1)S(1)} %get-tuple-element.54), channel_id=1, source_target_pairs={{0,4},{2,6},{4,0},{6,2},{8,12},{10,14},{12,8},{14,10},{1,5},{3,7},... | collective-permute-start | bytes 393224 | tf_op jit(solution)/shard_map/ppermute | solution.py:387
  15.6 0.0 collective-permute-done.refs_1_
  15.6 0.8 %pair0.1 = (f32[2,1,1,64,128]{4,3,2,1,0:T(8,128)S(1)}, f32[2,1,1,64,128]{4,3,2,1,0:T(8,128)S(1)}, bf16[2,1,512,128]{3,2,1,0:T(8,128)(2,1)S(1)}) custom-call(bf16[2,256,128]{2,1,0:T(8,128)(2,1)S(1)} %get-tuple-element.29.refs_0_, bf16[2,256,128]{2,1,0:T(8,128)(2,1)S(1)} %collective-permute-done.refs_1_, bf16[1,2,256,128]{3,2,1,0:T(8,128)(2,1)S(1)} %bitcast.9, ...), custom_call_target="tpu_custom_call" | custom-call | flops 1000000 | bytes 1000 | tf_op jit(solution)/shard_map/pair0/pallas_call | solution.py:271
  16.4 0.1 collective-permute-start.6
  16.5 0.1 collective-permute-done.2.refs_0_
  16.5 2.0 %pair1.1 = (f32[2,1,1,64,128]{4,3,2,1,0:T(8,128)S(1)}, f32[2,1,1,64,128]{4,3,2,1,0:T(8,128)S(1)}) custom-call(bf16[8,64,128]{2,1,0:T(8,128)(2,1)S(1)} %collective-permute-done.2.refs_0_, f32[2,2,64,128]{3,2,1,0:T(8,128)S(1)} %get-tuple-element.30.gains.refs_1_, bf16[2,2,256,64]{3,2,1,0:T(8,128)(2,1)S(1)} %get-tuple-element.31.w_in.refs_2_, ...), custom_call_target="tpu_custom_call" | custom-call | flops 1000000 | bytes 1000 | tf_op jit(solution)/shard_map/pair1/pallas_call | solution.py:271
  18.5 0.5 %collective-permute-start.7 = (f32[2,1,1,64,128]{4,3,2,1,0:T(8,128)S(1)}, f32[2,1,1,64,128]{4,3,2,1,0:T(8,128)S(1)}, u32[]{:S(2)}, u32[]{:S(2)}) collective-permute-start(f32[2,1,1,64,128]{4,3,2,1,0:T(8,128)S(1)} %get-tuple-element.46), channel_id=1, source_target_pairs={{0,1},{1,0},{2,3},{3,2},{4,5},{5,4},{6,7},{7,6},{8,9},{9,8},{10,11... | collective-permute-start | bytes 196616 | tf_op jit(solution)/shard_map/ppermute | solution.py:417
  19.0 0.3 %collective-permute-done.3 = bf16[2,256,128]{2,1,0:T(8,128)(2,1)S(1)} collective-permute-done((bf16[2,256,128]{2,1,0:T(8,128)(2,1)S(1)}, bf16[2,256,128]{2,1,0:T(8,128)(2,1)S(1)}, u32[]{:S(2)}, u32[]{:S(2)}) %collective-permute-start.3) | collective-permute-done | bytes 131104 | tf_op jit(solution)/shard_map/ppermute | solution.py:387
  19.3 0.1 collective-permute-done.4
  19.4 1.0 %pair2.1 = (f32[2,1,2,64,128]{4,3,2,1,0:T(8,128)S(1)}, f32[2,1,2,64,128]{4,3,2,1,0:T(8,128)S(1)}) custom-call(bf16[2,1,512,128]{3,2,1,0:T(8,128)(2,1)S(1)} %get-tuple-element.40.refs_5_.refs_0_, bf16[1,2,256,128]{3,2,1,0:T(8,128)(2,1)S(1)} %bitcast.10, bf16[1,2,256,128]{3,2,1,0:T(8,128)(2,1)S(1)} %bitcast.11, ...), custom_call_target="tpu_custom_call" | custom-call | flops 1000000 | bytes 1000 | tf_op jit(solution)/shard_map/pair2/pallas_call | solution.py:271
  20.4 0.1 collective-permute-start.5
  20.5 0.0 collective-permute-done.6.refs_1_
  20.5 0.0 collective-permute-done.7.refs_3_
  20.5 1.0 %trans0.1 = (f32[256,128]{1,0:T(8,128)S(1)}, f32[128,128]{1,0:T(8,128)S(1)}) custom-call(f32[2,1,1,64,128]{4,3,2,1,0:T(8,128)S(1)} %get-tuple-element.43.refs_0_, f32[2,1,1,64,128]{4,3,2,1,0:T(8,128)S(1)} %collective-permute-done.6.refs_1_, f32[2,1,1,64,128]{4,3,2,1,0:T(8,128)S(1)} %get-tuple-element.45.refs_2_, ...), custom_call_target="tpu_custom_call" | custom-call | flops 1400000000 | bytes 1500000 | tf_op jit(solution)/shard_map/trans0/pallas_call | solution.py:344
  21.6 0.3 %collective-permute-done.5.refs_1_ = f32[2,1,2,64,128]{4,3,2,1,0:T(8,128)S(1)} collective-permute-done((f32[2,1,2,64,128]{4,3,2,1,0:T(8,128)S(1)}, f32[2,1,2,64,128]{4,3,2,1,0:T(8,128)S(1)}, u32[]{:S(2)}, u32[]{:S(2)}) %collective-permute-start.5) | collective-permute-done | bytes 131104 | tf_op jit(solution)/shard_map/ppermute | solution.py:417
  21.8 1.6 %trans1.1 = f32[256,128]{1,0:T(8,128)} custom-call(f32[2,1,2,64,128]{4,3,2,1,0:T(8,128)S(1)} %get-tuple-element.41.refs_4_.refs_0_, f32[2,1,2,64,128]{4,3,2,1,0:T(8,128)S(1)} %collective-permute-done.5.refs_1_, f32[128,128]{1,0:T(8,128)S(1)} %get-tuple-element.51.refs_2_, f32[256,128]{1,0:T(8,128)S(1)} %get-tuple-element.52.refs_3_, ...), custom_call_target="tpu_custom_call" | custom-call | flops 1400000000 | bytes 1500000 | tf_op jit(solution)/shard_map/trans1/pallas_call | solution.py:344
  (2 shorter events, 0.0 us)
Async XLA Ops:
  0.0 10.5 %collective-permute-start.1 = (bf16[8,64,128]{2,1,0:T(8,128)(2,1)}, bf16[8,64,128]{2,1,0:T(8,128)(2,1)S(1)}, u32[]{:S(2)}, u32[]{:S(2)}) collective-permute-start(bf16[8,64,128]{2,1,0:T(8,128)(2,1)} %bitcast.13), channel_id=1, source_target_pairs={{0,8},{4,12},{8,0},{12,4},{1,9},{5,13},{9,1},{13,5},{2,10},{6,14},... | collective-permute-start | bytes 393224 | tf_op jit(solution)/shard_map/ppermute | solution.py:364
  7.4 8.2 %collective-permute-start = (bf16[2,256,128]{2,1,0:T(8,128)(2,1)S(1)}, bf16[2,256,128]{2,1,0:T(8,128)(2,1)S(1)}, u32[]{:S(2)}, u32[]{:S(2)}) collective-permute-start(bf16[2,256,128]{2,1,0:T(8,128)(2,1)S(1)} %get-tuple-element.29.refs_0_), channel_id=1, source_target_pairs={{0,2},{2,0},{1,3},{3,1},{4,6},{6,4},{5,7},{7,5},{8,10},{10,8},{9,1... | collective-permute-start | bytes 393224 | tf_op jit(solution)/shard_map/ppermute | solution.py:371
  10.6 6.0 %collective-permute-start.2 = (bf16[8,64,128]{2,1,0:T(8,128)(2,1)S(1)}, bf16[8,64,128]{2,1,0:T(8,128)(2,1)S(1)}, u32[]{:S(2)}, u32[]{:S(2)}) collective-permute-start(bf16[8,64,128]{2,1,0:T(8,128)(2,1)S(1)} %broadcast_select_fusion.1), channel_id=1, source_target_pairs={{0,6},{2,4},{4,2},{6,0},{8,14},{10,12},{12,10},{14,8},{1,7},{3,5},... | collective-permute-start | bytes 393224 | tf_op jit(solution)/shard_map/ppermute | solution.py:387
  13.8 5.5 %collective-permute-start.3 = (bf16[2,256,128]{2,1,0:T(8,128)(2,1)S(1)}, bf16[2,256,128]{2,1,0:T(8,128)(2,1)S(1)}, u32[]{:S(2)}, u32[]{:S(2)}) collective-permute-start(bf16[2,256,128]{2,1,0:T(8,128)(2,1)S(1)} %get-tuple-element.53), channel_id=1, source_target_pairs={{0,2},{2,0},{4,6},{6,4},{8,10},{10,8},{12,14},{14,12},{1,3},{3,1},... | collective-permute-start | bytes 393224 | tf_op jit(solution)/shard_map/ppermute | solution.py:387
  14.4 5.0 %collective-permute-start.4 = (bf16[2,256,128]{2,1,0:T(8,128)(2,1)S(1)}, bf16[2,256,128]{2,1,0:T(8,128)(2,1)S(1)}, u32[]{:S(2)}, u32[]{:S(2)}) collective-permute-start(bf16[2,256,128]{2,1,0:T(8,128)(2,1)S(1)} %get-tuple-element.54), channel_id=1, source_target_pairs={{0,4},{2,6},{4,0},{6,2},{8,12},{10,14},{12,8},{14,10},{1,5},{3,7},... | collective-permute-start | bytes 393224 | tf_op jit(solution)/shard_map/ppermute | solution.py:387
  16.4 4.1 %collective-permute-start.6 = (f32[2,1,1,64,128]{4,3,2,1,0:T(8,128)S(1)}, f32[2,1,1,64,128]{4,3,2,1,0:T(8,128)S(1)}, u32[]{:S(2)}, u32[]{:S(2)}) collective-permute-start(f32[2,1,1,64,128]{4,3,2,1,0:T(8,128)S(1)} %get-tuple-element.44), channel_id=1, source_target_pairs={{0,1},{1,0},{2,3},{3,2},{4,5},{5,4},{6,7},{7,6},{8,9},{9,8},{10,11... | collective-permute-start | bytes 196616 | tf_op jit(solution)/shard_map/ppermute | solution.py:417
  18.5 2.0 %collective-permute-start.7 = (f32[2,1,1,64,128]{4,3,2,1,0:T(8,128)S(1)}, f32[2,1,1,64,128]{4,3,2,1,0:T(8,128)S(1)}, u32[]{:S(2)}, u32[]{:S(2)}) collective-permute-start(f32[2,1,1,64,128]{4,3,2,1,0:T(8,128)S(1)} %get-tuple-element.46), channel_id=1, source_target_pairs={{0,1},{1,0},{2,3},{3,2},{4,5},{5,4},{6,7},{7,6},{8,9},{9,8},{10,11... | collective-permute-start | bytes 196616 | tf_op jit(solution)/shard_map/ppermute | solution.py:417
  20.4 1.4 %collective-permute-start.5 = (f32[2,1,2,64,128]{4,3,2,1,0:T(8,128)S(1)}, f32[2,1,2,64,128]{4,3,2,1,0:T(8,128)S(1)}, u32[]{:S(2)}, u32[]{:S(2)}) collective-permute-start(f32[2,1,2,64,128]{4,3,2,1,0:T(8,128)S(1)} %get-tuple-element.42), channel_id=1, source_target_pairs={{0,1},{1,0},{2,3},{3,2},{4,5},{5,4},{6,7},{7,6},{8,9},{9,8},{10,11... | collective-permute-start | bytes 393224 | tf_op jit(solution)/shard_map/ppermute | solution.py:417
